TPU v7x, 32 devices: a whole 2x2x4 slice. The times are simulated.
32 devices in a mesh: grp: 2 (over y), tr: 8 (over z, x), root: 2 (over core).
Axes of the slice: x: 2, y: 2, z: 4, core: 2. Of those that a mesh axis runs over, the one named last changes fastest.
Arguments:
- residual: bfloat16 [128, 65536], P('root', ('grp', 'tr')), parts along dimension 1, may hold values from -8 to 8
- subspace: bfloat16 [512, 65536], P(None, ('grp', 'tr')), parts along dimension 1, may hold values from -1 to 1, as said below
- inverses: bfloat16 [16, 512, 512], P(('grp', 'tr')), parts along dimension 0, may hold values from -1 to 3, as said below
- owner_offset: int32 [128], P(('grp', 'tr')), parts along dimension 0, may hold values from 0 to 3, as said below
- listed: int32 [128], P(('grp', 'tr')), parts along dimension 0, may hold values from 0 to 1, as said below
Outputs:
- corrections: float32 [128, 65536], P('root', ('grp', 'tr')), parts along dimension 1
There are 2 independent parts, one for each index of `grp`. A program takes and returns all parts, laid end to end along the dimension named above; each array names one. Nothing has to cross between parts.
Inputs may be any that keep to these rules, and one draw needn't show every extreme that they name: Each entry of subspace lies within the stated range; rows are not normalized. `inverses`: each inverse is a dense real matrix. `owner_offset`: among the 8 blocks of each shard, at least one is listed and has offset 3. Each shard has at least one listed block and at least one unlisted block.
All inputs are finite; a program needn't handle non-finite values.
Results may differ from a plain program's by a relative error of at most 0.0065.
Values may be sent and summed in bfloat16 or wider, within the bound.
No kernel may reach another device: no remote copies, remote signals or barrier semaphores. Data moves between devices by JAX's collectives and lax.ppermute only.
A program may use at most 64 MiB of HBM per device.

v0:
```python
import jax
import jax.numpy as jnp
from jax import lax
from jax.sharding import PartitionSpec as P

BLK = 512
OFFS = 4
PASSES = 2


def from_behind(block, axis, distance):
    devices = range(lax.axis_size(axis))
    route = [((i - distance) % len(devices), i) for i in devices]
    return lax.ppermute(block, axis, route)


def per_device(residual, subspace, inverses, owner_offset, listed):
    root_count, row_count = residual.shape
    block_count = row_count // BLK
    blocks = residual.reshape(root_count, block_count, BLK)
    chosen_mask = listed > 0
    inverse = inverses[0]
    target = jnp.arange(OFFS, dtype=jnp.int32)
    held_inverses = [inverse]
    for offset in range(1, OFFS):
        held_inverses.append(from_behind(inverse, "tr", -offset))
    inverse_table = jnp.stack(held_inverses)
    selector = (owner_offset[:, None] == target[None, :]).astype(jnp.bfloat16)
    picked = jnp.einsum(
        "jd,dbc->jbc", selector, inverse_table, preferred_element_type=jnp.float32
    ).astype(jnp.bfloat16)
    solved = jnp.einsum("rjb,jbc->rjc", blocks, picked, preferred_element_type=jnp.float32)
    precond = jnp.where(chosen_mask[None, :, None], solved, blocks.astype(jnp.float32)).reshape(
        root_count, row_count
    )
    current = precond
    for repeat in range(PASSES):
        rounded = current.astype(jnp.bfloat16)
        partial_correlation = lax.dot_general(
            rounded, subspace, (((1,), (1,)), ((), ())), preferred_element_type=jnp.float32
        )
        correlation = lax.psum(partial_correlation, "tr")
        coefficients = correlation.astype(jnp.bfloat16)
        current = current - jnp.dot(coefficients, subspace, preferred_element_type=jnp.float32)
    return current


def solution(mesh):
    return jax.shard_map(
        per_device,
        mesh=mesh,
        in_specs=(
            P("root", ("grp", "tr")),
            P(None, ("grp", "tr")),
            P(("grp", "tr"), None, None),
            P(("grp", "tr")),
            P(("grp", "tr")),
        ),
        out_specs=P("root", ("grp", "tr")),
        check_vma=False,
    )
```

profile of v0, /device:TPU:0, one launch (start us, length us, event | category | flops | bytes accessed | tf_op | source)
XLA Modules:
  0.0 140.2 jit_solution(10332493646921314701)
XLA Ops:
  0.0 0.0 copy-start.2
  0.0 6.0 %collective-permute-start = (bf16[512,512]{1,0:T(8,128)(2,1)}, bf16[512,512]{1,0:T(8,128)(2,1)S(1)}, u32[]{:S(2)}, u32[]{:S(2)}) collective-permute-start(bf16[512,512]{1,0:T(8,128)(2,1)} %bitcast.28), channel_id=1, source_target_pairs={{2,0},{4,2},{6,4},{8,6},{10,8},{12,10},{14,12},{0,14},{3,1},{5,3},... | collective-permute-start | bytes 1572872 | tf_op jit(solution)/shard_map/ppermute | solution.py:14
  6.0 0.4 collective-permute-start.1
  6.4 0.0 collective-permute-start.2
  6.4 0.7 broadcast_compare_fusion
  7.1 11.6 %collective-permute-done = bf16[512,512]{1,0:T(8,128)(2,1)S(1)} collective-permute-done((bf16[512,512]{1,0:T(8,128)(2,1)}, bf16[512,512]{1,0:T(8,128)(2,1)S(1)}, u32[]{:S(2)}, u32[]{:S(2)}) %collective-permute-start) | collective-permute-done | bytes 524320 | tf_op jit(solution)/shard_map/ppermute | solution.py:14
  18.7 11.2 %collective-permute-done.1 = bf16[512,512]{1,0:T(8,128)(2,1)S(1)} collective-permute-done((bf16[512,512]{1,0:T(8,128)(2,1)}, bf16[512,512]{1,0:T(8,128)(2,1)S(1)}, u32[]{:S(2)}, u32[]{:S(2)}) %collective-permute-start.1) | collective-permute-done | bytes 524320 | tf_op jit(solution)/shard_map/ppermute | solution.py:14
  29.9 10.1 %collective-permute-done.2 = bf16[512,512]{1,0:T(8,128)(2,1)S(1)} collective-permute-done((bf16[512,512]{1,0:T(8,128)(2,1)}, bf16[512,512]{1,0:T(8,128)(2,1)S(1)}, u32[]{:S(2)}, u32[]{:S(2)}) %collective-permute-start.2) | collective-permute-done | bytes 524320 | tf_op jit(solution)/shard_map/ppermute | solution.py:14
  40.0 1.3 pad_maximum_fusion
  41.3 0.0 copy-done.2
  41.3 0.0 copy-start.3
  41.3 1.5 %fusion.1 = bf16[8,512,512]{2,0,1:T(8,128)(2,1)S(1)} fusion(bf16[4,512,512]{2,1,0:T(8,128)(2,1)S(1)} %pad_maximum_fusion, s32[8]{0:T(128)S(1)} %copy-done.2), kind=kOutput, calls=%fused_computation.5 | convolution fusion | flops 16777248 | bytes 6291488 | tf_op jit(solution)/shard_map/jd,dbc->jbc/dot_general | solution.py:29
  42.9 0.0 copy-done.3
  42.9 0.0 copy-start
  42.9 2.5 %fusion.5 = f32[8,8,8,512]{3,2,1,0:T(8,128)S(1)} fusion(bf16[8,512,512]{2,0,1:T(8,128)(2,1)S(1)} %fusion.1, bf16[8,8,8,512]{3,2,1,0:T(8,128)(2,1)S(1)} %bitcast.34, pred[8]{0:T(512)(128)(4,1)S(1)} %broadcast_compare_fusion), kind=kOutput, calls=%fused_computation.9 | convolution fusion | flops 268959744 | bytes 5767176 | tf_op jit(solution)/shard_map/rjb,jbc->rjc/dot_general | solution.py:32
  45.3 0.1 copy.12
  45.4 0.0 copy-done
  45.4 1.4 %fusion.10 = f32[64,512]{1,0:T(8,128)S(1)} fusion(bf16[512,4096]{1,0:T(8,128)(2,1)S(1)} %copy-done, f32[64,4096]{1,0:T(8,128)S(1)} %bitcast.26), kind=kOutput, calls=%fused_computation.14 | convolution fusion | flops 268697600 | bytes 5373952 | tf_op jit(solution)/shard_map/dot_general | solution.py:39
  46.8 50.4 %all-reduce.2 = bf16[64,512]{1,0:T(8,128)(2,1)S(1)} all-reduce(f32[64,512]{1,0:T(8,128)S(1)} %fusion.10), channel_id=1, replica_groups=mesh['grp'=2,'tr'=8,'root'=2] {'tr'}, use_global_device_ids=true, to_apply=%region_0.1 | all-reduce | flops 32768 | bytes 196608 | tf_op jit(solution)/shard_map/psum | solution.py:42
  97.2 0.0 copy-start.1
  97.2 3.2 %convolution_subtract_fusion.1 = f32[64,4096]{1,0:T(8,128)S(1)} fusion(f32[64,4096]{1,0:T(8,128)S(1)} %bitcast.27, bf16[512,4096]{1,0:T(8,128)(2,1)} %param.6, bf16[64,512]{1,0:T(8,128)(2,1)S(1)} %all-reduce.2), kind=kOutput, calls=%fused_computation.2 | convolution fusion | flops 268697600 | bytes 6356992 | tf_op jit(solution)/shard_map/dot_general | solution.py:44
  100.4 0.3 copy-done.1
  100.7 1.4 fusion.8
  102.1 34.1 %all-reduce.3 = bf16[64,512]{1,0:T(8,128)(2,1)S(1)} all-reduce(f32[64,512]{1,0:T(8,128)S(1)} %fusion.8), channel_id=1, replica_groups=mesh['grp'=2,'tr'=8,'root'=2] {'tr'}, use_global_device_ids=true, to_apply=%region_1.2 | all-reduce | flops 32768 | bytes 196608 | tf_op jit(solution)/shard_map/psum | solution.py:42
  136.2 4.0 %convolution_subtract_fusion = f32[64,4096]{1,0:T(8,128)} fusion(f32[64,4096]{1,0:T(8,128)S(1)} %convolution_subtract_fusion.1, bf16[512,4096]{1,0:T(8,128)(2,1)} %param.6, bf16[64,512]{1,0:T(8,128)(2,1)S(1)} %all-reduce.3), kind=kOutput, calls=%fused_computation.1 | convolution fusion | flops 268697600 | bytes 6356992 | tf_op jit(solution)/shard_map/dot_general | solution.py:44
Async XLA Ops:
  0.0 41.3 %copy-start.2 = (s32[8]{0:T(128)S(1)}, s32[8]{0:T(128)}, u32[]{:S(2)}) copy-start(s32[8]{0:T(128)} %param.8) | copy-start | bytes 100
  0.0 18.7 %collective-permute-start = (bf16[512,512]{1,0:T(8,128)(2,1)}, bf16[512,512]{1,0:T(8,128)(2,1)S(1)}, u32[]{:S(2)}, u32[]{:S(2)}) collective-permute-start(bf16[512,512]{1,0:T(8,128)(2,1)} %bitcast.28), channel_id=1, source_target_pairs={{2,0},{4,2},{6,4},{8,6},{10,8},{12,10},{14,12},{0,14},{3,1},{5,3},... | collective-permute-start | bytes 1572872 | tf_op jit(solution)/shard_map/ppermute | solution.py:14
  6.0 23.9 %collective-permute-start.1 = (bf16[512,512]{1,0:T(8,128)(2,1)}, bf16[512,512]{1,0:T(8,128)(2,1)S(1)}, u32[]{:S(2)}, u32[]{:S(2)}) collective-permute-start(bf16[512,512]{1,0:T(8,128)(2,1)} %bitcast.29), channel_id=1, source_target_pairs={{4,0},{6,2},{8,4},{10,6},{12,8},{14,10},{0,12},{2,14},{5,1},{7,3},... | collective-permute-start | bytes 1572872 | tf_op jit(solution)/shard_map/ppermute | solution.py:14
  6.4 33.6 %collective-permute-start.2 = (bf16[512,512]{1,0:T(8,128)(2,1)}, bf16[512,512]{1,0:T(8,128)(2,1)S(1)}, u32[]{:S(2)}, u32[]{:S(2)}) collective-permute-start(bf16[512,512]{1,0:T(8,128)(2,1)} %bitcast.30), channel_id=1, source_target_pairs={{6,0},{8,2},{10,4},{12,6},{14,8},{0,10},{2,12},{4,14},{7,1},{9,3},... | collective-permute-start | bytes 1572872 | tf_op jit(solution)/shard_map/ppermute | solution.py:14
  41.3 1.5 %copy-start.3 = (bf16[64,4096]{1,0:T(8,128)(2,1)S(1)}, bf16[64,4096]{1,0:T(8,128)(2,1)}, u32[]{:S(2)}) copy-start(bf16[64,4096]{1,0:T(8,128)(2,1)} %param.5) | copy-start | bytes 1572868
  42.9 2.6 %copy-start = (bf16[512,4096]{1,0:T(8,128)(2,1)S(1)}, bf16[512,4096]{1,0:T(8,128)(2,1)}, u32[]{:S(2)}) copy-start(bf16[512,4096]{1,0:T(8,128)(2,1)} %param.6) | copy-start | bytes 12582916
  97.2 3.5 %copy-start.1 = (bf16[512,4096]{1,0:T(8,128)(2,1)S(1)}, bf16[512,4096]{1,0:T(8,128)(2,1)}, u32[]{:S(2)}) copy-start(bf16[512,4096]{1,0:T(8,128)(2,1)} %param.6) | copy-start | bytes 12582916
where the time goes:
time: 140 us
  blocking collectives  84.5 us (60%)
  waiting for transfers between devices  32.9 us (24%)
  matrix products  14 us (10%)
  starting transfers between devices  6.43 us (5%)
  other arithmetic  1.96 us (1%)
    psum x2, blocking collectives, per_device(): correlation = lax.psum(partial_correlation, 'tr')  84.5 us
    ppermute x3, waiting for transfers between devices, from_behind(): return lax.ppermute(block, axis, route)  32.9 us
    dot_general x2, matrix products, per_device(): jnp.dot(coefficients, subspace, preferred_element_type=jnp.float32)  7.19 us
    ppermute x3, starting transfers between devices, from_behind(): return lax.ppermute(block, axis, route)  6.43 us
    dot_general x2, matrix products, per_device(): lax.dot_general(rounded, subspace, (((1,), (1,)), ((), ())), preferred_el...  2.8 us
  transfers between devices with their start and end apart: 3, of which 3 were waited for; matrix products, arithmetic and copies ran while one was open for 0% of the time, Pallas kernels for 0%

commit v1 on v0

v1 whole, which is shorter than its diff:
```python
import jax
import jax.numpy as jnp
from jax import lax
from jax.experimental import pallas as pl
from jax.experimental.pallas import tpu as pltpu
from jax.sharding import PartitionSpec as P

OFFS = 4
F32 = jnp.float32
BF16 = jnp.bfloat16
VMEM = pl.BlockSpec(memory_space=pltpu.VMEM)
SMEM = pl.BlockSpec(memory_space=pltpu.SMEM)
ACROSS = (((1,), (1,)), ((), ()))


def from_ahead(block, distance):
    n = lax.axis_size("tr")
    return lax.ppermute(block, "tr", [((i + distance) % n, i) for i in range(n)])


def other_core(block):
    return lax.ppermute(block, "root", [(0, 1), (1, 0)])


def sum_over_tr(part):
    n = lax.axis_size("tr")
    step = 1
    while step < n:
        part = part + lax.ppermute(part, "tr", [(i, i ^ step) for i in range(n)])
        step *= 2
    return part


def precond_kernel(
    offset_ref, listed_ref, core_ref, residual_ref, subspace_ref, own_ref,
    *rest,
):
    halves, (precond_ref, corr_ref, total_ref) = rest[:-3], rest[-3:]
    size = own_ref.shape[0]
    half = halves[0].shape[0]
    mine = core_ref[0] * half
    total_ref[...] = jnp.zeros_like(total_ref)

    @pl.loop(0, residual_ref.shape[1] // size)
    def _(b):
        base = b * size
        columns = pl.ds(pl.multiple_of(base, size), size)
        of_mine = pl.ds(pl.multiple_of(base + mine, half), half)
        of_other = pl.ds(pl.multiple_of(base + half - mine, half), half)
        marked = listed_ref[b] > 0
        offset = offset_ref[b]

        @pl.when(jnp.logical_not(marked))
        def _():
            precond_ref[:, columns] = residual_ref[:, columns].astype(F32)

        @pl.when(jnp.logical_and(marked, offset == 0))
        def _():
            precond_ref[:, columns] = jnp.dot(
                residual_ref[:, columns], own_ref[...], preferred_element_type=F32
            )

        for distance in range(1, OFFS):
            @pl.when(jnp.logical_and(marked, offset == distance))
            def _():
                precond_ref[:, columns] = jnp.dot(
                    residual_ref[:, of_mine], halves[2 * distance - 2][...], preferred_element_type=F32
                ) + jnp.dot(
                    residual_ref[:, of_other], halves[2 * distance - 1][...], preferred_element_type=F32
                )

        total_ref[...] += lax.dot_general(
            precond_ref[:, columns].astype(BF16), subspace_ref[:, columns], ACROSS,
            preferred_element_type=F32,
        )

    corr_ref[...] = total_ref[...].astype(corr_ref.dtype)


def first_kernel(width, precond_ref, coef_ref, subspace_ref, first_ref, corr_ref, total_ref):
    total_ref[...] = jnp.zeros_like(total_ref)

    @pl.loop(0, precond_ref.shape[1] // width)
    def _(b):
        columns = pl.ds(pl.multiple_of(b * width, width), width)
        basis = subspace_ref[:, columns]
        first = precond_ref[:, columns] - jnp.dot(coef_ref[...], basis, preferred_element_type=F32)
        first_ref[:, columns] = first
        total_ref[...] += lax.dot_general(first.astype(BF16), basis, ACROSS, preferred_element_type=F32)

    corr_ref[...] = total_ref[...].astype(corr_ref.dtype)


def last_kernel(width, first_ref, coef_ref, subspace_ref, out_ref):
    @pl.loop(0, first_ref.shape[1] // width)
    def _(b):
        columns = pl.ds(pl.multiple_of(b * width, width), width)
        out_ref[:, columns] = first_ref[:, columns] - jnp.dot(
            coef_ref[...], subspace_ref[:, columns], preferred_element_type=F32
        )


PARAMS = pltpu.CompilerParams(vmem_limit_bytes=24 * 1024 * 1024)


def per_device(residual, subspace, inverses, owner_offset, listed):
    roots, columns = residual.shape
    vectors = subspace.shape[0]
    inverse = inverses[0]
    size = inverse.shape[0]
    core = lax.axis_index("root")
    half = size // lax.axis_size("root")
    my_half = lax.dynamic_slice_in_dim(inverse, core * half, half, 0)
    fetched = [from_ahead(my_half, distance) for distance in range(1, OFFS)]
    halves = []
    for block in fetched:
        halves += [block, other_core(block)]

    corr_shape = jax.ShapeDtypeStruct((roots, vectors), BF16)
    wide = jax.ShapeDtypeStruct((roots, columns), F32)
    total = [pltpu.VMEM((roots, vectors), F32)]
    precond, corr = pl.pallas_call(
        precond_kernel,
        out_shape=(wide, corr_shape),
        in_specs=[SMEM] * 3 + [VMEM] * (3 + len(halves)),
        out_specs=(VMEM, VMEM),
        scratch_shapes=total,
        compiler_params=PARAMS,
    )(owner_offset, listed, core.astype(jnp.int32)[None], residual, subspace, inverse, *halves)
    coef = sum_over_tr(corr)

    def body(kernel):
        def call(*refs):
            kernel(size, *refs)
        return call

    first, corr = pl.pallas_call(
        body(first_kernel),
        out_shape=(wide, corr_shape),
        in_specs=[VMEM] * 3,
        out_specs=(VMEM, VMEM),
        scratch_shapes=total,
        compiler_params=PARAMS,
    )(precond, coef, subspace)
    coef = sum_over_tr(corr)
    return pl.pallas_call(
        body(last_kernel),
        out_shape=wide,
        in_specs=[VMEM] * 3,
        out_specs=VMEM,
        compiler_params=PARAMS,
    )(first, coef, subspace)


def solution(mesh):
    return jax.shard_map(
        per_device,
        mesh=mesh,
        in_specs=(
            P("root", ("grp", "tr")),
            P(None, ("grp", "tr")),
            P(("grp", "tr"), None, None),
            P(("grp", "tr")),
            P(("grp", "tr")),
        ),
        out_specs=P("root", ("grp", "tr")),
        check_vma=False,
    )
```

time: 140 us -> 75.1 us (0.54)
  blocking collectives: 84.5 us -> 0 us
  starting transfers between devices: 6.43 us -> 26.8 us
  matrix products: 14 us -> 0 us
  Pallas kernels: 0 us -> 10 us
  local copies, waits for them, and re-layouts: 0.34 us -> 6.55 us
  other arithmetic: 1.96 us -> 0.11 us
  waiting for transfers between devices: 32.9 us -> 31.3 us
    psum x2 -> x0, blocking collectives: 84.5 us -> none  [per_device(): correlation = lax.psum(partial_correlation, 'tr')]
    ppermute x3 -> x12, starting transfers between devices: 6.43 us -> 26.8 us  [the longest x6 19.9 us: sum_over_tr(): part = part + lax.ppermute(part, 'tr', [(i, i ^ step) for i in range(n)])]
    dot_general x6 -> x0, matrix products: 14 us -> none  [the longest x2 7.19 us: per_device(): jnp.dot(coefficients, subspace, preferred_element_type=jnp.float32)]
    pallas_call x0 -> x3, Pallas kernels: none -> 10 us  [the longest x1 4.05 us: per_device(): pl.pallas_call(precond_kernel, out_shape=(wide, corr_shape), in_specs=[SM...]
    unnamed x8 -> x12, local copies, waits for them, and re-layouts: 0.27 us -> 5.58 us
    ppermute x3 -> x12, waiting for transfers between devices: 32.9 us -> 31.3 us  [the longest x3 15 us: from_ahead(): lax.ppermute(block, 'tr', [((i + distance) % n, i) for i in range(n)])]
  transfers between devices with their start and end apart: 3 -> 12, of which waited for: 3 -> 10; matrix products, arithmetic and copies ran while one was open for 0% -> 0% of each run, Pallas kernels for 0% -> 0%
where the time goes in v1:
time: 75.1 us; the launch traced here: 74.8 us
  waiting for transfers between devices  31.3 us (42%)
  starting transfers between devices  26.8 us (36%)
  Pallas kernels  10 us (13%)
  local copies, waits for them, and re-layouts  6.55 us (9%)
    ppermute x6, starting transfers between devices, sum_over_tr(): part = part + lax.ppermute(part, 'tr', [(i, i ^ step) for i in range(n)])  19.9 us
    ppermute x3, waiting for transfers between devices, from_ahead(): lax.ppermute(block, 'tr', [((i + distance) % n, i) for i in range(n)])  15 us
    ppermute x6, waiting for transfers between devices, sum_over_tr(): part = part + lax.ppermute(part, 'tr', [(i, i ^ step) for i in range(n)])  14.8 us
    ppermute x3, starting transfers between devices, from_ahead(): lax.ppermute(block, 'tr', [((i + distance) % n, i) for i in range(n)])  6.9 us
    unnamed x12, local copies, waits for them, and re-layouts  5.58 us
    pallas_call x1, Pallas kernels, per_device(): pl.pallas_call(precond_kernel, out_shape=(wide, corr_shape), in_specs=[SM...  4.05 us
    pallas_call x1, Pallas kernels, per_device(): pl.pallas_call(body(first_kernel), out_shape=(wide, corr_shape), in_specs...  3.31 us
    pallas_call x1, Pallas kernels, per_device(): pl.pallas_call(body(last_kernel), out_shape=wide, in_specs=[VMEM] * 3, ou...  2.69 us
  transfers between devices with their start and end apart: 12, of which 10 were waited for; matrix products, arithmetic and copies ran while one was open for 0% of the time, Pallas kernels for 0%

profile of v1, /device:TPU:0, one launch (start us, length us, event | category | flops | bytes accessed | tf_op | source)
XLA Modules:
  0.0 74.8 jit_solution(864492626943485820)
XLA Ops:
  0.0 1.0 %dynamic-slice_bitcast_fusion = bf16[256,512]{1,0:T(8,128)(2,1)S(1)} fusion(bf16[1,512,512]{2,1,0:T(8,128)(2,1)} %param.7, s32[]{:T(128)S(6)} %select_n.3), kind=kLoop, calls=%fused_computation | loop fusion | bytes 524292 | tf_op jit(solution)/shard_map/dynamic_slice | solution.py:113
  1.0 5.0 %collective-permute-start.4 = (bf16[256,512]{1,0:T(8,128)(2,1)S(1)}, bf16[256,512]{1,0:T(8,128)(2,1)S(1)}, u32[]{:S(2)}, u32[]{:S(2)}) collective-permute-start(bf16[256,512]{1,0:T(8,128)(2,1)S(1)} %dynamic-slice_bitcast_fusion), channel_id=1, source_target_pairs={{6,0},{8,2},{10,4},{12,6},{14,8},{0,10},{2,12},{4,14},{7,1},{9,3},... | collective-permute-start | bytes 786440 | tf_op jit(solution)/shard_map/ppermute | solution.py:18
  6.0 1.3 %collective-permute-start.2 = (bf16[256,512]{1,0:T(8,128)(2,1)S(1)}, bf16[256,512]{1,0:T(8,128)(2,1)S(1)}, u32[]{:S(2)}, u32[]{:S(2)}) collective-permute-start(bf16[256,512]{1,0:T(8,128)(2,1)S(1)} %dynamic-slice_bitcast_fusion), channel_id=1, source_target_pairs={{4,0},{6,2},{8,4},{10,6},{12,8},{14,10},{0,12},{2,14},{5,1},{7,3},... | collective-permute-start | bytes 786440 | tf_op jit(solution)/shard_map/ppermute | solution.py:18
  7.3 0.5 collective-permute-start
  7.9 4.9 %collective-permute-done.4.rest_4_ = bf16[256,512]{1,0:T(8,128)(2,1)S(1)} collective-permute-done((bf16[256,512]{1,0:T(8,128)(2,1)S(1)}, bf16[256,512]{1,0:T(8,128)(2,1)S(1)}, u32[]{:S(2)}, u32[]{:S(2)}) %collective-permute-start.4) | collective-permute-done | bytes 262176 | tf_op jit(solution)/shard_map/ppermute | solution.py:18
  12.7 0.0 collective-permute-start.5
  12.7 7.0 %collective-permute-done.2.rest_2_ = bf16[256,512]{1,0:T(8,128)(2,1)S(1)} collective-permute-done((bf16[256,512]{1,0:T(8,128)(2,1)S(1)}, bf16[256,512]{1,0:T(8,128)(2,1)S(1)}, u32[]{:S(2)}, u32[]{:S(2)}) %collective-permute-start.2) | collective-permute-done | bytes 262176 | tf_op jit(solution)/shard_map/ppermute | solution.py:18
  19.7 0.0 collective-permute-start.3
  19.7 3.1 %collective-permute-done.rest_0_ = bf16[256,512]{1,0:T(8,128)(2,1)S(1)} collective-permute-done((bf16[256,512]{1,0:T(8,128)(2,1)S(1)}, bf16[256,512]{1,0:T(8,128)(2,1)S(1)}, u32[]{:S(2)}, u32[]{:S(2)}) %collective-permute-start) | collective-permute-done | bytes 262176 | tf_op jit(solution)/shard_map/ppermute | solution.py:18
  22.8 0.0 collective-permute-start.1
  22.8 0.0 collective-permute-done.5.rest_5_
  22.8 1.5 %collective-permute-done.1.rest_1_ = bf16[256,512]{1,0:T(8,128)(2,1)S(1)} collective-permute-done((bf16[256,512]{1,0:T(8,128)(2,1)S(1)}, bf16[256,512]{1,0:T(8,128)(2,1)S(1)}, u32[]{:S(2)}, u32[]{:S(2)}) %collective-permute-start.1) | collective-permute-done | bytes 262176 | tf_op jit(solution)/shard_map/ppermute | solution.py:22
  24.4 2.2 %copy-done = bf16[512,4096]{1,0:T(8,128)(2,1)S(1)} copy-done((bf16[512,4096]{1,0:T(8,128)(2,1)S(1)}, bf16[512,4096]{1,0:T(8,128)(2,1)}, u32[]{:S(2)}) %copy-start) | copy-done | bytes 4194328
  26.6 1.0 %copy-done.2 = bf16[1,512,512]{2,1,0:T(8,128)(2,1)S(1)} copy-done((bf16[1,512,512]{2,1,0:T(8,128)(2,1)S(1)}, bf16[1,512,512]{2,1,0:T(8,128)(2,1)}, u32[]{:S(2)}) %copy-start.2) | copy-done | bytes 524312
  27.6 1.0 %copy-done.3 = bf16[64,4096]{1,0:T(8,128)(2,1)S(1)} copy-done((bf16[64,4096]{1,0:T(8,128)(2,1)S(1)}, bf16[64,4096]{1,0:T(8,128)(2,1)}, u32[]{:S(2)}) %copy-start.3) | copy-done | bytes 524312
  28.6 0.7 copy-done.4
  29.3 0.7 copy-done.5
  30.0 4.0 %shard_map.55 = (f32[64,4096]{1,0:T(8,128)S(1)}, bf16[64,512]{1,0:T(8,128)(2,1)S(1)}) custom-call(s32[8]{0:T(128)S(1)} %copy-done.4, s32[8]{0:T(128)S(1)} %copy-done.5, s32[1]{0:T(128)} %bitcast.core_ref, bf16[64,4096]{1,0:T(8,128)(2,1)S(1)} %copy-done.3, bf16[512,4096]{1,0:T(8,128)(2,1)S(1)} %copy-done, bf16[512,512]{1,0:T(8,128)(2,1)S(1)} %bitcast.4, ...), custom_call_target="tpu_custom_call" | custom-call | tf_op jit(solution)/shard_map/pallas_call | solution.py:122
  34.0 2.8 %collective-permute-start.6 = (bf16[64,512]{1,0:T(8,128)(2,1)S(1)}, bf16[64,512]{1,0:T(8,128)(2,1)S(1)}, u32[]{:S(2)}, u32[]{:S(2)}) collective-permute-start(bf16[64,512]{1,0:T(8,128)(2,1)S(1)} %get-tuple-element.10), channel_id=1, source_target_pairs={{0,2},{2,0},{4,6},{6,4},{8,10},{10,8},{12,14},{14,12},{1,3},{3,1},... | collective-permute-start | bytes 196616 | tf_op jit(solution)/shard_map/ppermute | solution.py:29
  36.8 2.4 %collective-permute-done.6 = bf16[64,512]{1,0:T(8,128)(2,1)S(1)} collective-permute-done((bf16[64,512]{1,0:T(8,128)(2,1)S(1)}, bf16[64,512]{1,0:T(8,128)(2,1)S(1)}, u32[]{:S(2)}, u32[]{:S(2)}) %collective-permute-start.6) | collective-permute-done | bytes 65568 | tf_op jit(solution)/shard_map/ppermute | solution.py:29
  39.2 7.4 %collective-permute-start.7 = (bf16[64,512]{1,0:T(8,128)(2,1)S(1)}, bf16[64,512]{1,0:T(8,128)(2,1)S(1)}, u32[]{:S(2)}, u32[]{:S(2)}) collective-permute-start(bf16[64,512]{1,0:T(8,128)(2,1)S(1)} %add.22), channel_id=1, source_target_pairs={{0,4},{2,6},{4,0},{6,2},{8,12},{10,14},{12,8},{14,10},{1,5},{3,7},... | collective-permute-start | bytes 196616 | tf_op jit(solution)/shard_map/ppermute | solution.py:29
  46.6 2.2 %collective-permute-done.7 = bf16[64,512]{1,0:T(8,128)(2,1)S(1)} collective-permute-done((bf16[64,512]{1,0:T(8,128)(2,1)S(1)}, bf16[64,512]{1,0:T(8,128)(2,1)S(1)}, u32[]{:S(2)}, u32[]{:S(2)}) %collective-permute-start.7) | collective-permute-done | bytes 65568 | tf_op jit(solution)/shard_map/ppermute | solution.py:29
  48.9 3.0 %collective-permute-start.8 = (bf16[64,512]{1,0:T(8,128)(2,1)S(1)}, bf16[64,512]{1,0:T(8,128)(2,1)S(1)}, u32[]{:S(2)}, u32[]{:S(2)}) collective-permute-start(bf16[64,512]{1,0:T(8,128)(2,1)S(1)} %add.23), channel_id=1, source_target_pairs={{0,8},{2,10},{4,12},{6,14},{8,0},{10,2},{12,4},{14,6},{1,9},{3,11}... | collective-permute-start | bytes 196616 | tf_op jit(solution)/shard_map/ppermute | solution.py:29
  51.9 2.2 %collective-permute-done.8 = bf16[64,512]{1,0:T(8,128)(2,1)S(1)} collective-permute-done((bf16[64,512]{1,0:T(8,128)(2,1)S(1)}, bf16[64,512]{1,0:T(8,128)(2,1)S(1)}, u32[]{:S(2)}, u32[]{:S(2)}) %collective-permute-start.8) | collective-permute-done | bytes 65568 | tf_op jit(solution)/shard_map/ppermute | solution.py:29
  54.2 3.3 %shard_map.56 = (f32[64,4096]{1,0:T(8,128)S(1)}, bf16[64,512]{1,0:T(8,128)(2,1)S(1)}) custom-call(f32[64,4096]{1,0:T(8,128)S(1)} %get-tuple-element.9.refs_0_, bf16[64,512]{1,0:T(8,128)(2,1)S(1)} %add.24.refs_1_, bf16[512,4096]{1,0:T(8,128)(2,1)S(1)} %copy-done.1), custom_call_target="tpu_custom_call" | custom-call | tf_op jit(solution)/shard_map/pallas_call | solution.py:137
  57.5 2.0 %collective-permute-start.9 = (bf16[64,512]{1,0:T(8,128)(2,1)S(1)}, bf16[64,512]{1,0:T(8,128)(2,1)S(1)}, u32[]{:S(2)}, u32[]{:S(2)}) collective-permute-start(bf16[64,512]{1,0:T(8,128)(2,1)S(1)} %get-tuple-element.12), channel_id=1, source_target_pairs={{0,2},{2,0},{4,6},{6,4},{8,10},{10,8},{12,14},{14,12},{1,3},{3,1},... | collective-permute-start | bytes 196616 | tf_op jit(solution)/shard_map/ppermute | solution.py:29
  59.4 2.4 %collective-permute-done.9 = bf16[64,512]{1,0:T(8,128)(2,1)S(1)} collective-permute-done((bf16[64,512]{1,0:T(8,128)(2,1)S(1)}, bf16[64,512]{1,0:T(8,128)(2,1)S(1)}, u32[]{:S(2)}, u32[]{:S(2)}) %collective-permute-start.9) | collective-permute-done | bytes 65568 | tf_op jit(solution)/shard_map/ppermute | solution.py:29
  61.8 2.1 %collective-permute-start.10 = (bf16[64,512]{1,0:T(8,128)(2,1)S(1)}, bf16[64,512]{1,0:T(8,128)(2,1)S(1)}, u32[]{:S(2)}, u32[]{:S(2)}) collective-permute-start(bf16[64,512]{1,0:T(8,128)(2,1)S(1)} %add.25), channel_id=1, source_target_pairs={{0,4},{2,6},{4,0},{6,2},{8,12},{10,14},{12,8},{14,10},{1,5},{3,7},... | collective-permute-start | bytes 196616 | tf_op jit(solution)/shard_map/ppermute | solution.py:29
  63.9 2.9 %collective-permute-done.10 = bf16[64,512]{1,0:T(8,128)(2,1)S(1)} collective-permute-done((bf16[64,512]{1,0:T(8,128)(2,1)S(1)}, bf16[64,512]{1,0:T(8,128)(2,1)S(1)}, u32[]{:S(2)}, u32[]{:S(2)}) %collective-permute-start.10) | collective-permute-done | bytes 65568 | tf_op jit(solution)/shard_map/ppermute | solution.py:29
  66.9 2.6 %collective-permute-start.11 = (bf16[64,512]{1,0:T(8,128)(2,1)S(1)}, bf16[64,512]{1,0:T(8,128)(2,1)S(1)}, u32[]{:S(2)}, u32[]{:S(2)}) collective-permute-start(bf16[64,512]{1,0:T(8,128)(2,1)S(1)} %add.26), channel_id=1, source_target_pairs={{0,8},{2,10},{4,12},{6,14},{8,0},{10,2},{12,4},{14,6},{1,9},{3,11}... | collective-permute-start | bytes 196616 | tf_op jit(solution)/shard_map/ppermute | solution.py:29
  69.5 2.6 %collective-permute-done.11 = bf16[64,512]{1,0:T(8,128)(2,1)S(1)} collective-permute-done((bf16[64,512]{1,0:T(8,128)(2,1)S(1)}, bf16[64,512]{1,0:T(8,128)(2,1)S(1)}, u32[]{:S(2)}, u32[]{:S(2)}) %collective-permute-start.11) | collective-permute-done | bytes 65568 | tf_op jit(solution)/shard_map/ppermute | solution.py:29
  72.1 2.7 %shard_map.57 = f32[64,4096]{1,0:T(8,128)} custom-call(f32[64,4096]{1,0:T(8,128)S(1)} %get-tuple-element.11.refs_0_, bf16[64,512]{1,0:T(8,128)(2,1)S(1)} %add.27.refs_1_, bf16[512,4096]{1,0:T(8,128)(2,1)S(1)} %copy-done.1), custom_call_target="tpu_custom_call" | custom-call | tf_op jit(solution)/shard_map/pallas_call | solution.py:146
  (14 shorter events, 0.1 us)
Async XLA Ops:
  1.0 11.8 %collective-permute-start.4 = (bf16[256,512]{1,0:T(8,128)(2,1)S(1)}, bf16[256,512]{1,0:T(8,128)(2,1)S(1)}, u32[]{:S(2)}, u32[]{:S(2)}) collective-permute-start(bf16[256,512]{1,0:T(8,128)(2,1)S(1)} %dynamic-slice_bitcast_fusion), channel_id=1, source_target_pairs={{6,0},{8,2},{10,4},{12,6},{14,8},{0,10},{2,12},{4,14},{7,1},{9,3},... | collective-permute-start | bytes 786440 | tf_op jit(solution)/shard_map/ppermute | solution.py:18
  6.0 13.7 %collective-permute-start.2 = (bf16[256,512]{1,0:T(8,128)(2,1)S(1)}, bf16[256,512]{1,0:T(8,128)(2,1)S(1)}, u32[]{:S(2)}, u32[]{:S(2)}) collective-permute-start(bf16[256,512]{1,0:T(8,128)(2,1)S(1)} %dynamic-slice_bitcast_fusion), channel_id=1, source_target_pairs={{4,0},{6,2},{8,4},{10,6},{12,8},{14,10},{0,12},{2,14},{5,1},{7,3},... | collective-permute-start | bytes 786440 | tf_op jit(solution)/shard_map/ppermute | solution.py:18
  7.3 15.5 %collective-permute-start = (bf16[256,512]{1,0:T(8,128)(2,1)S(1)}, bf16[256,512]{1,0:T(8,128)(2,1)S(1)}, u32[]{:S(2)}, u32[]{:S(2)}) collective-permute-start(bf16[256,512]{1,0:T(8,128)(2,1)S(1)} %dynamic-slice_bitcast_fusion), channel_id=1, source_target_pairs={{2,0},{4,2},{6,4},{8,6},{10,8},{12,10},{14,12},{0,14},{3,1},{5,3},... | collective-permute-start | bytes 786440 | tf_op jit(solution)/shard_map/ppermute | solution.py:18
  12.7 10.1 %collective-permute-start.5 = (bf16[256,512]{1,0:T(8,128)(2,1)S(1)}, bf16[256,512]{1,0:T(8,128)(2,1)S(1)}, u32[]{:S(2)}, u32[]{:S(2)}) collective-permute-start(bf16[256,512]{1,0:T(8,128)(2,1)S(1)} %collective-permute-done.4.rest_4_), channel_id=1, source_target_pairs={{0,1},{1,0},{2,3},{3,2},{4,5},{5,4},{6,7},{7,6},{8,9},{9,8},{10,11... | collective-permute-start | bytes 786440 | tf_op jit(solution)/shard_map/ppermute | solution.py:22
  19.7 3.1 %collective-permute-start.3 = (bf16[256,512]{1,0:T(8,128)(2,1)S(1)}, bf16[256,512]{1,0:T(8,128)(2,1)S(1)}, u32[]{:S(2)}, u32[]{:S(2)}) collective-permute-start(bf16[256,512]{1,0:T(8,128)(2,1)S(1)} %collective-permute-done.2.rest_2_), channel_id=1, source_target_pairs={{0,1},{1,0},{2,3},{3,2},{4,5},{5,4},{6,7},{7,6},{8,9},{9,8},{10,11... | collective-permute-start | bytes 786440 | tf_op jit(solution)/shard_map/ppermute | solution.py:22
  22.8 1.5 %collective-permute-start.1 = (bf16[256,512]{1,0:T(8,128)(2,1)S(1)}, bf16[256,512]{1,0:T(8,128)(2,1)S(1)}, u32[]{:S(2)}, u32[]{:S(2)}) collective-permute-start(bf16[256,512]{1,0:T(8,128)(2,1)S(1)} %collective-permute-done.rest_0_), channel_id=1, source_target_pairs={{0,1},{1,0},{2,3},{3,2},{4,5},{5,4},{6,7},{7,6},{8,9},{9,8},{10,11... | collective-permute-start | bytes 786440 | tf_op jit(solution)/shard_map/ppermute | solution.py:22
  24.4 2.2 %copy-start = (bf16[512,4096]{1,0:T(8,128)(2,1)S(1)}, bf16[512,4096]{1,0:T(8,128)(2,1)}, u32[]{:S(2)}) copy-start(bf16[512,4096]{1,0:T(8,128)(2,1)} %refs_2_.3) | copy-start | bytes 12582916
  26.6 1.0 %copy-start.2 = (bf16[1,512,512]{2,1,0:T(8,128)(2,1)S(1)}, bf16[1,512,512]{2,1,0:T(8,128)(2,1)}, u32[]{:S(2)}) copy-start(bf16[1,512,512]{2,1,0:T(8,128)(2,1)} %param.7) | copy-start | bytes 1572868
  27.6 1.0 %copy-start.3 = (bf16[64,4096]{1,0:T(8,128)(2,1)S(1)}, bf16[64,4096]{1,0:T(8,128)(2,1)}, u32[]{:S(2)}) copy-start(bf16[64,4096]{1,0:T(8,128)(2,1)} %residual_ref.1) | copy-start | bytes 1572868
  28.6 0.7 copy-start.4
  29.3 0.7 copy-start.5
  30.0 24.2 %copy-start.1 = (bf16[512,4096]{1,0:T(8,128)(2,1)S(1)}, bf16[512,4096]{1,0:T(8,128)(2,1)}, u32[]{:S(2)}) copy-start(bf16[512,4096]{1,0:T(8,128)(2,1)} %refs_2_.3) | copy-start | bytes 12582916
  34.0 5.1 %collective-permute-start.6 = (bf16[64,512]{1,0:T(8,128)(2,1)S(1)}, bf16[64,512]{1,0:T(8,128)(2,1)S(1)}, u32[]{:S(2)}, u32[]{:S(2)}) collective-permute-start(bf16[64,512]{1,0:T(8,128)(2,1)S(1)} %get-tuple-element.10), channel_id=1, source_target_pairs={{0,2},{2,0},{4,6},{6,4},{8,10},{10,8},{12,14},{14,12},{1,3},{3,1},... | collective-permute-start | bytes 196616 | tf_op jit(solution)/shard_map/ppermute | solution.py:29
  39.2 9.7 %collective-permute-start.7 = (bf16[64,512]{1,0:T(8,128)(2,1)S(1)}, bf16[64,512]{1,0:T(8,128)(2,1)S(1)}, u32[]{:S(2)}, u32[]{:S(2)}) collective-permute-start(bf16[64,512]{1,0:T(8,128)(2,1)S(1)} %add.22), channel_id=1, source_target_pairs={{0,4},{2,6},{4,0},{6,2},{8,12},{10,14},{12,8},{14,10},{1,5},{3,7},... | collective-permute-start | bytes 196616 | tf_op jit(solution)/shard_map/ppermute | solution.py:29
  48.9 5.3 %collective-permute-start.8 = (bf16[64,512]{1,0:T(8,128)(2,1)S(1)}, bf16[64,512]{1,0:T(8,128)(2,1)S(1)}, u32[]{:S(2)}, u32[]{:S(2)}) collective-permute-start(bf16[64,512]{1,0:T(8,128)(2,1)S(1)} %add.23), channel_id=1, source_target_pairs={{0,8},{2,10},{4,12},{6,14},{8,0},{10,2},{12,4},{14,6},{1,9},{3,11}... | collective-permute-start | bytes 196616 | tf_op jit(solution)/shard_map/ppermute | solution.py:29
  57.5 4.3 %collective-permute-start.9 = (bf16[64,512]{1,0:T(8,128)(2,1)S(1)}, bf16[64,512]{1,0:T(8,128)(2,1)S(1)}, u32[]{:S(2)}, u32[]{:S(2)}) collective-permute-start(bf16[64,512]{1,0:T(8,128)(2,1)S(1)} %get-tuple-element.12), channel_id=1, source_target_pairs={{0,2},{2,0},{4,6},{6,4},{8,10},{10,8},{12,14},{14,12},{1,3},{3,1},... | collective-permute-start | bytes 196616 | tf_op jit(solution)/shard_map/ppermute | solution.py:29
  61.8 5.0 %collective-permute-start.10 = (bf16[64,512]{1,0:T(8,128)(2,1)S(1)}, bf16[64,512]{1,0:T(8,128)(2,1)S(1)}, u32[]{:S(2)}, u32[]{:S(2)}) collective-permute-start(bf16[64,512]{1,0:T(8,128)(2,1)S(1)} %add.25), channel_id=1, source_target_pairs={{0,4},{2,6},{4,0},{6,2},{8,12},{10,14},{12,8},{14,10},{1,5},{3,7},... | collective-permute-start | bytes 196616 | tf_op jit(solution)/shard_map/ppermute | solution.py:29
  66.9 5.2 %collective-permute-start.11 = (bf16[64,512]{1,0:T(8,128)(2,1)S(1)}, bf16[64,512]{1,0:T(8,128)(2,1)S(1)}, u32[]{:S(2)}, u32[]{:S(2)}) collective-permute-start(bf16[64,512]{1,0:T(8,128)(2,1)S(1)} %add.26), channel_id=1, source_target_pairs={{0,8},{2,10},{4,12},{6,14},{8,0},{10,2},{12,4},{14,6},{1,9},{3,11}... | collective-permute-start | bytes 196616 | tf_op jit(solution)/shard_map/ppermute | solution.py:29

commit v2 on v1

v2 whole, which is shorter than its diff:
```python
import functools

import jax
import jax.numpy as jnp
from jax import lax
from jax.experimental import pallas as pl
from jax.experimental.pallas import tpu as pltpu
from jax.sharding import PartitionSpec as P

F32 = jnp.float32
BF16 = jnp.bfloat16
VMEM = pl.BlockSpec(memory_space=pltpu.VMEM)
SMEM = pl.BlockSpec(memory_space=pltpu.SMEM)
HBM = pl.BlockSpec(memory_space=pltpu.HBM)
ACROSS = (((1,), (1,)), ((), ()))
AHEAD, MIXED, SWAPPED = range(3)


def permute(block, source):
    n = lax.axis_size("tr")
    return lax.ppermute(block, "tr", [(source(i) % n, i) for i in range(n)])


def other_core(block):
    return lax.ppermute(block, "root", [(0, 1), (1, 0)])


def sum_over_tr(part):
    step = 1
    while step < lax.axis_size("tr"):
        part = part + permute(part, lambda i: i ^ step)
        step *= 2
    return part


def correlate(block, basis):
    return lax.dot_general(block.astype(BF16), basis, ACROSS, preferred_element_type=F32)


def chunk(b, size):
    return pl.ds(b * size, size)


def offset_of(kind):
    odd = lax.axis_index("tr") % 2
    return {AHEAD: 2, MIXED: 1 + 2 * odd, SWAPPED: 3 - 2 * odd}[kind]


def stage_kernel(
    offset_ref, listed_ref, residual_hbm, subspace_hbm, own_hbm,
    residual_ref, subspace_ref, precond_ref, corr_ref, own_ref, sems,
):
    size = own_ref.shape[0]
    count = residual_ref.shape[1] // size
    pltpu.make_async_copy(own_hbm, own_ref, sems.at[2 * count]).start()
    copies = []
    for b in range(count):
        columns = chunk(b, size)
        pair = [
            pltpu.make_async_copy(residual_hbm.at[:, columns], residual_ref.at[:, columns], sems.at[2 * b]),
            pltpu.make_async_copy(subspace_hbm.at[:, columns], subspace_ref.at[:, columns], sems.at[2 * b + 1]),
        ]
        for copy in pair:
            copy.start()
        copies.append(pair)
    corr_ref[...] = jnp.zeros_like(corr_ref)
    pltpu.make_async_copy(own_hbm, own_ref, sems.at[2 * count]).wait()
    for b in range(count):
        columns = chunk(b, size)
        for copy in copies[b]:
            copy.wait()

        listed = listed_ref[b] > 0
        own = jnp.logical_and(listed, offset_ref[b] == 0)

        @pl.when(own)
        def _():
            precond_ref[:, columns] = jnp.dot(
                residual_ref[:, columns], own_ref[...], preferred_element_type=F32
            )

        @pl.when(jnp.logical_not(listed))
        def _():
            precond_ref[:, columns] = residual_ref[:, columns].astype(F32)

        @pl.when(jnp.logical_or(own, jnp.logical_not(listed)))
        def _():
            corr_ref[...] += correlate(precond_ref[:, columns], subspace_ref[:, columns])


def fetched_kernel(kinds, offset_ref, listed_ref, residual_ref, subspace_ref, *rest):
    halves, (_, corr_in, precond_ref, corr_ref) = rest[: 2 * len(kinds)], rest[2 * len(kinds) :]
    half = halves[0].shape[0]
    size = 2 * half
    mine = lax.axis_index("root") * half
    corr_ref[...] = corr_in[...]
    for b in range(residual_ref.shape[1] // size):
        columns = chunk(b, size)
        of_mine = pl.ds(pl.multiple_of(b * size + mine, half), half)
        of_other = pl.ds(pl.multiple_of(b * size + half - mine, half), half)
        for k, kind in enumerate(kinds):
            @pl.when(jnp.logical_and(listed_ref[b] > 0, offset_ref[b] == offset_of(kind)))
            def _():
                solved = jnp.dot(
                    residual_ref[:, of_mine], halves[2 * k][...], preferred_element_type=F32
                ) + jnp.dot(
                    residual_ref[:, of_other], halves[2 * k + 1][...], preferred_element_type=F32
                )
                precond_ref[:, columns] = solved
                corr_ref[...] += correlate(solved, subspace_ref[:, columns])


def first_kernel(size, precond_ref, coef_ref, subspace_ref, first_ref, corr_ref):
    total = jnp.zeros(coef_ref.shape, F32)
    for b in range(precond_ref.shape[1] // size):
        columns = chunk(b, size)
        basis = subspace_ref[:, columns]
        first = precond_ref[:, columns] - jnp.dot(coef_ref[...], basis, preferred_element_type=F32)
        first_ref[:, columns] = first
        total += correlate(first, basis)
    corr_ref[...] = total.astype(corr_ref.dtype)


def last_kernel(size, first_ref, coef_ref, subspace_ref, out_hbm, out_ref, sems):
    copies = []
    for b in range(first_ref.shape[1] // size):
        columns = chunk(b, size)
        out_ref[:, columns] = first_ref[:, columns] - jnp.dot(
            coef_ref[...], subspace_ref[:, columns], preferred_element_type=F32
        )
        copy = pltpu.make_async_copy(out_ref.at[:, columns], out_hbm.at[:, columns], sems.at[b])
        copy.start()
        copies.append(copy)
    for copy in copies:
        copy.wait()


PARAMS = pltpu.CompilerParams(vmem_limit_bytes=24 * 1024 * 1024)


def cost(flops, bytes_accessed):
    return pl.CostEstimate(flops=flops, bytes_accessed=bytes_accessed, transcendentals=0)


def per_device(residual, subspace, inverses, owner_offset, listed):
    roots, columns = residual.shape
    vectors = subspace.shape[0]
    own = inverses[0]
    size = own.shape[0]
    count = columns // size
    core = lax.axis_index("root").astype(jnp.int32)
    half = size // lax.axis_size("root")

    wide = jax.ShapeDtypeStruct((roots, columns), F32)
    small = jax.ShapeDtypeStruct((roots, vectors), F32)
    sent = jax.ShapeDtypeStruct((roots, vectors), BF16)

    my_half = lax.dynamic_slice_in_dim(own, core * half, half, 0)
    mixed = permute(my_half, lambda i: i + 1 + 2 * (i % 2))
    ahead = permute(my_half, lambda i: i + 2)
    residual, subspace, precond, corr = pl.pallas_call(
        stage_kernel,
        out_shape=(
            jax.ShapeDtypeStruct(residual.shape, BF16),
            jax.ShapeDtypeStruct(subspace.shape, BF16),
            wide,
            small,
        ),
        in_specs=[SMEM, SMEM, HBM, HBM, HBM],
        out_specs=(VMEM,) * 4,
        scratch_shapes=[pltpu.VMEM((size, size), BF16), pltpu.SemaphoreType.DMA((2 * count + 1,))],
        cost_estimate=cost(4 * roots * vectors * columns, 16 * vectors * columns),
        compiler_params=pltpu.CompilerParams(vmem_limit_bytes=46 * 1024 * 1024),
    )(owner_offset, listed, residual, subspace, own)

    def fetched(kinds, halves, precond, corr):
        return pl.pallas_call(
            functools.partial(fetched_kernel, kinds),
            out_shape=(wide, small),
            in_specs=[SMEM] * 2 + [VMEM] * (4 + len(halves)),
            out_specs=(VMEM, VMEM),
            input_output_aliases={4 + len(halves): 0},
            cost_estimate=cost(0, 0),
            compiler_params=PARAMS,
        )(owner_offset, listed, residual, subspace, *halves, precond, corr)

    swapped = permute(ahead, lambda i: i ^ 1)
    mixed, corr = lax.optimization_barrier((mixed, corr))
    precond, corr = fetched(
        (AHEAD, MIXED, SWAPPED),
        (ahead, other_core(ahead), mixed, other_core(mixed), swapped, other_core(swapped)),
        precond, corr,
    )
    coef = sum_over_tr(corr.astype(BF16))

    def body(kernel):
        def call(*refs):
            kernel(size, *refs)
        return call

    first, corr = pl.pallas_call(
        body(first_kernel),
        out_shape=(wide, sent),
        in_specs=[VMEM] * 3,
        out_specs=(VMEM, VMEM),
        compiler_params=PARAMS,
    )(precond, coef, subspace)
    coef = sum_over_tr(corr)
    return pl.pallas_call(
        body(last_kernel),
        out_shape=wide,
        in_specs=[VMEM] * 3,
        out_specs=HBM,
        scratch_shapes=[pltpu.VMEM((roots, columns), F32), pltpu.SemaphoreType.DMA((count,))],
        compiler_params=PARAMS,
    )(first, coef, subspace)


def solution(mesh):
    return jax.shard_map(
        per_device,
        mesh=mesh,
        in_specs=(
            P("root", ("grp", "tr")),
            P(None, ("grp", "tr")),
            P(("grp", "tr"), None, None),
            P(("grp", "tr")),
            P(("grp", "tr")),
        ),
        out_specs=P("root", ("grp", "tr")),
        check_vma=False,
    )
```

time: 75.1 us -> 61.7 us (0.82)
  starting transfers between devices: 26.8 us -> 19.5 us
  waiting for transfers between devices: 31.3 us -> 26.6 us
  local copies, waits for them, and re-layouts: 6.55 us -> 4.36 us
  Pallas kernels: 10 us -> 10.8 us
    ppermute x9, starting transfers between devices: 26.8 us -> 18.9 us  [permute(): return lax.ppermute(block, 'tr', [(source(i) % n, i) for i in range(n)])]
    ppermute x9, waiting for transfers between devices: 29.8 us -> 25 us  [permute(): return lax.ppermute(block, 'tr', [(source(i) % n, i) for i in range(n)])]
    unnamed x12 -> x8, local copies, waits for them, and re-layouts: 5.58 us -> 3.39 us
    pallas_call x2 -> x3, Pallas kernels: 7.36 us -> 9.22 us  [the longest x1 3.57 us: fetched(): pl.pallas_call(functools.partial(fetched_kernel, kinds), out_shape=(wide,...]
    pallas_call x1, Pallas kernels: 2.69 us -> 1.59 us  [per_device(): pl.pallas_call(body(last_kernel), out_shape=wide, in_specs=[VMEM] * 3, ou...]
  transfers between devices with their start and end apart: 12 -> 12, of which waited for: 10 -> 9; matrix products, arithmetic and copies ran while one was open for 0% -> 0% of each run, Pallas kernels for 0% -> 5%
where the time goes in v2:
time: 61.7 us; the launch traced here: 61.5 us
  waiting for transfers between devices  26.6 us (43%)
  starting transfers between devices  19.5 us (32%)
  Pallas kernels  10.8 us (18%)
  local copies, waits for them, and re-layouts  4.36 us (7%)
    ppermute x9, waiting for transfers between devices, permute(): return lax.ppermute(block, 'tr', [(source(i) % n, i) for i in range(n)])  25 us
    ppermute x9, starting transfers between devices, permute(): return lax.ppermute(block, 'tr', [(source(i) % n, i) for i in range(n)])  18.9 us
    pallas_call x1, Pallas kernels, fetched(): pl.pallas_call(functools.partial(fetched_kernel, kinds), out_shape=(wide,...  3.57 us
    unnamed x8, local copies, waits for them, and re-layouts  3.39 us
    pallas_call x1, Pallas kernels, per_device(): pl.pallas_call(stage_kernel, out_shape=(jax.ShapeDtypeStruct(residual.sha...  3.23 us
    pallas_call x1, Pallas kernels, per_device(): pl.pallas_call(body(first_kernel), out_shape=(wide, sent), in_specs=[VMEM...  2.42 us
    pallas_call x1, Pallas kernels, per_device(): pl.pallas_call(body(last_kernel), out_shape=wide, in_specs=[VMEM] * 3, ou...  1.59 us
    ppermute x3, waiting for transfers between devices, other_core(): return lax.ppermute(block, 'root', [(0, 1), (1, 0)])  1.53 us
  transfers between devices with their start and end apart: 12, of which 9 were waited for; matrix products, arithmetic and copies ran while one was open for 0% of the time, Pallas kernels for 5%

profile of v2, /device:TPU:0, one launch (start us, length us, event | category | flops | bytes accessed | tf_op | source)
XLA Modules:
  0.0 61.5 jit_solution(10299486820796070920)
XLA Ops:
  0.0 1.0 %dynamic-slice_bitcast_fusion = bf16[256,512]{1,0:T(8,128)(2,1)S(1)} fusion(bf16[1,512,512]{2,1,0:T(8,128)(2,1)} %param.7, s32[]{:T(128)S(6)} %select_n.3), kind=kLoop, calls=%fused_computation | loop fusion | bytes 524292 | tf_op jit(solution)/shard_map/dynamic_slice | solution.py:158
  1.0 5.1 %collective-permute-start = (bf16[256,512]{1,0:T(8,128)(2,1)S(1)}, bf16[256,512]{1,0:T(8,128)(2,1)S(1)}, u32[]{:S(2)}, u32[]{:S(2)}) collective-permute-start(bf16[256,512]{1,0:T(8,128)(2,1)S(1)} %dynamic-slice_bitcast_fusion), channel_id=1, source_target_pairs={{4,0},{6,2},{8,4},{10,6},{12,8},{14,10},{0,12},{2,14},{5,1},{7,3},... | collective-permute-start | bytes 786440 | tf_op jit(solution)/shard_map/ppermute | solution.py:21
  6.1 0.4 collective-permute-start.2
  6.4 6.4 %collective-permute-done.rest_0_ = bf16[256,512]{1,0:T(8,128)(2,1)S(1)} collective-permute-done((bf16[256,512]{1,0:T(8,128)(2,1)S(1)}, bf16[256,512]{1,0:T(8,128)(2,1)S(1)}, u32[]{:S(2)}, u32[]{:S(2)}) %collective-permute-start) | collective-permute-done | bytes 262176 | tf_op jit(solution)/shard_map/ppermute | solution.py:21
  12.8 0.3 collective-permute-start.4
  13.1 1.0 %copy-done = bf16[1,512,512]{2,1,0:T(8,128)(2,1)S(1)} copy-done((bf16[1,512,512]{2,1,0:T(8,128)(2,1)S(1)}, bf16[1,512,512]{2,1,0:T(8,128)(2,1)}, u32[]{:S(2)}) %copy-start) | copy-done | bytes 524312
  14.2 1.0 %copy-done.1 = bf16[64,4096]{1,0:T(8,128)(2,1)S(1)} copy-done((bf16[64,4096]{1,0:T(8,128)(2,1)S(1)}, bf16[64,4096]{1,0:T(8,128)(2,1)}, u32[]{:S(2)}) %copy-start.1) | copy-done | bytes 524312
  15.2 0.7 %copy-done.2 = s32[8]{0:T(128)S(1)} copy-done((s32[8]{0:T(128)S(1)}, s32[8]{0:T(128)}, u32[]{:S(2)}) %copy-start.2) | copy-done | bytes 56
  15.9 0.7 %copy-done.3 = s32[8]{0:T(128)S(1)} copy-done((s32[8]{0:T(128)S(1)}, s32[8]{0:T(128)}, u32[]{:S(2)}) %copy-start.3) | copy-done | bytes 56
  16.5 3.2 %shard_map.55 = (bf16[64,4096]{1,0:T(8,128)(2,1)S(1)}, bf16[512,4096]{1,0:T(8,128)(2,1)S(1)}, f32[64,4096]{1,0:T(8,128)S(1)}, f32[64,512]{1,0:T(8,128)S(1)}) custom-call(s32[8]{0:T(128)S(1)} %copy-done.2, s32[8]{0:T(128)S(1)} %copy-done.3, bf16[64,4096]{1,0:T(8,128)(2,1)S(1)} %copy-done.1, bf16[512,4096]{1,0:T(8,128)(2,1)} %subspace_hbm.1, ...), custom_call_target="tpu_custom_call" | custom-call | flops 536870912 | bytes 33554432 | tf_op jit(solution)/shard_map/pallas_call | solution.py:161
  19.8 0.0 collective-permute-done.2.rest_2_
  19.8 0.1 collective-permute-start.3
  19.9 0.5 collective-permute-start.1
  20.4 2.1 %collective-permute-done.4.rest_4_ = bf16[256,512]{1,0:T(8,128)(2,1)S(1)} collective-permute-done((bf16[256,512]{1,0:T(8,128)(2,1)S(1)}, bf16[256,512]{1,0:T(8,128)(2,1)S(1)}, u32[]{:S(2)}, u32[]{:S(2)}) %collective-permute-start.4) | collective-permute-done | bytes 262176 | tf_op jit(solution)/shard_map/ppermute | solution.py:21
  22.5 0.0 collective-permute-start.5
  22.5 0.0 collective-permute-done.1.rest_1_
  22.5 1.5 %collective-permute-done.5.rest_5_ = bf16[256,512]{1,0:T(8,128)(2,1)S(1)} collective-permute-done((bf16[256,512]{1,0:T(8,128)(2,1)S(1)}, bf16[256,512]{1,0:T(8,128)(2,1)S(1)}, u32[]{:S(2)}, u32[]{:S(2)}) %collective-permute-start.5) | collective-permute-done | bytes 262176 | tf_op jit(solution)/shard_map/ppermute | solution.py:25
  24.0 3.6 %shard_map.56 = (f32[64,4096]{1,0:T(8,128)S(1)}, f32[64,512]{1,0:T(8,128)S(1)}) custom-call(s32[8]{0:T(128)S(1)} %copy-done.2, s32[8]{0:T(128)S(1)} %copy-done.3, bf16[64,4096]{1,0:T(8,128)(2,1)S(1)} %get-tuple-element.15.residual_ref, bf16[512,4096]{1,0:T(8,128)(2,1)S(1)} %get-tuple-element.16.subspace_ref.refs_2_, ...), custom_call_target="tpu_custom_call", output_to_operand_aliasing={{0}: (10, {})} | custom-call | tf_op jit(solution)/shard_map/pallas_call | solution.py:177
  27.6 1.5 %collective-permute-start.6 = (bf16[64,512]{1,0:T(8,128)(2,1)S(1)}, bf16[64,512]{1,0:T(8,128)(2,1)S(1)}, u32[]{:S(2)}, u32[]{:S(2)}) collective-permute-start(bf16[64,512]{1,0:T(8,128)(2,1)S(1)} %convert_element_type.3), channel_id=1, source_target_pairs={{2,0},{0,2},{6,4},{4,6},{10,8},{8,10},{14,12},{12,14},{3,1},{1,3},... | collective-permute-start | bytes 196616 | tf_op jit(solution)/shard_map/ppermute | solution.py:21
  29.1 2.8 %collective-permute-done.6 = bf16[64,512]{1,0:T(8,128)(2,1)S(1)} collective-permute-done((bf16[64,512]{1,0:T(8,128)(2,1)S(1)}, bf16[64,512]{1,0:T(8,128)(2,1)S(1)}, u32[]{:S(2)}, u32[]{:S(2)}) %collective-permute-start.6) | collective-permute-done | bytes 65568 | tf_op jit(solution)/shard_map/ppermute | solution.py:21
  32.0 3.4 %collective-permute-start.7 = (bf16[64,512]{1,0:T(8,128)(2,1)S(1)}, bf16[64,512]{1,0:T(8,128)(2,1)S(1)}, u32[]{:S(2)}, u32[]{:S(2)}) collective-permute-start(bf16[64,512]{1,0:T(8,128)(2,1)S(1)} %convert_add_fusion), channel_id=1, source_target_pairs={{4,0},{6,2},{0,4},{2,6},{12,8},{14,10},{8,12},{10,14},{5,1},{7,3},... | collective-permute-start | bytes 196616 | tf_op jit(solution)/shard_map/ppermute | solution.py:21
  35.4 2.2 %collective-permute-done.7 = bf16[64,512]{1,0:T(8,128)(2,1)S(1)} collective-permute-done((bf16[64,512]{1,0:T(8,128)(2,1)S(1)}, bf16[64,512]{1,0:T(8,128)(2,1)S(1)}, u32[]{:S(2)}, u32[]{:S(2)}) %collective-permute-start.7) | collective-permute-done | bytes 65568 | tf_op jit(solution)/shard_map/ppermute | solution.py:21
  37.7 2.2 %collective-permute-start.8 = (bf16[64,512]{1,0:T(8,128)(2,1)S(1)}, bf16[64,512]{1,0:T(8,128)(2,1)S(1)}, u32[]{:S(2)}, u32[]{:S(2)}) collective-permute-start(bf16[64,512]{1,0:T(8,128)(2,1)S(1)} %add.23), channel_id=1, source_target_pairs={{8,0},{10,2},{12,4},{14,6},{0,8},{2,10},{4,12},{6,14},{9,1},{11,3}... | collective-permute-start | bytes 196616 | tf_op jit(solution)/shard_map/ppermute | solution.py:21
  39.8 3.0 %collective-permute-done.8 = bf16[64,512]{1,0:T(8,128)(2,1)S(1)} collective-permute-done((bf16[64,512]{1,0:T(8,128)(2,1)S(1)}, bf16[64,512]{1,0:T(8,128)(2,1)S(1)}, u32[]{:S(2)}, u32[]{:S(2)}) %collective-permute-start.8) | collective-permute-done | bytes 65568 | tf_op jit(solution)/shard_map/ppermute | solution.py:21
  42.9 2.4 %shard_map.57 = (f32[64,4096]{1,0:T(8,128)S(1)}, bf16[64,512]{1,0:T(8,128)(2,1)S(1)}) custom-call(f32[64,4096]{1,0:T(8,128)S(1)} %get-tuple-element.21.refs_0_, bf16[64,512]{1,0:T(8,128)(2,1)S(1)} %add.24.refs_1_, bf16[512,4096]{1,0:T(8,128)(2,1)S(1)} %get-tuple-element.16.subspace_ref.refs_2_), custom_call_target="tpu_custom_call" | custom-call | tf_op jit(solution)/shard_map/pallas_call | solution.py:201
  45.3 1.9 %collective-permute-start.9 = (bf16[64,512]{1,0:T(8,128)(2,1)S(1)}, bf16[64,512]{1,0:T(8,128)(2,1)S(1)}, u32[]{:S(2)}, u32[]{:S(2)}) collective-permute-start(bf16[64,512]{1,0:T(8,128)(2,1)S(1)} %get-tuple-element.24), channel_id=1, source_target_pairs={{2,0},{0,2},{6,4},{4,6},{10,8},{8,10},{14,12},{12,14},{3,1},{1,3},... | collective-permute-start | bytes 196616 | tf_op jit(solution)/shard_map/ppermute | solution.py:21
  47.3 2.4 %collective-permute-done.9 = bf16[64,512]{1,0:T(8,128)(2,1)S(1)} collective-permute-done((bf16[64,512]{1,0:T(8,128)(2,1)S(1)}, bf16[64,512]{1,0:T(8,128)(2,1)S(1)}, u32[]{:S(2)}, u32[]{:S(2)}) %collective-permute-start.9) | collective-permute-done | bytes 65568 | tf_op jit(solution)/shard_map/ppermute | solution.py:21
  49.7 2.1 %collective-permute-start.10 = (bf16[64,512]{1,0:T(8,128)(2,1)S(1)}, bf16[64,512]{1,0:T(8,128)(2,1)S(1)}, u32[]{:S(2)}, u32[]{:S(2)}) collective-permute-start(bf16[64,512]{1,0:T(8,128)(2,1)S(1)} %add.25), channel_id=1, source_target_pairs={{4,0},{6,2},{0,4},{2,6},{12,8},{14,10},{8,12},{10,14},{5,1},{7,3},... | collective-permute-start | bytes 196616 | tf_op jit(solution)/shard_map/ppermute | solution.py:21
  51.8 2.8 %collective-permute-done.10 = bf16[64,512]{1,0:T(8,128)(2,1)S(1)} collective-permute-done((bf16[64,512]{1,0:T(8,128)(2,1)S(1)}, bf16[64,512]{1,0:T(8,128)(2,1)S(1)}, u32[]{:S(2)}, u32[]{:S(2)}) %collective-permute-start.10) | collective-permute-done | bytes 65568 | tf_op jit(solution)/shard_map/ppermute | solution.py:21
  54.6 2.0 %collective-permute-start.11 = (bf16[64,512]{1,0:T(8,128)(2,1)S(1)}, bf16[64,512]{1,0:T(8,128)(2,1)S(1)}, u32[]{:S(2)}, u32[]{:S(2)}) collective-permute-start(bf16[64,512]{1,0:T(8,128)(2,1)S(1)} %add.26), channel_id=1, source_target_pairs={{8,0},{10,2},{12,4},{14,6},{0,8},{2,10},{4,12},{6,14},{9,1},{11,3}... | collective-permute-start | bytes 196616 | tf_op jit(solution)/shard_map/ppermute | solution.py:21
  56.6 3.2 %collective-permute-done.11 = bf16[64,512]{1,0:T(8,128)(2,1)S(1)} collective-permute-done((bf16[64,512]{1,0:T(8,128)(2,1)S(1)}, bf16[64,512]{1,0:T(8,128)(2,1)S(1)}, u32[]{:S(2)}, u32[]{:S(2)}) %collective-permute-start.11) | collective-permute-done | bytes 65568 | tf_op jit(solution)/shard_map/ppermute | solution.py:21
  59.9 1.6 %shard_map.58 = f32[64,4096]{1,0:T(8,128)} custom-call(f32[64,4096]{1,0:T(8,128)S(1)} %get-tuple-element.23.refs_0_, bf16[64,512]{1,0:T(8,128)(2,1)S(1)} %add.27.refs_1_, bf16[512,4096]{1,0:T(8,128)(2,1)S(1)} %get-tuple-element.16.subspace_ref.refs_2_), custom_call_target="tpu_custom_call" | custom-call | tf_op jit(solution)/shard_map/pallas_call | solution.py:209
  (12 shorter events, 0.1 us)
Async XLA Ops:
  1.0 11.9 %collective-permute-start = (bf16[256,512]{1,0:T(8,128)(2,1)S(1)}, bf16[256,512]{1,0:T(8,128)(2,1)S(1)}, u32[]{:S(2)}, u32[]{:S(2)}) collective-permute-start(bf16[256,512]{1,0:T(8,128)(2,1)S(1)} %dynamic-slice_bitcast_fusion), channel_id=1, source_target_pairs={{4,0},{6,2},{8,4},{10,6},{12,8},{14,10},{0,12},{2,14},{5,1},{7,3},... | collective-permute-start | bytes 786440 | tf_op jit(solution)/shard_map/ppermute | solution.py:21
  6.1 13.7 %collective-permute-start.2 = (bf16[256,512]{1,0:T(8,128)(2,1)S(1)}, bf16[256,512]{1,0:T(8,128)(2,1)S(1)}, u32[]{:S(2)}, u32[]{:S(2)}) collective-permute-start(bf16[256,512]{1,0:T(8,128)(2,1)S(1)} %dynamic-slice_bitcast_fusion), channel_id=1, source_target_pairs={{2,0},{8,2},{6,4},{12,6},{10,8},{0,10},{14,12},{4,14},{3,1},{9,3},... | collective-permute-start | bytes 786440 | tf_op jit(solution)/shard_map/ppermute | solution.py:21
  12.8 9.6 %collective-permute-start.4 = (bf16[256,512]{1,0:T(8,128)(2,1)S(1)}, bf16[256,512]{1,0:T(8,128)(2,1)S(1)}, u32[]{:S(2)}, u32[]{:S(2)}) collective-permute-start(bf16[256,512]{1,0:T(8,128)(2,1)S(1)} %collective-permute-done.rest_0_), channel_id=1, source_target_pairs={{2,0},{0,2},{6,4},{4,6},{10,8},{8,10},{14,12},{12,14},{3,1},{1,3},... | collective-permute-start | bytes 786440 | tf_op jit(solution)/shard_map/ppermute | solution.py:21
  13.1 1.0 %copy-start = (bf16[1,512,512]{2,1,0:T(8,128)(2,1)S(1)}, bf16[1,512,512]{2,1,0:T(8,128)(2,1)}, u32[]{:S(2)}) copy-start(bf16[1,512,512]{2,1,0:T(8,128)(2,1)} %param.7) | copy-start | bytes 1572868
  14.2 1.0 %copy-start.1 = (bf16[64,4096]{1,0:T(8,128)(2,1)S(1)}, bf16[64,4096]{1,0:T(8,128)(2,1)}, u32[]{:S(2)}) copy-start(bf16[64,4096]{1,0:T(8,128)(2,1)} %residual_hbm.1) | copy-start | bytes 1572868
  15.2 0.7 %copy-start.2 = (s32[8]{0:T(128)S(1)}, s32[8]{0:T(128)}, u32[]{:S(2)}) copy-start(s32[8]{0:T(128)} %offset_ref.3) | copy-start | bytes 100
  15.9 0.7 %copy-start.3 = (s32[8]{0:T(128)S(1)}, s32[8]{0:T(128)}, u32[]{:S(2)}) copy-start(s32[8]{0:T(128)} %listed_ref.3) | copy-start | bytes 100
  19.8 2.7 %collective-permute-start.3 = (bf16[256,512]{1,0:T(8,128)(2,1)S(1)}, bf16[256,512]{1,0:T(8,128)(2,1)S(1)}, u32[]{:S(2)}, u32[]{:S(2)}) collective-permute-start(bf16[256,512]{1,0:T(8,128)(2,1)S(1)} %collective-permute-done.2.rest_2_), channel_id=1, source_target_pairs={{0,1},{1,0},{2,3},{3,2},{4,5},{5,4},{6,7},{7,6},{8,9},{9,8},{10,11... | collective-permute-start | bytes 786440 | tf_op jit(solution)/shard_map/ppermute | solution.py:25
  19.9 2.6 %collective-permute-start.1 = (bf16[256,512]{1,0:T(8,128)(2,1)S(1)}, bf16[256,512]{1,0:T(8,128)(2,1)S(1)}, u32[]{:S(2)}, u32[]{:S(2)}) collective-permute-start(bf16[256,512]{1,0:T(8,128)(2,1)S(1)} %collective-permute-done.rest_0_), channel_id=1, source_target_pairs={{0,1},{1,0},{2,3},{3,2},{4,5},{5,4},{6,7},{7,6},{8,9},{9,8},{10,11... | collective-permute-start | bytes 786440 | tf_op jit(solution)/shard_map/ppermute | solution.py:25
  22.5 1.5 %collective-permute-start.5 = (bf16[256,512]{1,0:T(8,128)(2,1)S(1)}, bf16[256,512]{1,0:T(8,128)(2,1)S(1)}, u32[]{:S(2)}, u32[]{:S(2)}) collective-permute-start(bf16[256,512]{1,0:T(8,128)(2,1)S(1)} %collective-permute-done.4.rest_4_), channel_id=1, source_target_pairs={{0,1},{1,0},{2,3},{3,2},{4,5},{5,4},{6,7},{7,6},{8,9},{9,8},{10,11... | collective-permute-start | bytes 786440 | tf_op jit(solution)/shard_map/ppermute | solution.py:25
  27.6 4.3 %collective-permute-start.6 = (bf16[64,512]{1,0:T(8,128)(2,1)S(1)}, bf16[64,512]{1,0:T(8,128)(2,1)S(1)}, u32[]{:S(2)}, u32[]{:S(2)}) collective-permute-start(bf16[64,512]{1,0:T(8,128)(2,1)S(1)} %convert_element_type.3), channel_id=1, source_target_pairs={{2,0},{0,2},{6,4},{4,6},{10,8},{8,10},{14,12},{12,14},{3,1},{1,3},... | collective-permute-start | bytes 196616 | tf_op jit(solution)/shard_map/ppermute | solution.py:21
  32.0 5.7 %collective-permute-start.7 = (bf16[64,512]{1,0:T(8,128)(2,1)S(1)}, bf16[64,512]{1,0:T(8,128)(2,1)S(1)}, u32[]{:S(2)}, u32[]{:S(2)}) collective-permute-start(bf16[64,512]{1,0:T(8,128)(2,1)S(1)} %convert_add_fusion), channel_id=1, source_target_pairs={{4,0},{6,2},{0,4},{2,6},{12,8},{14,10},{8,12},{10,14},{5,1},{7,3},... | collective-permute-start | bytes 196616 | tf_op jit(solution)/shard_map/ppermute | solution.py:21
  37.7 5.2 %collective-permute-start.8 = (bf16[64,512]{1,0:T(8,128)(2,1)S(1)}, bf16[64,512]{1,0:T(8,128)(2,1)S(1)}, u32[]{:S(2)}, u32[]{:S(2)}) collective-permute-start(bf16[64,512]{1,0:T(8,128)(2,1)S(1)} %add.23), channel_id=1, source_target_pairs={{8,0},{10,2},{12,4},{14,6},{0,8},{2,10},{4,12},{6,14},{9,1},{11,3}... | collective-permute-start | bytes 196616 | tf_op jit(solution)/shard_map/ppermute | solution.py:21
  45.3 4.3 %collective-permute-start.9 = (bf16[64,512]{1,0:T(8,128)(2,1)S(1)}, bf16[64,512]{1,0:T(8,128)(2,1)S(1)}, u32[]{:S(2)}, u32[]{:S(2)}) collective-permute-start(bf16[64,512]{1,0:T(8,128)(2,1)S(1)} %get-tuple-element.24), channel_id=1, source_target_pairs={{2,0},{0,2},{6,4},{4,6},{10,8},{8,10},{14,12},{12,14},{3,1},{1,3},... | collective-permute-start | bytes 196616 | tf_op jit(solution)/shard_map/ppermute | solution.py:21
  49.7 4.9 %collective-permute-start.10 = (bf16[64,512]{1,0:T(8,128)(2,1)S(1)}, bf16[64,512]{1,0:T(8,128)(2,1)S(1)}, u32[]{:S(2)}, u32[]{:S(2)}) collective-permute-start(bf16[64,512]{1,0:T(8,128)(2,1)S(1)} %add.25), channel_id=1, source_target_pairs={{4,0},{6,2},{0,4},{2,6},{12,8},{14,10},{8,12},{10,14},{5,1},{7,3},... | collective-permute-start | bytes 196616 | tf_op jit(solution)/shard_map/ppermute | solution.py:21
  54.6 5.2 %collective-permute-start.11 = (bf16[64,512]{1,0:T(8,128)(2,1)S(1)}, bf16[64,512]{1,0:T(8,128)(2,1)S(1)}, u32[]{:S(2)}, u32[]{:S(2)}) collective-permute-start(bf16[64,512]{1,0:T(8,128)(2,1)S(1)} %add.26), channel_id=1, source_target_pairs={{8,0},{10,2},{12,4},{14,6},{0,8},{2,10},{4,12},{6,14},{9,1},{11,3}... | collective-permute-start | bytes 196616 | tf_op jit(solution)/shard_map/ppermute | solution.py:21

commit v3 on v2

v3 whole, which is shorter than its diff:
```python
import functools

import jax
import jax.numpy as jnp
from jax import lax
from jax.experimental import pallas as pl
from jax.experimental.pallas import tpu as pltpu
from jax.sharding import PartitionSpec as P

F32 = jnp.float32
BF16 = jnp.bfloat16
VMEM = pl.BlockSpec(memory_space=pltpu.VMEM)
SMEM = pl.BlockSpec(memory_space=pltpu.SMEM)
HBM = pl.BlockSpec(memory_space=pltpu.HBM)
ACROSS = (((1,), (1,)), ((), ()))
AHEAD, MIXED, SWAPPED = range(3)


def permute(block, source):
    n = lax.axis_size("tr")
    return lax.ppermute(block, "tr", [(source(i) % n, i) for i in range(n)])


def permute_cores(block, source):
    n, cores = lax.axis_size("tr"), lax.axis_size("root")
    pairs = []
    for i in range(n):
        for core in range(cores):
            at, of = source(i, core)
            pairs.append((at % n * cores + of, i * cores + core))
    return lax.ppermute(block, ("tr", "root"), pairs)


def other_core(block):
    return lax.ppermute(block, "root", [(0, 1), (1, 0)])


PAD = 16


def diagonal(rows, half):
    row = lax.broadcasted_iota(jnp.int32, rows, 0) + half * rows[0]
    return row == lax.broadcasted_iota(jnp.int32, rows, 1)


def encode(message_ref, values, half):
    count = values.shape[0]
    rounded = values.astype(BF16)
    lost = jnp.where(diagonal(values.shape, half), values - rounded.astype(F32), 0.0)
    lost = jnp.sum(lost, axis=0, keepdims=True)
    message_ref[:count, :] = rounded
    message_ref[count:, :] = jnp.broadcast_to(lost, (PAD, values.shape[1])).astype(BF16)


def decode(message_ref, half):
    count = message_ref.shape[0] - PAD
    values = message_ref[:count, :].astype(F32)
    lost = message_ref[count : count + 1, :].astype(F32)
    return values + jnp.where(diagonal(values.shape, half), lost, 0.0)


def gram_kernel(subspace_hbm, subspace_ref, kept_ref, message_ref, gram_ref, sems):
    vectors, columns = subspace_hbm.shape
    core = lax.axis_index("root")
    block = vectors // 2
    part = block // 2
    pieces = sems.shape[0]
    width = columns // pieces
    copies = [
        pltpu.make_async_copy(
            subspace_hbm.at[:, chunk(b, width)], subspace_ref.at[:, chunk(b, width)], sems.at[b]
        )
        for b in range(pieces)
    ]
    for copy in copies:
        copy.start()
    for b in range(pieces):
        copies[b].wait()
        span = chunk(b, width)
        of_core = subspace_ref[pl.ds(pl.multiple_of(core * block, block), block), span]
        of_part = subspace_ref[pl.ds(pl.multiple_of(core * part, part), part), span]
        top, bottom = correlate(of_core, of_core), correlate(of_part, subspace_ref[block:, span])
        if b == 0:
            gram_ref[:block, :] = top
            gram_ref[block:, :] = bottom
        else:
            gram_ref[:block, :] += top
            gram_ref[block:, :] += bottom
    half = lax.axis_index("tr") % 2
    count = kept_ref.shape[0]
    kept_ref[...] = gram_ref[pl.ds(pl.multiple_of(half * count, count), count), :]
    given = gram_ref[pl.ds(pl.multiple_of((1 - half) * count, count), count), :]
    encode(message_ref, given, 1 - half)


def kept_kernel(kept_ref, got_ref, message_ref):
    half = lax.axis_index("tr") % 2
    encode(message_ref, kept_ref[...] + decode(got_ref, half), half)


def add_kernel(sent_ref, got_ref, message_ref):
    half = lax.axis_index("tr") % 2
    encode(message_ref, decode(sent_ref, half) + decode(got_ref, half), half)


def assemble_kernel(mine_ref, got_ref, mine_other_ref, got_other_ref, gram_ref, lost_ref, packed_ref):
    half = lax.axis_index("tr") % 2
    core = lax.axis_index("root")
    count = mine_ref.shape[0] - PAD
    block = mine_ref.shape[1]
    part = block // 2
    for owner, near_ref, far_ref in ((core, mine_ref, got_ref), (1 - core, mine_other_ref, got_other_ref)):
        packed_ref[pl.ds(pl.multiple_of(half * count, count), count), :] = near_ref[:count, :]
        packed_ref[pl.ds(pl.multiple_of((1 - half) * count, count), count), :] = far_ref[:count, :]
        at = pl.ds(pl.multiple_of(owner * block, block), block)
        gram_ref[at, at] = packed_ref[:block, :]
        gram_ref[pl.ds(pl.multiple_of(owner * part, part), part), block:] = packed_ref[block:, :]
        lost = near_ref[count : count + 8, :].astype(F32) + far_ref[count : count + 8, :].astype(F32)
        lost_ref[:, at] = lost


def correlate(block, basis):
    return lax.dot_general(block.astype(BF16), basis, ACROSS, preferred_element_type=F32)


def chunk(b, size):
    return pl.ds(b * size, size)


def offset_of(kind):
    odd = lax.axis_index("tr") % 2
    return {AHEAD: 2, MIXED: 1 + 2 * odd, SWAPPED: 3 - 2 * odd}[kind]


def local_kernel(offset_ref, listed_ref, residual_ref, subspace_ref, own_ref, precond_ref, corr_ref):
    size = own_ref.shape[0]
    corr_ref[...] = jnp.zeros_like(corr_ref)
    for b in range(residual_ref.shape[1] // size):
        columns = chunk(b, size)
        listed = listed_ref[b] > 0
        own = jnp.logical_and(listed, offset_ref[b] == 0)

        @pl.when(own)
        def _():
            precond_ref[:, columns] = jnp.dot(
                residual_ref[:, columns], own_ref[...], preferred_element_type=F32
            )

        @pl.when(jnp.logical_not(listed))
        def _():
            precond_ref[:, columns] = residual_ref[:, columns].astype(F32)

        @pl.when(jnp.logical_or(own, jnp.logical_not(listed)))
        def _():
            corr_ref[...] += correlate(precond_ref[:, columns], subspace_ref[:, columns])


def fetched_kernel(kinds, offset_ref, listed_ref, residual_ref, subspace_ref, *rest):
    halves, (_, corr_in, precond_ref, corr_ref) = rest[: 2 * len(kinds)], rest[2 * len(kinds) :]
    half = halves[0].shape[0]
    size = 2 * half
    mine = lax.axis_index("root") * half
    corr_ref[...] = corr_in[...]
    for b in range(residual_ref.shape[1] // size):
        columns = chunk(b, size)
        of_mine = pl.ds(pl.multiple_of(b * size + mine, half), half)
        of_other = pl.ds(pl.multiple_of(b * size + half - mine, half), half)
        for k, kind in enumerate(kinds):
            @pl.when(jnp.logical_and(listed_ref[b] > 0, offset_ref[b] == offset_of(kind)))
            def _():
                solved = jnp.dot(
                    residual_ref[:, of_mine], halves[2 * k][...], preferred_element_type=F32
                ) + jnp.dot(
                    residual_ref[:, of_other], halves[2 * k + 1][...], preferred_element_type=F32
                )
                precond_ref[:, columns] = solved
                corr_ref[...] += correlate(solved, subspace_ref[:, columns])


def last_kernel(size, precond_ref, corr_ref, got_ref, gram_ref, lost_ref, subspace_ref, out_hbm, out_ref, sems):
    corr = corr_ref[...].astype(F32) + got_ref[...].astype(F32)
    block = gram_ref.shape[0] // 2
    coef = corr.astype(BF16)
    left, right = coef[:, :block], coef[:, block:]
    off = gram_ref[:block, block:]
    again = jnp.concatenate(
        [
            jnp.dot(left, gram_ref[:block, :block], preferred_element_type=F32)
            + lax.dot_general(right, off, ACROSS, preferred_element_type=F32),
            jnp.dot(left, off, preferred_element_type=F32)
            + jnp.dot(right, gram_ref[block:, block:], preferred_element_type=F32),
        ],
        axis=1,
    )
    coef_2 = corr - again - coef.astype(F32) * lost_ref[0:1, :]
    total = coef.astype(F32) + coef_2
    lead = total.astype(BF16)
    trail = (total - lead.astype(F32)).astype(BF16)
    copies = []
    for b in range(precond_ref.shape[1] // size):
        columns = chunk(b, size)
        basis = subspace_ref[:, columns]
        out_ref[:, columns] = precond_ref[:, columns] - (
            jnp.dot(lead, basis, preferred_element_type=F32)
            + jnp.dot(trail, basis, preferred_element_type=F32)
        )
        copy = pltpu.make_async_copy(out_ref.at[:, columns], out_hbm.at[:, columns], sems.at[b])
        copy.start()
        copies.append(copy)
    for copy in copies:
        copy.wait()


PARAMS = pltpu.CompilerParams(vmem_limit_bytes=24 * 1024 * 1024)


def cost(flops, bytes_accessed):
    return pl.CostEstimate(flops=flops, bytes_accessed=bytes_accessed, transcendentals=0)


def per_device(residual, subspace, inverses, owner_offset, listed):
    roots, columns = residual.shape
    vectors = subspace.shape[0]
    own = inverses[0]
    size = own.shape[0]
    count = columns // size
    core = lax.axis_index("root").astype(jnp.int32)
    half = size // lax.axis_size("root")

    block = vectors // 2
    count_half = (block + block // 2) // 2

    def shape(*dims, dtype=BF16):
        return jax.ShapeDtypeStruct(dims, dtype)

    wide = shape(roots, columns, dtype=F32)
    small = shape(roots, vectors, dtype=F32)
    message = shape(count_half + PAD, block)

    def call(kernel, outs, *args, scratch=(), **more):
        return pl.pallas_call(
            kernel,
            out_shape=outs,
            in_specs=[VMEM] * len(args),
            out_specs=jax.tree.map(lambda _: VMEM, outs),
            scratch_shapes=list(scratch),
            compiler_params=PARAMS,
            **more,
        )(*args)

    my_half = lax.dynamic_slice_in_dim(own, core * half, half, 0)
    ahead = permute(my_half, lambda i: i + 2)
    mixed = permute_cores(my_half, lambda i, core: (i ^ 1, 1) if core else (i + 1 + 2 * (i % 2), 0))

    subspace, kept, given = pl.pallas_call(
        gram_kernel,
        out_shape=(shape(*subspace.shape), shape(count_half, block, dtype=F32), message),
        in_specs=[HBM],
        out_specs=(VMEM,) * 3,
        scratch_shapes=[pltpu.VMEM((2 * count_half, block), F32), pltpu.SemaphoreType.DMA((4,))],
        cost_estimate=cost(2 * vectors * vectors * columns, 16 * vectors * columns),
        compiler_params=pltpu.CompilerParams(vmem_limit_bytes=46 * 1024 * 1024),
    )(subspace)
    gram = call(kept_kernel, message, kept, permute(given, lambda i: i ^ 1))
    ahead, gram = lax.optimization_barrier((ahead, gram))
    swapped = permute(ahead, lambda i: i ^ 1)
    gram = call(add_kernel, message, gram, permute(gram, lambda i: i ^ 2))
    mixed = permute_cores(mixed, lambda i, core: (i + 4, 1) if core and i % 2 else (i, core))
    mixed, swapped, gram = lax.optimization_barrier((mixed, swapped, gram))
    step = 4
    while step < lax.axis_size("tr"):
        gram = call(add_kernel, message, gram, permute(gram, lambda i: i ^ step))
        step *= 2

    precond, corr = pl.pallas_call(
        local_kernel,
        out_shape=(wide, small),
        in_specs=[SMEM, SMEM, VMEM, VMEM, VMEM],
        out_specs=(VMEM,) * 2,
        compiler_params=PARAMS,
    )(owner_offset, listed, residual, subspace, own)

    def fetched(kinds, halves, precond, corr):
        return pl.pallas_call(
            functools.partial(fetched_kernel, kinds),
            out_shape=(wide, small),
            in_specs=[SMEM] * 2 + [VMEM] * (4 + len(halves)),
            out_specs=(VMEM, VMEM),
            input_output_aliases={4 + len(halves): 0},
            cost_estimate=cost(0, 0),
            compiler_params=PARAMS,
        )(owner_offset, listed, residual, subspace, *halves, precond, corr)

    mixed, corr = lax.optimization_barrier((mixed, corr))
    precond, corr = fetched(
        (AHEAD, MIXED, SWAPPED),
        (ahead, other_core(ahead), mixed, other_core(mixed), swapped, other_core(swapped)),
        precond, corr,
    )
    gram_far = permute(gram, lambda i: i ^ 1)
    gram, lost = call(
        assemble_kernel,
        (shape(vectors, vectors), shape(8, vectors, dtype=F32)),
        gram, gram_far, other_core(gram), other_core(gram_far),
        scratch=[pltpu.VMEM((2 * count_half, block), BF16)],
    )

    corr = corr.astype(BF16)
    step = 1
    while 2 * step < lax.axis_size("tr"):
        corr = corr + permute(corr, lambda i: i ^ step)
        step *= 2
    got = permute(corr, lambda i: i ^ step)

    def last(*refs):
        last_kernel(size, *refs)

    return pl.pallas_call(
        last,
        out_shape=wide,
        in_specs=[VMEM] * 6,
        out_specs=HBM,
        scratch_shapes=[pltpu.VMEM((roots, columns), F32), pltpu.SemaphoreType.DMA((count,))],
        compiler_params=PARAMS,
    )(precond, corr, got, gram, lost, subspace)


def solution(mesh):
    return jax.shard_map(
        per_device,
        mesh=mesh,
        in_specs=(
            P("root", ("grp", "tr")),
            P(None, ("grp", "tr")),
            P(("grp", "tr"), None, None),
            P(("grp", "tr")),
            P(("grp", "tr")),
        ),
        out_specs=P("root", ("grp", "tr")),
        check_vma=False,
    )
```

time: 61.7 us -> 47.9 us (0.78)
  waiting for transfers between devices: 26.6 us -> 14.8 us
  local copies, waits for them, and re-layouts: 4.36 us -> 0.99 us
  starting transfers between devices: 19.5 us -> 21.6 us
    ppermute x9, waiting for transfers between devices: 25 us -> 14.8 us  [permute(): return lax.ppermute(block, 'tr', [(source(i) % n, i) for i in range(n)])]
    unnamed x8, local copies, waits for them, and re-layouts: 3.39 us -> 0.03 us
    ppermute x3 -> x5, waiting for transfers between devices: 1.53 us -> 0.01 us  [other_core(): return lax.ppermute(block, 'root', [(0, 1), (1, 0)])]
    ppermute x0 -> x2, starting transfers between devices: none -> 1.04 us  [permute_cores(): return lax.ppermute(block, ('tr', 'root'), pairs)]
    ppermute x9, starting transfers between devices: 18.9 us -> 19.7 us  [permute(): return lax.ppermute(block, 'tr', [(source(i) % n, i) for i in range(n)])]
    pallas_call x3 -> x7, Pallas kernels: 7.24 us -> 7.32 us  [the longest x1 2.95 us: per_device(): pl.pallas_call(gram_kernel, out_shape=(shape(*subspace.shape), shape(coun...]
  transfers between devices with their start and end apart: 12 -> 16, of which waited for: 9 -> 8; matrix products, arithmetic and copies ran while one was open for 0% -> 0% of each run, Pallas kernels for 5% -> 16%
where the time goes in v3:
time: 47.9 us; the launch traced here: 48.1 us
  starting transfers between devices  21.6 us (45%)
  waiting for transfers between devices  14.8 us (31%)
  Pallas kernels  10.5 us (22%)
  local copies, waits for them, and re-layouts  0.99 us (2%)
    ppermute x9, starting transfers between devices, permute(): return lax.ppermute(block, 'tr', [(source(i) % n, i) for i in range(n)])  19.7 us
    ppermute x9, waiting for transfers between devices, permute(): return lax.ppermute(block, 'tr', [(source(i) % n, i) for i in range(n)])  14.8 us
    pallas_call x1, Pallas kernels, fetched(): pl.pallas_call(functools.partial(fetched_kernel, kinds), out_shape=(wide,...  3.16 us
    pallas_call x1, Pallas kernels, per_device(): pl.pallas_call(gram_kernel, out_shape=(shape(*subspace.shape), shape(coun...  2.95 us
    pallas_call x1, Pallas kernels, per_device(): pl.pallas_call(last, out_shape=wide, in_specs=[VMEM] * 6, out_specs=HBM,...  2.55 us
    pallas_call x1, Pallas kernels, per_device(): pl.pallas_call(local_kernel, out_shape=(wide, small), in_specs=[SMEM, SME...  1.43 us
    ppermute x2, starting transfers between devices, permute_cores(): return lax.ppermute(block, ('tr', 'root'), pairs)  1.04 us
    dynamic_slice x1, local copies, waits for them, and re-layouts, per_device(): my_half = lax.dynamic_slice_in_dim(own, core * half, half, 0)  0.97 us
  transfers between devices with their start and end apart: 16, of which 8 were waited for; matrix products, arithmetic and copies ran while one was open for 0% of the time, Pallas kernels for 16%

profile of v3, /device:TPU:0, one launch (start us, length us, event | category | flops | bytes accessed | tf_op | source)
XLA Modules:
  0.0 48.1 jit_solution(8922340306321556848)
XLA Ops:
  0.0 1.0 %dynamic-slice_bitcast_fusion = bf16[256,512]{1,0:T(8,128)(2,1)S(1)} fusion(bf16[1,512,512]{2,1,0:T(8,128)(2,1)} %param.7, s32[]{:T(128)S(6)} %select_n.3), kind=kLoop, calls=%fused_computation | loop fusion | bytes 524292 | tf_op jit(solution)/shard_map/dynamic_slice | solution.py:251
  1.0 0.0 copy-start.2
  1.0 5.1 %collective-permute-start = (bf16[256,512]{1,0:T(8,128)(2,1)S(1)}, bf16[256,512]{1,0:T(8,128)(2,1)S(1)}, u32[]{:S(2)}, u32[]{:S(2)}) collective-permute-start(bf16[256,512]{1,0:T(8,128)(2,1)S(1)} %dynamic-slice_bitcast_fusion), channel_id=1, source_target_pairs={{4,0},{6,2},{8,4},{10,6},{12,8},{14,10},{0,12},{2,14},{5,1},{7,3},... | collective-permute-start | bytes 786440 | tf_op jit(solution)/shard_map/ppermute | solution.py:21
  6.1 0.4 collective-permute-start.3
  6.5 3.0 %shard_map.55 = (bf16[512,4096]{1,0:T(8,128)(2,1)S(1)}, f32[192,256]{1,0:T(8,128)S(1)}, bf16[208,256]{1,0:T(8,128)(2,1)S(1)}) custom-call(bf16[512,4096]{1,0:T(8,128)(2,1)} %subspace_hbm.1), custom_call_target="tpu_custom_call" | custom-call | flops 2147483648 | bytes 33554432 | tf_op jit(solution)/shard_map/pallas_call | solution.py:255
  9.4 1.7 %collective-permute-start.1 = (bf16[208,256]{1,0:T(8,128)(2,1)S(1)}, bf16[208,256]{1,0:T(8,128)(2,1)S(1)}, u32[]{:S(2)}, u32[]{:S(2)}) collective-permute-start(bf16[208,256]{1,0:T(8,128)(2,1)S(1)} %get-tuple-element.23), channel_id=1, source_target_pairs={{2,0},{0,2},{6,4},{4,6},{10,8},{8,10},{14,12},{12,14},{3,1},{1,3},... | collective-permute-start | bytes 319496 | tf_op jit(solution)/shard_map/ppermute | solution.py:21
  11.2 5.0 %collective-permute-done.1.got_ref = bf16[208,256]{1,0:T(8,128)(2,1)S(1)} collective-permute-done((bf16[208,256]{1,0:T(8,128)(2,1)S(1)}, bf16[208,256]{1,0:T(8,128)(2,1)S(1)}, u32[]{:S(2)}, u32[]{:S(2)}) %collective-permute-start.1) | collective-permute-done | bytes 106528 | tf_op jit(solution)/shard_map/ppermute | solution.py:21
  16.2 0.1 shard_map.56.sent_ref
  16.3 0.7 %collective-permute-start.4 = (bf16[256,512]{1,0:T(8,128)(2,1)S(1)}, bf16[256,512]{1,0:T(8,128)(2,1)S(1)}, u32[]{:S(2)}, u32[]{:S(2)}) collective-permute-start(bf16[256,512]{1,0:T(8,128)(2,1)S(1)} %collective-permute-done.3), channel_id=1, source_target_pairs={{0,0},{1,1},{2,2},{11,3},{4,4},{5,5},{6,6},{15,7},{8,8},{9,9},{10,... | collective-permute-start | bytes 786440 | tf_op jit(solution)/shard_map/ppermute | solution.py:31
  17.0 2.4 %collective-permute-start.5 = (bf16[256,512]{1,0:T(8,128)(2,1)S(1)}, bf16[256,512]{1,0:T(8,128)(2,1)S(1)}, u32[]{:S(2)}, u32[]{:S(2)}) collective-permute-start(bf16[256,512]{1,0:T(8,128)(2,1)S(1)} %collective-permute-done.rest_0_), channel_id=1, source_target_pairs={{2,0},{0,2},{6,4},{4,6},{10,8},{8,10},{14,12},{12,14},{3,1},{1,3},... | collective-permute-start | bytes 786440 | tf_op jit(solution)/shard_map/ppermute | solution.py:21
  19.4 0.2 collective-permute-start.6
  19.6 1.4 %shard_map.58 = (f32[64,4096]{1,0:T(8,128)S(1)}, f32[64,512]{1,0:T(8,128)S(1)}) custom-call(s32[8]{0:T(128)S(1)} %copy-done.2, s32[8]{0:T(128)S(1)} %copy-done.3, bf16[64,4096]{1,0:T(8,128)(2,1)S(1)} %copy-done, bf16[512,4096]{1,0:T(8,128)(2,1)S(1)} %get-tuple-element.21.subspace_ref.refs_5_, bf16[512,512]{1,0:T(8,128)(2,1)S(1)} %bitcast.3), custom_call_target="tpu_custom_call" | custom-call | tf_op jit(solution)/shard_map/pallas_call | solution.py:275
  21.0 0.1 collective-permute-start.2
  21.1 3.0 %collective-permute-done.6.got_ref = bf16[208,256]{1,0:T(8,128)(2,1)S(1)} collective-permute-done((bf16[208,256]{1,0:T(8,128)(2,1)S(1)}, bf16[208,256]{1,0:T(8,128)(2,1)S(1)}, u32[]{:S(2)}, u32[]{:S(2)}) %collective-permute-start.6) | collective-permute-done | bytes 106528 | tf_op jit(solution)/shard_map/ppermute | solution.py:21
  24.1 0.1 shard_map.57.sent_ref
  24.2 0.3 collective-permute-done.5.rest_4_
  24.5 0.5 %collective-permute-start.8 = (bf16[256,512]{1,0:T(8,128)(2,1)S(1)}, bf16[256,512]{1,0:T(8,128)(2,1)S(1)}, u32[]{:S(2)}, u32[]{:S(2)}) collective-permute-start(bf16[256,512]{1,0:T(8,128)(2,1)S(1)} %collective-permute-done.5.rest_4_), channel_id=1, source_target_pairs={{0,1},{1,0},{2,3},{3,2},{4,5},{5,4},{6,7},{7,6},{8,9},{9,8},{10,11... | collective-permute-start | bytes 786440 | tf_op jit(solution)/shard_map/ppermute | solution.py:35
  25.0 2.8 %collective-permute-start.12 = (bf16[208,256]{1,0:T(8,128)(2,1)S(1)}, bf16[208,256]{1,0:T(8,128)(2,1)S(1)}, u32[]{:S(2)}, u32[]{:S(2)}) collective-permute-start(bf16[208,256]{1,0:T(8,128)(2,1)S(1)} %shard_map.57.sent_ref), channel_id=1, source_target_pairs={{8,0},{10,2},{12,4},{14,6},{0,8},{2,10},{4,12},{6,14},{9,1},{11,3}... | collective-permute-start | bytes 319496 | tf_op jit(solution)/shard_map/ppermute | solution.py:21
  27.9 3.2 %shard_map.59 = (f32[64,4096]{1,0:T(8,128)S(1)}, f32[64,512]{1,0:T(8,128)S(1)}) custom-call(s32[8]{0:T(128)S(1)} %copy-done.2, s32[8]{0:T(128)S(1)} %copy-done.3, bf16[64,4096]{1,0:T(8,128)(2,1)S(1)} %copy-done, bf16[512,4096]{1,0:T(8,128)(2,1)S(1)} %get-tuple-element.21.subspace_ref.refs_5_, ...), custom_call_target="tpu_custom_call", output_to_operand_aliasing={{0}: (10, {})} | custom-call | tf_op jit(solution)/shard_map/pallas_call | solution.py:284
  31.1 2.0 %collective-permute-start.9 = (bf16[64,512]{1,0:T(8,128)(2,1)S(1)}, bf16[64,512]{1,0:T(8,128)(2,1)S(1)}, u32[]{:S(2)}, u32[]{:S(2)}) collective-permute-start(bf16[64,512]{1,0:T(8,128)(2,1)S(1)} %convert_element_type.3), channel_id=1, source_target_pairs={{2,0},{0,2},{6,4},{4,6},{10,8},{8,10},{14,12},{12,14},{3,1},{1,3},... | collective-permute-start | bytes 196616 | tf_op jit(solution)/shard_map/ppermute | solution.py:21
  33.1 0.3 collective-permute-done.12.got_ref
  33.3 0.1 shard_map.60.mine_ref
  33.5 1.5 %collective-permute-start.13 = (bf16[208,256]{1,0:T(8,128)(2,1)S(1)}, bf16[208,256]{1,0:T(8,128)(2,1)S(1)}, u32[]{:S(2)}, u32[]{:S(2)}) collective-permute-start(bf16[208,256]{1,0:T(8,128)(2,1)S(1)} %shard_map.60.mine_ref), channel_id=1, source_target_pairs={{2,0},{0,2},{6,4},{4,6},{10,8},{8,10},{14,12},{12,14},{3,1},{1,3},... | collective-permute-start | bytes 319496 | tf_op jit(solution)/shard_map/ppermute | solution.py:21
  35.0 0.4 collective-permute-done.9
  35.4 2.6 %collective-permute-start.10 = (bf16[64,512]{1,0:T(8,128)(2,1)S(1)}, bf16[64,512]{1,0:T(8,128)(2,1)S(1)}, u32[]{:S(2)}, u32[]{:S(2)}) collective-permute-start(bf16[64,512]{1,0:T(8,128)(2,1)S(1)} %convert_add_fusion), channel_id=1, source_target_pairs={{4,0},{6,2},{0,4},{2,6},{12,8},{14,10},{8,12},{10,14},{5,1},{7,3},... | collective-permute-start | bytes 196616 | tf_op jit(solution)/shard_map/ppermute | solution.py:21
  38.0 0.2 collective-permute-done.13.got_ref
  38.2 0.3 collective-permute-start.15
  38.5 1.7 %collective-permute-done.10 = bf16[64,512]{1,0:T(8,128)(2,1)S(1)} collective-permute-done((bf16[64,512]{1,0:T(8,128)(2,1)S(1)}, bf16[64,512]{1,0:T(8,128)(2,1)S(1)}, u32[]{:S(2)}, u32[]{:S(2)}) %collective-permute-start.10) | collective-permute-done | bytes 65568 | tf_op jit(solution)/shard_map/ppermute | solution.py:21
  40.3 1.2 %collective-permute-start.11 = (bf16[64,512]{1,0:T(8,128)(2,1)S(1)}, bf16[64,512]{1,0:T(8,128)(2,1)S(1)}, u32[]{:S(2)}, u32[]{:S(2)}) collective-permute-start(bf16[64,512]{1,0:T(8,128)(2,1)S(1)} %add.11.refs_1_), channel_id=1, source_target_pairs={{8,0},{10,2},{12,4},{14,6},{0,8},{2,10},{4,12},{6,14},{9,1},{11,3}... | collective-permute-start | bytes 196616 | tf_op jit(solution)/shard_map/ppermute | solution.py:21
  41.5 0.1 shard_map.61
  41.6 3.9 %collective-permute-done.11.refs_2_ = bf16[64,512]{1,0:T(8,128)(2,1)S(1)} collective-permute-done((bf16[64,512]{1,0:T(8,128)(2,1)S(1)}, bf16[64,512]{1,0:T(8,128)(2,1)S(1)}, u32[]{:S(2)}, u32[]{:S(2)}) %collective-permute-start.11) | collective-permute-done | bytes 65568 | tf_op jit(solution)/shard_map/ppermute | solution.py:21
  45.5 2.5 %shard_map.62 = f32[64,4096]{1,0:T(8,128)} custom-call(f32[64,4096]{1,0:T(8,128)S(1)} %get-tuple-element.32.refs_0_, bf16[64,512]{1,0:T(8,128)(2,1)S(1)} %add.11.refs_1_, bf16[64,512]{1,0:T(8,128)(2,1)S(1)} %collective-permute-done.11.refs_2_, bf16[512,512]{1,0:T(8,128)(2,1)S(1)} %get-tuple-element.35.refs_3_, f32[8,512]{1,0:T(8,128)S(1)} %get-tuple-element.36.refs_4_, ...), custom_call_target="tpu_custom_call" | custom-call | tf_op jit(solution)/shard_map/pallas_call | solution.py:318
  (20 shorter events, 0.1 us)
Async XLA Ops:
  1.0 18.6 %copy-start = (bf16[64,4096]{1,0:T(8,128)(2,1)S(1)}, bf16[64,4096]{1,0:T(8,128)(2,1)}, u32[]{:S(2)}) copy-start(bf16[64,4096]{1,0:T(8,128)(2,1)} %residual_ref.3) | copy-start | bytes 1572868
  1.0 18.6 %copy-start.1 = (bf16[1,512,512]{2,1,0:T(8,128)(2,1)S(1)}, bf16[1,512,512]{2,1,0:T(8,128)(2,1)}, u32[]{:S(2)}) copy-start(bf16[1,512,512]{2,1,0:T(8,128)(2,1)} %param.7) | copy-start | bytes 1572868
  1.0 18.6 %copy-start.2 = (s32[8]{0:T(128)S(1)}, s32[8]{0:T(128)}, u32[]{:S(2)}) copy-start(s32[8]{0:T(128)} %offset_ref.3) | copy-start | bytes 100
  1.0 18.6 %copy-start.3 = (s32[8]{0:T(128)S(1)}, s32[8]{0:T(128)}, u32[]{:S(2)}) copy-start(s32[8]{0:T(128)} %listed_ref.3) | copy-start | bytes 100
  1.0 15.2 %collective-permute-start = (bf16[256,512]{1,0:T(8,128)(2,1)S(1)}, bf16[256,512]{1,0:T(8,128)(2,1)S(1)}, u32[]{:S(2)}, u32[]{:S(2)}) collective-permute-start(bf16[256,512]{1,0:T(8,128)(2,1)S(1)} %dynamic-slice_bitcast_fusion), channel_id=1, source_target_pairs={{4,0},{6,2},{8,4},{10,6},{12,8},{14,10},{0,12},{2,14},{5,1},{7,3},... | collective-permute-start | bytes 786440 | tf_op jit(solution)/shard_map/ppermute | solution.py:21
  6.1 10.2 %collective-permute-start.3 = (bf16[256,512]{1,0:T(8,128)(2,1)S(1)}, bf16[256,512]{1,0:T(8,128)(2,1)S(1)}, u32[]{:S(2)}, u32[]{:S(2)}) collective-permute-start(bf16[256,512]{1,0:T(8,128)(2,1)S(1)} %dynamic-slice_bitcast_fusion), channel_id=1, source_target_pairs={{2,0},{3,1},{8,2},{1,3},{6,4},{7,5},{12,6},{5,7},{10,8},{11,9},{0,... | collective-permute-start | bytes 786440 | tf_op jit(solution)/shard_map/ppermute | solution.py:31
  9.4 6.7 %collective-permute-start.1 = (bf16[208,256]{1,0:T(8,128)(2,1)S(1)}, bf16[208,256]{1,0:T(8,128)(2,1)S(1)}, u32[]{:S(2)}, u32[]{:S(2)}) collective-permute-start(bf16[208,256]{1,0:T(8,128)(2,1)S(1)} %get-tuple-element.23), channel_id=1, source_target_pairs={{2,0},{0,2},{6,4},{4,6},{10,8},{8,10},{14,12},{12,14},{3,1},{1,3},... | collective-permute-start | bytes 319496 | tf_op jit(solution)/shard_map/ppermute | solution.py:21
  16.3 7.9 %collective-permute-start.4 = (bf16[256,512]{1,0:T(8,128)(2,1)S(1)}, bf16[256,512]{1,0:T(8,128)(2,1)S(1)}, u32[]{:S(2)}, u32[]{:S(2)}) collective-permute-start(bf16[256,512]{1,0:T(8,128)(2,1)S(1)} %collective-permute-done.3), channel_id=1, source_target_pairs={{0,0},{1,1},{2,2},{11,3},{4,4},{5,5},{6,6},{15,7},{8,8},{9,9},{10,... | collective-permute-start | bytes 786440 | tf_op jit(solution)/shard_map/ppermute | solution.py:31
  17.0 7.5 %collective-permute-start.5 = (bf16[256,512]{1,0:T(8,128)(2,1)S(1)}, bf16[256,512]{1,0:T(8,128)(2,1)S(1)}, u32[]{:S(2)}, u32[]{:S(2)}) collective-permute-start(bf16[256,512]{1,0:T(8,128)(2,1)S(1)} %collective-permute-done.rest_0_), channel_id=1, source_target_pairs={{2,0},{0,2},{6,4},{4,6},{10,8},{8,10},{14,12},{12,14},{3,1},{1,3},... | collective-permute-start | bytes 786440 | tf_op jit(solution)/shard_map/ppermute | solution.py:21
  19.4 4.7 %collective-permute-start.6 = (bf16[208,256]{1,0:T(8,128)(2,1)S(1)}, bf16[208,256]{1,0:T(8,128)(2,1)S(1)}, u32[]{:S(2)}, u32[]{:S(2)}) collective-permute-start(bf16[208,256]{1,0:T(8,128)(2,1)S(1)} %shard_map.56.sent_ref), channel_id=1, source_target_pairs={{4,0},{6,2},{0,4},{2,6},{12,8},{14,10},{8,12},{10,14},{5,1},{7,3},... | collective-permute-start | bytes 319496 | tf_op jit(solution)/shard_map/ppermute | solution.py:21
  21.0 6.8 %collective-permute-start.2 = (bf16[256,512]{1,0:T(8,128)(2,1)S(1)}, bf16[256,512]{1,0:T(8,128)(2,1)S(1)}, u32[]{:S(2)}, u32[]{:S(2)}) collective-permute-start(bf16[256,512]{1,0:T(8,128)(2,1)S(1)} %collective-permute-done.rest_0_), channel_id=1, source_target_pairs={{0,1},{1,0},{2,3},{3,2},{4,5},{5,4},{6,7},{7,6},{8,9},{9,8},{10,11... | collective-permute-start | bytes 786440 | tf_op jit(solution)/shard_map/ppermute | solution.py:35
  24.5 3.3 %collective-permute-start.7 = (bf16[256,512]{1,0:T(8,128)(2,1)S(1)}, bf16[256,512]{1,0:T(8,128)(2,1)S(1)}, u32[]{:S(2)}, u32[]{:S(2)}) collective-permute-start(bf16[256,512]{1,0:T(8,128)(2,1)S(1)} %collective-permute-done.4.rest_2_), channel_id=1, source_target_pairs={{0,1},{1,0},{2,3},{3,2},{4,5},{5,4},{6,7},{7,6},{8,9},{9,8},{10,11... | collective-permute-start | bytes 786440 | tf_op jit(solution)/shard_map/ppermute | solution.py:35
  24.5 3.3 %collective-permute-start.8 = (bf16[256,512]{1,0:T(8,128)(2,1)S(1)}, bf16[256,512]{1,0:T(8,128)(2,1)S(1)}, u32[]{:S(2)}, u32[]{:S(2)}) collective-permute-start(bf16[256,512]{1,0:T(8,128)(2,1)S(1)} %collective-permute-done.5.rest_4_), channel_id=1, source_target_pairs={{0,1},{1,0},{2,3},{3,2},{4,5},{5,4},{6,7},{7,6},{8,9},{9,8},{10,11... | collective-permute-start | bytes 786440 | tf_op jit(solution)/shard_map/ppermute | solution.py:35
  25.0 8.3 %collective-permute-start.12 = (bf16[208,256]{1,0:T(8,128)(2,1)S(1)}, bf16[208,256]{1,0:T(8,128)(2,1)S(1)}, u32[]{:S(2)}, u32[]{:S(2)}) collective-permute-start(bf16[208,256]{1,0:T(8,128)(2,1)S(1)} %shard_map.57.sent_ref), channel_id=1, source_target_pairs={{8,0},{10,2},{12,4},{14,6},{0,8},{2,10},{4,12},{6,14},{9,1},{11,3}... | collective-permute-start | bytes 319496 | tf_op jit(solution)/shard_map/ppermute | solution.py:21
  31.1 4.4 %collective-permute-start.9 = (bf16[64,512]{1,0:T(8,128)(2,1)S(1)}, bf16[64,512]{1,0:T(8,128)(2,1)S(1)}, u32[]{:S(2)}, u32[]{:S(2)}) collective-permute-start(bf16[64,512]{1,0:T(8,128)(2,1)S(1)} %convert_element_type.3), channel_id=1, source_target_pairs={{2,0},{0,2},{6,4},{4,6},{10,8},{8,10},{14,12},{12,14},{3,1},{1,3},... | collective-permute-start | bytes 196616 | tf_op jit(solution)/shard_map/ppermute | solution.py:21
  33.5 4.8 %collective-permute-start.13 = (bf16[208,256]{1,0:T(8,128)(2,1)S(1)}, bf16[208,256]{1,0:T(8,128)(2,1)S(1)}, u32[]{:S(2)}, u32[]{:S(2)}) collective-permute-start(bf16[208,256]{1,0:T(8,128)(2,1)S(1)} %shard_map.60.mine_ref), channel_id=1, source_target_pairs={{2,0},{0,2},{6,4},{4,6},{10,8},{8,10},{14,12},{12,14},{3,1},{1,3},... | collective-permute-start | bytes 319496 | tf_op jit(solution)/shard_map/ppermute | solution.py:21
  35.4 4.8 %collective-permute-start.10 = (bf16[64,512]{1,0:T(8,128)(2,1)S(1)}, bf16[64,512]{1,0:T(8,128)(2,1)S(1)}, u32[]{:S(2)}, u32[]{:S(2)}) collective-permute-start(bf16[64,512]{1,0:T(8,128)(2,1)S(1)} %convert_add_fusion), channel_id=1, source_target_pairs={{4,0},{6,2},{0,4},{2,6},{12,8},{14,10},{8,12},{10,14},{5,1},{7,3},... | collective-permute-start | bytes 196616 | tf_op jit(solution)/shard_map/ppermute | solution.py:21
  38.0 3.5 %collective-permute-start.14 = (bf16[208,256]{1,0:T(8,128)(2,1)S(1)}, bf16[208,256]{1,0:T(8,128)(2,1)S(1)}, u32[]{:S(2)}, u32[]{:S(2)}) collective-permute-start(bf16[208,256]{1,0:T(8,128)(2,1)S(1)} %shard_map.60.mine_ref), channel_id=1, source_target_pairs={{0,1},{1,0},{2,3},{3,2},{4,5},{5,4},{6,7},{7,6},{8,9},{9,8},{10,11... | collective-permute-start | bytes 319496 | tf_op jit(solution)/shard_map/ppermute | solution.py:35
  38.2 3.3 %collective-permute-start.15 = (bf16[208,256]{1,0:T(8,128)(2,1)S(1)}, bf16[208,256]{1,0:T(8,128)(2,1)S(1)}, u32[]{:S(2)}, u32[]{:S(2)}) collective-permute-start(bf16[208,256]{1,0:T(8,128)(2,1)S(1)} %collective-permute-done.13.got_ref), channel_id=1, source_target_pairs={{0,1},{1,0},{2,3},{3,2},{4,5},{5,4},{6,7},{7,6},{8,9},{9,8},{10,11... | collective-permute-start | bytes 319496 | tf_op jit(solution)/shard_map/ppermute | solution.py:35
  40.3 5.2 %collective-permute-start.11 = (bf16[64,512]{1,0:T(8,128)(2,1)S(1)}, bf16[64,512]{1,0:T(8,128)(2,1)S(1)}, u32[]{:S(2)}, u32[]{:S(2)}) collective-permute-start(bf16[64,512]{1,0:T(8,128)(2,1)S(1)} %add.11.refs_1_), channel_id=1, source_target_pairs={{8,0},{10,2},{12,4},{14,6},{0,8},{2,10},{4,12},{6,14},{9,1},{11,3}... | collective-permute-start | bytes 196616 | tf_op jit(solution)/shard_map/ppermute | solution.py:21

commit v4 on v3

--- a/solution.py
+++ b/solution.py
@@ -195,15 +195,14 @@
     coef_2 = corr - again - coef.astype(F32) * lost_ref[0:1, :]
     total = coef.astype(F32) + coef_2
     lead = total.astype(BF16)
-    trail = (total - lead.astype(F32)).astype(BF16)
+    both = jnp.concatenate([lead, (total - lead.astype(F32)).astype(BF16)], axis=0)
+    roots = lead.shape[0]
     copies = []
     for b in range(precond_ref.shape[1] // size):
         columns = chunk(b, size)
         basis = subspace_ref[:, columns]
-        out_ref[:, columns] = precond_ref[:, columns] - (
-            jnp.dot(lead, basis, preferred_element_type=F32)
-            + jnp.dot(trail, basis, preferred_element_type=F32)
-        )
+        step = jnp.dot(both, basis, preferred_element_type=F32)
+        out_ref[:, columns] = precond_ref[:, columns] - (step[:roots, :] + step[roots:, :])
         copy = pltpu.make_async_copy(out_ref.at[:, columns], out_hbm.at[:, columns], sems.at[b])
         copy.start()
         copies.append(copy)
@@ -250,7 +249,7 @@
 
     my_half = lax.dynamic_slice_in_dim(own, core * half, half, 0)
     ahead = permute(my_half, lambda i: i + 2)
-    mixed = permute_cores(my_half, lambda i, core: (i ^ 1, 1) if core else (i + 1 + 2 * (i % 2), 0))
+    mixed = permute_cores(my_half, lambda i, core: (i ^ core, core))
 
     subspace, kept, given = pl.pallas_call(
         gram_kernel,
@@ -261,12 +260,16 @@
         cost_estimate=cost(2 * vectors * vectors * columns, 16 * vectors * columns),
         compiler_params=pltpu.CompilerParams(vmem_limit_bytes=46 * 1024 * 1024),
     )(subspace)
+    mixed, kept = lax.optimization_barrier((mixed, kept))
+    mixed = permute_cores(
+        mixed,
+        lambda i, core: ((i + 4, 1) if i % 2 else (i, 1)) if core else (i + 1 + 2 * (i % 2), 0),
+    )
     gram = call(kept_kernel, message, kept, permute(given, lambda i: i ^ 1))
     ahead, gram = lax.optimization_barrier((ahead, gram))
     swapped = permute(ahead, lambda i: i ^ 1)
     gram = call(add_kernel, message, gram, permute(gram, lambda i: i ^ 2))
-    mixed = permute_cores(mixed, lambda i, core: (i + 4, 1) if core and i % 2 else (i, core))
-    mixed, swapped, gram = lax.optimization_barrier((mixed, swapped, gram))
+    mixed, gram = lax.optimization_barrier((mixed, gram))
     step = 4
     while step < lax.axis_size("tr"):
         gram = call(add_kernel, message, gram, permute(gram, lambda i: i ^ step))

time: 47.9 us -> 46.7 us (0.975)
  starting transfers between devices: 21.6 us -> 17.9 us
  waiting for transfers between devices: 14.8 us -> 17.7 us
  Pallas kernels: 10.5 us -> 9.69 us
    ppermute x9, starting transfers between devices: 19.7 us -> 15.1 us  [permute(): return lax.ppermute(block, 'tr', [(source(i) % n, i) for i in range(n)])]
    ppermute x2, starting transfers between devices: 1.04 us -> 2.57 us  [permute_cores(): return lax.ppermute(block, ('tr', 'root'), pairs)]
    ppermute x9, waiting for transfers between devices: 14.8 us -> 16.3 us  [permute(): return lax.ppermute(block, 'tr', [(source(i) % n, i) for i in range(n)])]
    ppermute x5, waiting for transfers between devices: 0.01 us -> 1.38 us  [other_core(): return lax.ppermute(block, 'root', [(0, 1), (1, 0)])]
    pallas_call x1, Pallas kernels: 2.55 us -> 1.67 us  [per_device(): pl.pallas_call(last, out_shape=wide, in_specs=[VMEM] * 6, out_specs=HBM,...]
    ppermute x5, starting transfers between devices: 0.88 us -> 0.26 us  [other_core(): return lax.ppermute(block, 'root', [(0, 1), (1, 0)])]
    pallas_call x1, Pallas kernels: 1.43 us -> 1.91 us  [per_device(): pl.pallas_call(local_kernel, out_shape=(wide, small), in_specs=[SMEM, SME...]
  transfers between devices with their start and end apart: 16 -> 16, of which waited for: 8 -> 8; matrix products, arithmetic and copies ran while one was open for 0% -> 0% of each run, Pallas kernels for 16% -> 17%
where the time goes in v4:
time: 46.7 us; the launch traced here: 46.5 us
  starting transfers between devices  17.9 us (38%)
  waiting for transfers between devices  17.7 us (38%)
  Pallas kernels  9.69 us (21%)
  local copies, waits for them, and re-layouts  0.99 us (2%)
    ppermute x9, waiting for transfers between devices, permute(): return lax.ppermute(block, 'tr', [(source(i) % n, i) for i in range(n)])  16.3 us
    ppermute x9, starting transfers between devices, permute(): return lax.ppermute(block, 'tr', [(source(i) % n, i) for i in range(n)])  15.1 us
    pallas_call x1, Pallas kernels, per_device(): pl.pallas_call(gram_kernel, out_shape=(shape(*subspace.shape), shape(coun...  2.96 us
    pallas_call x1, Pallas kernels, fetched(): pl.pallas_call(functools.partial(fetched_kernel, kinds), out_shape=(wide,...  2.76 us
    ppermute x2, starting transfers between devices, permute_cores(): return lax.ppermute(block, ('tr', 'root'), pairs)  2.57 us
    pallas_call x1, Pallas kernels, per_device(): pl.pallas_call(local_kernel, out_shape=(wide, small), in_specs=[SMEM, SME...  1.91 us
    pallas_call x1, Pallas kernels, per_device(): pl.pallas_call(last, out_shape=wide, in_specs=[VMEM] * 6, out_specs=HBM,...  1.67 us
    ppermute x5, waiting for transfers between devices, other_core(): return lax.ppermute(block, 'root', [(0, 1), (1, 0)])  1.38 us
  transfers between devices with their start and end apart: 16, of which 8 were waited for; matrix products, arithmetic and copies ran while one was open for 0% of the time, Pallas kernels for 17%

profile of v4, /device:TPU:0, one launch (start us, length us, event | category | flops | bytes accessed | tf_op | source)
XLA Modules:
  0.0 46.5 jit_solution(14085309567335514340)
XLA Ops:
  0.0 1.0 %dynamic-slice_bitcast_fusion = bf16[256,512]{1,0:T(8,128)(2,1)S(1)} fusion(bf16[1,512,512]{2,1,0:T(8,128)(2,1)} %param.7, s32[]{:T(128)S(6)} %select_n.3), kind=kLoop, calls=%fused_computation | loop fusion | bytes 524292 | tf_op jit(solution)/shard_map/dynamic_slice | solution.py:250
  1.0 0.0 copy-start
  1.0 5.1 %collective-permute-start = (bf16[256,512]{1,0:T(8,128)(2,1)S(1)}, bf16[256,512]{1,0:T(8,128)(2,1)S(1)}, u32[]{:S(2)}, u32[]{:S(2)}) collective-permute-start(bf16[256,512]{1,0:T(8,128)(2,1)S(1)} %dynamic-slice_bitcast_fusion), channel_id=1, source_target_pairs={{4,0},{6,2},{8,4},{10,6},{12,8},{14,10},{0,12},{2,14},{5,1},{7,3},... | collective-permute-start | bytes 786440 | tf_op jit(solution)/shard_map/ppermute | solution.py:21
  6.1 0.7 %collective-permute-start.1 = (bf16[256,512]{1,0:T(8,128)(2,1)S(1)}, bf16[256,512]{1,0:T(8,128)(2,1)S(1)}, u32[]{:S(2)}, u32[]{:S(2)}) collective-permute-start(bf16[256,512]{1,0:T(8,128)(2,1)S(1)} %dynamic-slice_bitcast_fusion), channel_id=1, source_target_pairs={{0,0},{3,1},{2,2},{1,3},{4,4},{7,5},{6,6},{5,7},{8,8},{11,9},{10,1... | collective-permute-start | bytes 786440 | tf_op jit(solution)/shard_map/ppermute | solution.py:31
  6.8 3.0 %shard_map.55 = (bf16[512,4096]{1,0:T(8,128)(2,1)S(1)}, f32[192,256]{1,0:T(8,128)S(1)}, bf16[208,256]{1,0:T(8,128)(2,1)S(1)}) custom-call(bf16[512,4096]{1,0:T(8,128)(2,1)} %subspace_hbm.1), custom_call_target="tpu_custom_call" | custom-call | flops 2147483648 | bytes 33554432 | tf_op jit(solution)/shard_map/pallas_call | solution.py:254
  9.8 1.6 %collective-permute-start.2 = (bf16[208,256]{1,0:T(8,128)(2,1)S(1)}, bf16[208,256]{1,0:T(8,128)(2,1)S(1)}, u32[]{:S(2)}, u32[]{:S(2)}) collective-permute-start(bf16[208,256]{1,0:T(8,128)(2,1)S(1)} %get-tuple-element.25), channel_id=1, source_target_pairs={{2,0},{0,2},{6,4},{4,6},{10,8},{8,10},{14,12},{12,14},{3,1},{1,3},... | collective-permute-start | bytes 319496 | tf_op jit(solution)/shard_map/ppermute | solution.py:21
  11.3 1.9 %collective-permute-start.4 = (bf16[256,512]{1,0:T(8,128)(2,1)S(1)}, bf16[256,512]{1,0:T(8,128)(2,1)S(1)}, u32[]{:S(2)}, u32[]{:S(2)}) collective-permute-start(bf16[256,512]{1,0:T(8,128)(2,1)S(1)} %collective-permute-done.1), channel_id=1, source_target_pairs={{2,0},{1,1},{8,2},{11,3},{6,4},{5,5},{12,6},{15,7},{10,8},{9,9},{0... | collective-permute-start | bytes 786440 | tf_op jit(solution)/shard_map/ppermute | solution.py:31
  13.2 1.4 %collective-permute-done.2.got_ref = bf16[208,256]{1,0:T(8,128)(2,1)S(1)} collective-permute-done((bf16[208,256]{1,0:T(8,128)(2,1)S(1)}, bf16[208,256]{1,0:T(8,128)(2,1)S(1)}, u32[]{:S(2)}, u32[]{:S(2)}) %collective-permute-start.2) | collective-permute-done | bytes 106528 | tf_op jit(solution)/shard_map/ppermute | solution.py:21
  14.6 0.1 shard_map.56.sent_ref
  14.7 2.5 %collective-permute-start.7 = (bf16[256,512]{1,0:T(8,128)(2,1)S(1)}, bf16[256,512]{1,0:T(8,128)(2,1)S(1)}, u32[]{:S(2)}, u32[]{:S(2)}) collective-permute-start(bf16[256,512]{1,0:T(8,128)(2,1)S(1)} %collective-permute-done.rest_0_), channel_id=1, source_target_pairs={{2,0},{0,2},{6,4},{4,6},{10,8},{8,10},{14,12},{12,14},{3,1},{1,3},... | collective-permute-start | bytes 786440 | tf_op jit(solution)/shard_map/ppermute | solution.py:21
  17.3 1.9 %shard_map.58 = (f32[64,4096]{1,0:T(8,128)S(1)}, f32[64,512]{1,0:T(8,128)S(1)}) custom-call(s32[8]{0:T(128)S(1)} %copy-done.2, s32[8]{0:T(128)S(1)} %copy-done.3, bf16[64,4096]{1,0:T(8,128)(2,1)S(1)} %copy-done, bf16[512,4096]{1,0:T(8,128)(2,1)S(1)} %get-tuple-element.22.subspace_ref.refs_5_, bf16[512,512]{1,0:T(8,128)(2,1)S(1)} %bitcast.3), custom_call_target="tpu_custom_call" | custom-call | tf_op jit(solution)/shard_map/pallas_call | solution.py:278
  19.2 0.1 collective-permute-start.3
  19.3 3.8 %collective-permute-done.5.got_ref = bf16[208,256]{1,0:T(8,128)(2,1)S(1)} collective-permute-done((bf16[208,256]{1,0:T(8,128)(2,1)S(1)}, bf16[208,256]{1,0:T(8,128)(2,1)S(1)}, u32[]{:S(2)}, u32[]{:S(2)}) %collective-permute-start.5) | collective-permute-done | bytes 106528 | tf_op jit(solution)/shard_map/ppermute | solution.py:21
  23.1 0.1 shard_map.57.sent_ref
  23.2 0.1 collective-permute-start.6
  23.3 2.1 %collective-permute-done.7.rest_4_ = bf16[256,512]{1,0:T(8,128)(2,1)S(1)} collective-permute-done((bf16[256,512]{1,0:T(8,128)(2,1)S(1)}, bf16[256,512]{1,0:T(8,128)(2,1)S(1)}, u32[]{:S(2)}, u32[]{:S(2)}) %collective-permute-start.7) | collective-permute-done | bytes 262176 | tf_op jit(solution)/shard_map/ppermute | solution.py:21
  25.4 0.0 collective-permute-start.8
  25.5 0.1 collective-permute-start.12
  25.6 1.4 %collective-permute-done.8.rest_5_ = bf16[256,512]{1,0:T(8,128)(2,1)S(1)} collective-permute-done((bf16[256,512]{1,0:T(8,128)(2,1)S(1)}, bf16[256,512]{1,0:T(8,128)(2,1)S(1)}, u32[]{:S(2)}, u32[]{:S(2)}) %collective-permute-start.8) | collective-permute-done | bytes 262176 | tf_op jit(solution)/shard_map/ppermute | solution.py:35
  27.0 2.8 %shard_map.59 = (f32[64,4096]{1,0:T(8,128)S(1)}, f32[64,512]{1,0:T(8,128)S(1)}) custom-call(s32[8]{0:T(128)S(1)} %copy-done.2, s32[8]{0:T(128)S(1)} %copy-done.3, bf16[64,4096]{1,0:T(8,128)(2,1)S(1)} %copy-done, bf16[512,4096]{1,0:T(8,128)(2,1)S(1)} %get-tuple-element.22.subspace_ref.refs_5_, ...), custom_call_target="tpu_custom_call", output_to_operand_aliasing={{0}: (10, {})} | custom-call | tf_op jit(solution)/shard_map/pallas_call | solution.py:287
  29.7 2.9 %collective-permute-start.9 = (bf16[64,512]{1,0:T(8,128)(2,1)S(1)}, bf16[64,512]{1,0:T(8,128)(2,1)S(1)}, u32[]{:S(2)}, u32[]{:S(2)}) collective-permute-start(bf16[64,512]{1,0:T(8,128)(2,1)S(1)} %convert_element_type.3), channel_id=1, source_target_pairs={{2,0},{0,2},{6,4},{4,6},{10,8},{8,10},{14,12},{12,14},{3,1},{1,3},... | collective-permute-start | bytes 196616 | tf_op jit(solution)/shard_map/ppermute | solution.py:21
  32.7 0.1 shard_map.60.mine_ref
  32.8 1.6 %collective-permute-start.13 = (bf16[208,256]{1,0:T(8,128)(2,1)S(1)}, bf16[208,256]{1,0:T(8,128)(2,1)S(1)}, u32[]{:S(2)}, u32[]{:S(2)}) collective-permute-start(bf16[208,256]{1,0:T(8,128)(2,1)S(1)} %shard_map.60.mine_ref), channel_id=1, source_target_pairs={{2,0},{0,2},{6,4},{4,6},{10,8},{8,10},{14,12},{12,14},{3,1},{1,3},... | collective-permute-start | bytes 319496 | tf_op jit(solution)/shard_map/ppermute | solution.py:21
  34.4 0.7 %collective-permute-done.9 = bf16[64,512]{1,0:T(8,128)(2,1)S(1)} collective-permute-done((bf16[64,512]{1,0:T(8,128)(2,1)S(1)}, bf16[64,512]{1,0:T(8,128)(2,1)S(1)}, u32[]{:S(2)}, u32[]{:S(2)}) %collective-permute-start.9) | collective-permute-done | bytes 65568 | tf_op jit(solution)/shard_map/ppermute | solution.py:21
  35.1 0.1 collective-permute-start.10
  35.2 0.1 collective-permute-start.14
  35.2 2.4 %collective-permute-done.13.got_ref = bf16[208,256]{1,0:T(8,128)(2,1)S(1)} collective-permute-done((bf16[208,256]{1,0:T(8,128)(2,1)S(1)}, bf16[208,256]{1,0:T(8,128)(2,1)S(1)}, u32[]{:S(2)}, u32[]{:S(2)}) %collective-permute-start.13) | collective-permute-done | bytes 106528 | tf_op jit(solution)/shard_map/ppermute | solution.py:21
  37.6 1.8 %collective-permute-done.10 = bf16[64,512]{1,0:T(8,128)(2,1)S(1)} collective-permute-done((bf16[64,512]{1,0:T(8,128)(2,1)S(1)}, bf16[64,512]{1,0:T(8,128)(2,1)S(1)}, u32[]{:S(2)}, u32[]{:S(2)}) %collective-permute-start.10) | collective-permute-done | bytes 65568 | tf_op jit(solution)/shard_map/ppermute | solution.py:21
  39.4 1.2 %collective-permute-start.11 = (bf16[64,512]{1,0:T(8,128)(2,1)S(1)}, bf16[64,512]{1,0:T(8,128)(2,1)S(1)}, u32[]{:S(2)}, u32[]{:S(2)}) collective-permute-start(bf16[64,512]{1,0:T(8,128)(2,1)S(1)} %add.11.refs_1_), channel_id=1, source_target_pairs={{8,0},{10,2},{12,4},{14,6},{0,8},{2,10},{4,12},{6,14},{9,1},{11,3}... | collective-permute-start | bytes 196616 | tf_op jit(solution)/shard_map/ppermute | solution.py:21
  40.6 0.1 shard_map.61
  40.7 4.1 %collective-permute-done.11.refs_2_ = bf16[64,512]{1,0:T(8,128)(2,1)S(1)} collective-permute-done((bf16[64,512]{1,0:T(8,128)(2,1)S(1)}, bf16[64,512]{1,0:T(8,128)(2,1)S(1)}, u32[]{:S(2)}, u32[]{:S(2)}) %collective-permute-start.11) | collective-permute-done | bytes 65568 | tf_op jit(solution)/shard_map/ppermute | solution.py:21
  44.8 1.7 %shard_map.62 = f32[64,4096]{1,0:T(8,128)} custom-call(f32[64,4096]{1,0:T(8,128)S(1)} %get-tuple-element.34.refs_0_, bf16[64,512]{1,0:T(8,128)(2,1)S(1)} %add.11.refs_1_, bf16[64,512]{1,0:T(8,128)(2,1)S(1)} %collective-permute-done.11.refs_2_, bf16[512,512]{1,0:T(8,128)(2,1)S(1)} %get-tuple-element.37.refs_3_, f32[8,512]{1,0:T(8,128)S(1)} %get-tuple-element.38.refs_4_, ...), custom_call_target="tpu_custom_call" | custom-call | tf_op jit(solution)/shard_map/pallas_call | solution.py:321
  (20 shorter events, 0.1 us)
Async XLA Ops:
  1.0 16.3 %copy-start = (bf16[64,4096]{1,0:T(8,128)(2,1)S(1)}, bf16[64,4096]{1,0:T(8,128)(2,1)}, u32[]{:S(2)}) copy-start(bf16[64,4096]{1,0:T(8,128)(2,1)} %residual_ref.3) | copy-start | bytes 1572868
  1.0 16.3 %copy-start.1 = (bf16[1,512,512]{2,1,0:T(8,128)(2,1)S(1)}, bf16[1,512,512]{2,1,0:T(8,128)(2,1)}, u32[]{:S(2)}) copy-start(bf16[1,512,512]{2,1,0:T(8,128)(2,1)} %param.7) | copy-start | bytes 1572868
  1.0 16.3 %copy-start.2 = (s32[8]{0:T(128)S(1)}, s32[8]{0:T(128)}, u32[]{:S(2)}) copy-start(s32[8]{0:T(128)} %offset_ref.3) | copy-start | bytes 100
  1.0 16.3 %copy-start.3 = (s32[8]{0:T(128)S(1)}, s32[8]{0:T(128)}, u32[]{:S(2)}) copy-start(s32[8]{0:T(128)} %listed_ref.3) | copy-start | bytes 100
  1.0 13.7 %collective-permute-start = (bf16[256,512]{1,0:T(8,128)(2,1)S(1)}, bf16[256,512]{1,0:T(8,128)(2,1)S(1)}, u32[]{:S(2)}, u32[]{:S(2)}) collective-permute-start(bf16[256,512]{1,0:T(8,128)(2,1)S(1)} %dynamic-slice_bitcast_fusion), channel_id=1, source_target_pairs={{4,0},{6,2},{8,4},{10,6},{12,8},{14,10},{0,12},{2,14},{5,1},{7,3},... | collective-permute-start | bytes 786440 | tf_op jit(solution)/shard_map/ppermute | solution.py:21
  6.1 5.2 %collective-permute-start.1 = (bf16[256,512]{1,0:T(8,128)(2,1)S(1)}, bf16[256,512]{1,0:T(8,128)(2,1)S(1)}, u32[]{:S(2)}, u32[]{:S(2)}) collective-permute-start(bf16[256,512]{1,0:T(8,128)(2,1)S(1)} %dynamic-slice_bitcast_fusion), channel_id=1, source_target_pairs={{0,0},{3,1},{2,2},{1,3},{4,4},{7,5},{6,6},{5,7},{8,8},{11,9},{10,1... | collective-permute-start | bytes 786440 | tf_op jit(solution)/shard_map/ppermute | solution.py:31
  9.8 4.9 %collective-permute-start.2 = (bf16[208,256]{1,0:T(8,128)(2,1)S(1)}, bf16[208,256]{1,0:T(8,128)(2,1)S(1)}, u32[]{:S(2)}, u32[]{:S(2)}) collective-permute-start(bf16[208,256]{1,0:T(8,128)(2,1)S(1)} %get-tuple-element.25), channel_id=1, source_target_pairs={{2,0},{0,2},{6,4},{4,6},{10,8},{8,10},{14,12},{12,14},{3,1},{1,3},... | collective-permute-start | bytes 319496 | tf_op jit(solution)/shard_map/ppermute | solution.py:21
  11.3 11.9 %collective-permute-start.4 = (bf16[256,512]{1,0:T(8,128)(2,1)S(1)}, bf16[256,512]{1,0:T(8,128)(2,1)S(1)}, u32[]{:S(2)}, u32[]{:S(2)}) collective-permute-start(bf16[256,512]{1,0:T(8,128)(2,1)S(1)} %collective-permute-done.1), channel_id=1, source_target_pairs={{2,0},{1,1},{8,2},{11,3},{6,4},{5,5},{12,6},{15,7},{10,8},{9,9},{0... | collective-permute-start | bytes 786440 | tf_op jit(solution)/shard_map/ppermute | solution.py:31
  14.7 10.7 %collective-permute-start.7 = (bf16[256,512]{1,0:T(8,128)(2,1)S(1)}, bf16[256,512]{1,0:T(8,128)(2,1)S(1)}, u32[]{:S(2)}, u32[]{:S(2)}) collective-permute-start(bf16[256,512]{1,0:T(8,128)(2,1)S(1)} %collective-permute-done.rest_0_), channel_id=1, source_target_pairs={{2,0},{0,2},{6,4},{4,6},{10,8},{8,10},{14,12},{12,14},{3,1},{1,3},... | collective-permute-start | bytes 786440 | tf_op jit(solution)/shard_map/ppermute | solution.py:21
  17.3 5.8 %collective-permute-start.5 = (bf16[208,256]{1,0:T(8,128)(2,1)S(1)}, bf16[208,256]{1,0:T(8,128)(2,1)S(1)}, u32[]{:S(2)}, u32[]{:S(2)}) collective-permute-start(bf16[208,256]{1,0:T(8,128)(2,1)S(1)} %shard_map.56.sent_ref), channel_id=1, source_target_pairs={{4,0},{6,2},{0,4},{2,6},{12,8},{14,10},{8,12},{10,14},{5,1},{7,3},... | collective-permute-start | bytes 319496 | tf_op jit(solution)/shard_map/ppermute | solution.py:21
  19.2 6.4 %collective-permute-start.3 = (bf16[256,512]{1,0:T(8,128)(2,1)S(1)}, bf16[256,512]{1,0:T(8,128)(2,1)S(1)}, u32[]{:S(2)}, u32[]{:S(2)}) collective-permute-start(bf16[256,512]{1,0:T(8,128)(2,1)S(1)} %collective-permute-done.rest_0_), channel_id=1, source_target_pairs={{0,1},{1,0},{2,3},{3,2},{4,5},{5,4},{6,7},{7,6},{8,9},{9,8},{10,11... | collective-permute-start | bytes 786440 | tf_op jit(solution)/shard_map/ppermute | solution.py:35
  23.2 2.4 %collective-permute-start.6 = (bf16[256,512]{1,0:T(8,128)(2,1)S(1)}, bf16[256,512]{1,0:T(8,128)(2,1)S(1)}, u32[]{:S(2)}, u32[]{:S(2)}) collective-permute-start(bf16[256,512]{1,0:T(8,128)(2,1)S(1)} %collective-permute-done.4.rest_2_), channel_id=1, source_target_pairs={{0,1},{1,0},{2,3},{3,2},{4,5},{5,4},{6,7},{7,6},{8,9},{9,8},{10,11... | collective-permute-start | bytes 786440 | tf_op jit(solution)/shard_map/ppermute | solution.py:35
  25.4 1.5 %collective-permute-start.8 = (bf16[256,512]{1,0:T(8,128)(2,1)S(1)}, bf16[256,512]{1,0:T(8,128)(2,1)S(1)}, u32[]{:S(2)}, u32[]{:S(2)}) collective-permute-start(bf16[256,512]{1,0:T(8,128)(2,1)S(1)} %collective-permute-done.7.rest_4_), channel_id=1, source_target_pairs={{0,1},{1,0},{2,3},{3,2},{4,5},{5,4},{6,7},{7,6},{8,9},{9,8},{10,11... | collective-permute-start | bytes 786440 | tf_op jit(solution)/shard_map/ppermute | solution.py:35
  25.5 7.2 %collective-permute-start.12 = (bf16[208,256]{1,0:T(8,128)(2,1)S(1)}, bf16[208,256]{1,0:T(8,128)(2,1)S(1)}, u32[]{:S(2)}, u32[]{:S(2)}) collective-permute-start(bf16[208,256]{1,0:T(8,128)(2,1)S(1)} %shard_map.57.sent_ref), channel_id=1, source_target_pairs={{8,0},{10,2},{12,4},{14,6},{0,8},{2,10},{4,12},{6,14},{9,1},{11,3}... | collective-permute-start | bytes 319496 | tf_op jit(solution)/shard_map/ppermute | solution.py:21
  29.7 5.3 %collective-permute-start.9 = (bf16[64,512]{1,0:T(8,128)(2,1)S(1)}, bf16[64,512]{1,0:T(8,128)(2,1)S(1)}, u32[]{:S(2)}, u32[]{:S(2)}) collective-permute-start(bf16[64,512]{1,0:T(8,128)(2,1)S(1)} %convert_element_type.3), channel_id=1, source_target_pairs={{2,0},{0,2},{6,4},{4,6},{10,8},{8,10},{14,12},{12,14},{3,1},{1,3},... | collective-permute-start | bytes 196616 | tf_op jit(solution)/shard_map/ppermute | solution.py:21
  32.8 4.8 %collective-permute-start.13 = (bf16[208,256]{1,0:T(8,128)(2,1)S(1)}, bf16[208,256]{1,0:T(8,128)(2,1)S(1)}, u32[]{:S(2)}, u32[]{:S(2)}) collective-permute-start(bf16[208,256]{1,0:T(8,128)(2,1)S(1)} %shard_map.60.mine_ref), channel_id=1, source_target_pairs={{2,0},{0,2},{6,4},{4,6},{10,8},{8,10},{14,12},{12,14},{3,1},{1,3},... | collective-permute-start | bytes 319496 | tf_op jit(solution)/shard_map/ppermute | solution.py:21
  35.1 4.3 %collective-permute-start.10 = (bf16[64,512]{1,0:T(8,128)(2,1)S(1)}, bf16[64,512]{1,0:T(8,128)(2,1)S(1)}, u32[]{:S(2)}, u32[]{:S(2)}) collective-permute-start(bf16[64,512]{1,0:T(8,128)(2,1)S(1)} %convert_add_fusion), channel_id=1, source_target_pairs={{4,0},{6,2},{0,4},{2,6},{12,8},{14,10},{8,12},{10,14},{5,1},{7,3},... | collective-permute-start | bytes 196616 | tf_op jit(solution)/shard_map/ppermute | solution.py:21
  35.2 5.5 %collective-permute-start.14 = (bf16[208,256]{1,0:T(8,128)(2,1)S(1)}, bf16[208,256]{1,0:T(8,128)(2,1)S(1)}, u32[]{:S(2)}, u32[]{:S(2)}) collective-permute-start(bf16[208,256]{1,0:T(8,128)(2,1)S(1)} %shard_map.60.mine_ref), channel_id=1, source_target_pairs={{0,1},{1,0},{2,3},{3,2},{4,5},{5,4},{6,7},{7,6},{8,9},{9,8},{10,11... | collective-permute-start | bytes 319496 | tf_op jit(solution)/shard_map/ppermute | solution.py:35
  37.6 3.0 %collective-permute-start.15 = (bf16[208,256]{1,0:T(8,128)(2,1)S(1)}, bf16[208,256]{1,0:T(8,128)(2,1)S(1)}, u32[]{:S(2)}, u32[]{:S(2)}) collective-permute-start(bf16[208,256]{1,0:T(8,128)(2,1)S(1)} %collective-permute-done.13.got_ref), channel_id=1, source_target_pairs={{0,1},{1,0},{2,3},{3,2},{4,5},{5,4},{6,7},{7,6},{8,9},{9,8},{10,11... | collective-permute-start | bytes 319496 | tf_op jit(solution)/shard_map/ppermute | solution.py:35
  39.4 5.4 %collective-permute-start.11 = (bf16[64,512]{1,0:T(8,128)(2,1)S(1)}, bf16[64,512]{1,0:T(8,128)(2,1)S(1)}, u32[]{:S(2)}, u32[]{:S(2)}) collective-permute-start(bf16[64,512]{1,0:T(8,128)(2,1)S(1)} %add.11.refs_1_), channel_id=1, source_target_pairs={{8,0},{10,2},{12,4},{14,6},{0,8},{2,10},{4,12},{6,14},{9,1},{11,3}... | collective-permute-start | bytes 196616 | tf_op jit(solution)/shard_map/ppermute | solution.py:21

commit v5 on v4

--- a/solution.py
+++ b/solution.py
@@ -39,8 +39,14 @@
 
 
 def diagonal(rows, half):
+    quarter = rows[1] // 2
     row = lax.broadcasted_iota(jnp.int32, rows, 0) + half * rows[0]
-    return row == lax.broadcasted_iota(jnp.int32, rows, 1)
+    column = lax.broadcasted_iota(jnp.int32, rows, 1)
+    folded = row - 2 * quarter
+    at_end = jnp.logical_and(
+        folded >= 0, jnp.logical_or(column == folded, column == folded + quarter + quarter // 2)
+    )
+    return jnp.logical_or(at_end, jnp.logical_and(row < quarter, column == row))
 
 
 def encode(message_ref, values, half):
@@ -55,15 +61,14 @@
 def decode(message_ref, half):
     count = message_ref.shape[0] - PAD
     values = message_ref[:count, :].astype(F32)
-    lost = message_ref[count : count + 1, :].astype(F32)
+    lost = message_ref[count:, :].astype(F32)[0:1, :]
     return values + jnp.where(diagonal(values.shape, half), lost, 0.0)
 
 
 def gram_kernel(subspace_hbm, subspace_ref, kept_ref, message_ref, gram_ref, sems):
     vectors, columns = subspace_hbm.shape
     core = lax.axis_index("root")
-    block = vectors // 2
-    part = block // 2
+    quarter = vectors // 4
     pieces = sems.shape[0]
     width = columns // pieces
     copies = [
@@ -74,18 +79,27 @@
     ]
     for copy in copies:
         copy.start()
+    fold = quarter // 2
     for b in range(pieces):
         copies[b].wait()
         span = chunk(b, width)
-        of_core = subspace_ref[pl.ds(pl.multiple_of(core * block, block), block), span]
-        of_part = subspace_ref[pl.ds(pl.multiple_of(core * part, part), part), span]
-        top, bottom = correlate(of_core, of_core), correlate(of_part, subspace_ref[block:, span])
-        if b == 0:
-            gram_ref[:block, :] = top
-            gram_ref[block:, :] = bottom
-        else:
-            gram_ref[:block, :] += top
-            gram_ref[block:, :] += bottom
+
+        def rows(start, count):
+            return subspace_ref[pl.ds(pl.multiple_of(start, quarter), count), span]
+
+        near = correlate(rows(2 * core * quarter, 2 * quarter), rows(2 * core * quarter, 2 * quarter))
+        far = correlate(rows(core * quarter, quarter), subspace_ref[2 * quarter :, span])
+        parts = (
+            (0, quarter, slice(None), near[:quarter, :]),
+            (quarter, quarter, slice(None), far),
+            (2 * quarter, fold, slice(0, quarter), near[quarter : quarter + fold, quarter:]),
+            (2 * quarter, fold, slice(quarter, None), near[quarter + fold :, quarter:]),
+        )
+        for start, count, across, value in parts:
+            if b == 0:
+                gram_ref[start : start + count, across] = value
+            else:
+                gram_ref[start : start + count, across] += value
     half = lax.axis_index("tr") % 2
     count = kept_ref.shape[0]
     kept_ref[...] = gram_ref[pl.ds(pl.multiple_of(half * count, count), count), :]
@@ -107,16 +121,28 @@
     half = lax.axis_index("tr") % 2
     core = lax.axis_index("root")
     count = mine_ref.shape[0] - PAD
-    block = mine_ref.shape[1]
-    part = block // 2
+    quarter = mine_ref.shape[1] // 2
+    fold = quarter // 2
     for owner, near_ref, far_ref in ((core, mine_ref, got_ref), (1 - core, mine_other_ref, got_other_ref)):
-        packed_ref[pl.ds(pl.multiple_of(half * count, count), count), :] = near_ref[:count, :]
-        packed_ref[pl.ds(pl.multiple_of((1 - half) * count, count), count), :] = far_ref[:count, :]
-        at = pl.ds(pl.multiple_of(owner * block, block), block)
-        gram_ref[at, at] = packed_ref[:block, :]
-        gram_ref[pl.ds(pl.multiple_of(owner * part, part), part), block:] = packed_ref[block:, :]
-        lost = near_ref[count : count + 8, :].astype(F32) + far_ref[count : count + 8, :].astype(F32)
-        lost_ref[:, at] = lost
+        packed_ref[pl.ds(pl.multiple_of(half * count, count), count), :] = near_ref[:count, :].astype(F32)
+        packed_ref[pl.ds(pl.multiple_of((1 - half) * count, count), count), :] = far_ref[:count, :].astype(F32)
+        first = pl.ds(pl.multiple_of(2 * owner * quarter, quarter), quarter)
+        second = pl.ds(pl.multiple_of(2 * owner * quarter + quarter, quarter), quarter)
+        across = packed_ref[:quarter, quarter:]
+        gram_ref[first, first] = packed_ref[:quarter, :quarter].astype(BF16)
+        gram_ref[first, second] = across.astype(BF16)
+        gram_ref[second, first] = across.T.astype(BF16)
+        gram_ref[second, second] = jnp.concatenate(
+            [packed_ref[2 * quarter :, :quarter], packed_ref[2 * quarter :, quarter:]], axis=0
+        ).astype(BF16)
+        to = pl.ds(pl.multiple_of(owner * quarter, quarter), quarter)
+        outer = packed_ref[quarter : 2 * quarter, :]
+        gram_ref[to, 2 * quarter :] = outer.astype(BF16)
+        gram_ref[2 * quarter :, to] = outer.T.astype(BF16)
+        lost_ref[:, first] = jnp.where(half == 0, near_ref[count:, :quarter], far_ref[count:, :quarter]).astype(F32)
+        last = jnp.where(half == 0, far_ref[count:, :], near_ref[count:, :]).astype(F32)
+        lane = lax.broadcasted_iota(jnp.int32, (PAD, quarter), 1)
+        lost_ref[:, second] = jnp.where(lane < fold, last[:, :quarter], last[:, quarter:])
 
 
 def correlate(block, basis):
@@ -178,20 +204,9 @@
 
 
 def last_kernel(size, precond_ref, corr_ref, got_ref, gram_ref, lost_ref, subspace_ref, out_hbm, out_ref, sems):
-    corr = corr_ref[...].astype(F32) + got_ref[...].astype(F32)
-    block = gram_ref.shape[0] // 2
+    corr = corr_ref[...] + got_ref[...].astype(F32)
     coef = corr.astype(BF16)
-    left, right = coef[:, :block], coef[:, block:]
-    off = gram_ref[:block, block:]
-    again = jnp.concatenate(
-        [
-            jnp.dot(left, gram_ref[:block, :block], preferred_element_type=F32)
-            + lax.dot_general(right, off, ACROSS, preferred_element_type=F32),
-            jnp.dot(left, off, preferred_element_type=F32)
-            + jnp.dot(right, gram_ref[block:, block:], preferred_element_type=F32),
-        ],
-        axis=1,
-    )
+    again = jnp.dot(coef, gram_ref[...], preferred_element_type=F32)
     coef_2 = corr - again - coef.astype(F32) * lost_ref[0:1, :]
     total = coef.astype(F32) + coef_2
     lead = total.astype(BF16)
@@ -227,7 +242,7 @@
     half = size // lax.axis_size("root")
 
     block = vectors // 2
-    count_half = (block + block // 2) // 2
+    count_half = 5 * vectors // 16
 
     def shape(*dims, dtype=BF16):
         return jax.ShapeDtypeStruct(dims, dtype)
@@ -303,17 +318,16 @@
     gram_far = permute(gram, lambda i: i ^ 1)
     gram, lost = call(
         assemble_kernel,
-        (shape(vectors, vectors), shape(8, vectors, dtype=F32)),
+        (shape(vectors, vectors), shape(PAD, vectors, dtype=F32)),
         gram, gram_far, other_core(gram), other_core(gram_far),
-        scratch=[pltpu.VMEM((2 * count_half, block), BF16)],
-    )
-
-    corr = corr.astype(BF16)
+        scratch=[pltpu.VMEM((2 * count_half, block), F32)],
+    )
+
     step = 1
     while 2 * step < lax.axis_size("tr"):
-        corr = corr + permute(corr, lambda i: i ^ step)
+        corr = corr + permute(corr.astype(BF16), lambda i: i ^ step).astype(F32)
         step *= 2
-    got = permute(corr, lambda i: i ^ step)
+    got = permute(corr.astype(BF16), lambda i: i ^ step)
 
     def last(*refs):
         last_kernel(size, *refs)

time: 46.7 us -> 46.4 us (level)
  waiting for transfers between devices: 17.7 us -> 16.4 us
  starting transfers between devices: 17.9 us -> 18.4 us
    ppermute x9, waiting for transfers between devices: 16.3 us -> 15.1 us  [permute(): return lax.ppermute(block, 'tr', [(source(i) % n, i) for i in range(n)])]
    ppermute x9, starting transfers between devices: 15.1 us -> 15.5 us  [permute(): return lax.ppermute(block, 'tr', [(source(i) % n, i) for i in range(n)])]
    pallas_call x1, Pallas kernels: 1.91 us -> 2.39 us  [per_device(): pl.pallas_call(local_kernel, out_shape=(wide, small), in_specs=[SMEM, SME...]
  transfers between devices with their start and end apart: 16 -> 16, of which waited for: 8 -> 8; matrix products, arithmetic and copies ran while one was open for 0% -> 0% of each run, Pallas kernels for 17% -> 18%
where the time goes in v5:
time: 46.4 us; the launch traced here: 46 us
  starting transfers between devices  18.4 us (40%)
  waiting for transfers between devices  16.4 us (35%)
  Pallas kernels  9.98 us (22%)
  local copies, waits for them, and re-layouts  0.99 us (2%)
    ppermute x9, starting transfers between devices, permute(): return lax.ppermute(block, 'tr', [(source(i) % n, i) for i in range(n)])  15.5 us
    ppermute x9, waiting for transfers between devices, permute(): return lax.ppermute(block, 'tr', [(source(i) % n, i) for i in range(n)])  15.1 us
    pallas_call x1, Pallas kernels, per_device(): pl.pallas_call(gram_kernel, out_shape=(shape(*subspace.shape), shape(coun...  2.94 us
    ppermute x2, starting transfers between devices, permute_cores(): return lax.ppermute(block, ('tr', 'root'), pairs)  2.57 us
    pallas_call x1, Pallas kernels, per_device(): pl.pallas_call(local_kernel, out_shape=(wide, small), in_specs=[SMEM, SME...  2.39 us
    pallas_call x1, Pallas kernels, fetched(): pl.pallas_call(functools.partial(fetched_kernel, kinds), out_shape=(wide,...  2.36 us
    pallas_call x1, Pallas kernels, per_device(): pl.pallas_call(last, out_shape=wide, in_specs=[VMEM] * 6, out_specs=HBM,...  1.61 us
    ppermute x5, waiting for transfers between devices, other_core(): return lax.ppermute(block, 'root', [(0, 1), (1, 0)])  1.28 us
  transfers between devices with their start and end apart: 16, of which 8 were waited for; matrix products, arithmetic and copies ran while one was open for 0% of the time, Pallas kernels for 18%

profile of v5, /device:TPU:0, one launch (start us, length us, event | category | flops | bytes accessed | tf_op | source)
XLA Modules:
  0.0 46.0 jit_solution(15358171770674458054)
XLA Ops:
  0.0 1.0 %dynamic-slice_bitcast_fusion = bf16[256,512]{1,0:T(8,128)(2,1)S(1)} fusion(bf16[1,512,512]{2,1,0:T(8,128)(2,1)} %param.7, s32[]{:T(128)S(6)} %select_n.3), kind=kLoop, calls=%fused_computation | loop fusion | bytes 524292 | tf_op jit(solution)/shard_map/dynamic_slice | solution.py:265
  1.0 0.0 copy-start
  1.0 5.1 %collective-permute-start = (bf16[256,512]{1,0:T(8,128)(2,1)S(1)}, bf16[256,512]{1,0:T(8,128)(2,1)S(1)}, u32[]{:S(2)}, u32[]{:S(2)}) collective-permute-start(bf16[256,512]{1,0:T(8,128)(2,1)S(1)} %dynamic-slice_bitcast_fusion), channel_id=1, source_target_pairs={{4,0},{6,2},{8,4},{10,6},{12,8},{14,10},{0,12},{2,14},{5,1},{7,3},... | collective-permute-start | bytes 786440 | tf_op jit(solution)/shard_map/ppermute | solution.py:21
  6.1 0.7 %collective-permute-start.1 = (bf16[256,512]{1,0:T(8,128)(2,1)S(1)}, bf16[256,512]{1,0:T(8,128)(2,1)S(1)}, u32[]{:S(2)}, u32[]{:S(2)}) collective-permute-start(bf16[256,512]{1,0:T(8,128)(2,1)S(1)} %dynamic-slice_bitcast_fusion), channel_id=1, source_target_pairs={{0,0},{3,1},{2,2},{1,3},{4,4},{7,5},{6,6},{5,7},{8,8},{11,9},{10,1... | collective-permute-start | bytes 786440 | tf_op jit(solution)/shard_map/ppermute | solution.py:31
  6.8 2.9 %shard_map.55 = (bf16[512,4096]{1,0:T(8,128)(2,1)S(1)}, f32[160,256]{1,0:T(8,128)S(1)}, bf16[176,256]{1,0:T(8,128)(2,1)S(1)}) custom-call(bf16[512,4096]{1,0:T(8,128)(2,1)} %subspace_hbm.1), custom_call_target="tpu_custom_call" | custom-call | flops 2147483648 | bytes 33554432 | tf_op jit(solution)/shard_map/pallas_call | solution.py:269
  9.7 1.6 %collective-permute-start.2 = (bf16[176,256]{1,0:T(8,128)(2,1)S(1)}, bf16[176,256]{1,0:T(8,128)(2,1)S(1)}, u32[]{:S(2)}, u32[]{:S(2)}) collective-permute-start(bf16[176,256]{1,0:T(8,128)(2,1)S(1)} %get-tuple-element.25), channel_id=1, source_target_pairs={{2,0},{0,2},{6,4},{4,6},{10,8},{8,10},{14,12},{12,14},{3,1},{1,3},... | collective-permute-start | bytes 270344 | tf_op jit(solution)/shard_map/ppermute | solution.py:21
  11.3 1.9 %collective-permute-start.4 = (bf16[256,512]{1,0:T(8,128)(2,1)S(1)}, bf16[256,512]{1,0:T(8,128)(2,1)S(1)}, u32[]{:S(2)}, u32[]{:S(2)}) collective-permute-start(bf16[256,512]{1,0:T(8,128)(2,1)S(1)} %collective-permute-done.1), channel_id=1, source_target_pairs={{2,0},{1,1},{8,2},{11,3},{6,4},{5,5},{12,6},{15,7},{10,8},{9,9},{0... | collective-permute-start | bytes 786440 | tf_op jit(solution)/shard_map/ppermute | solution.py:31
  13.2 1.1 %collective-permute-done.2.got_ref = bf16[176,256]{1,0:T(8,128)(2,1)S(1)} collective-permute-done((bf16[176,256]{1,0:T(8,128)(2,1)S(1)}, bf16[176,256]{1,0:T(8,128)(2,1)S(1)}, u32[]{:S(2)}, u32[]{:S(2)}) %collective-permute-start.2) | collective-permute-done | bytes 90144 | tf_op jit(solution)/shard_map/ppermute | solution.py:21
  14.3 0.1 shard_map.56.sent_ref
  14.5 2.5 %collective-permute-start.7 = (bf16[256,512]{1,0:T(8,128)(2,1)S(1)}, bf16[256,512]{1,0:T(8,128)(2,1)S(1)}, u32[]{:S(2)}, u32[]{:S(2)}) collective-permute-start(bf16[256,512]{1,0:T(8,128)(2,1)S(1)} %collective-permute-done.rest_0_), channel_id=1, source_target_pairs={{2,0},{0,2},{6,4},{4,6},{10,8},{8,10},{14,12},{12,14},{3,1},{1,3},... | collective-permute-start | bytes 786440 | tf_op jit(solution)/shard_map/ppermute | solution.py:21
  17.0 2.4 %shard_map.58 = (f32[64,4096]{1,0:T(8,128)S(1)}, f32[64,512]{1,0:T(8,128)S(1)}) custom-call(s32[8]{0:T(128)S(1)} %copy-done.2, s32[8]{0:T(128)S(1)} %copy-done.3, bf16[64,4096]{1,0:T(8,128)(2,1)S(1)} %copy-done, bf16[512,4096]{1,0:T(8,128)(2,1)S(1)} %get-tuple-element.22.subspace_ref.refs_5_, bf16[512,512]{1,0:T(8,128)(2,1)S(1)} %bitcast.3), custom_call_target="tpu_custom_call" | custom-call | tf_op jit(solution)/shard_map/pallas_call | solution.py:293
  19.4 0.1 collective-permute-start.3
  19.5 3.3 %collective-permute-done.5.got_ref = bf16[176,256]{1,0:T(8,128)(2,1)S(1)} collective-permute-done((bf16[176,256]{1,0:T(8,128)(2,1)S(1)}, bf16[176,256]{1,0:T(8,128)(2,1)S(1)}, u32[]{:S(2)}, u32[]{:S(2)}) %collective-permute-start.5) | collective-permute-done | bytes 90144 | tf_op jit(solution)/shard_map/ppermute | solution.py:21
  22.7 0.1 shard_map.57.sent_ref
  22.9 0.1 collective-permute-start.6
  23.0 2.4 %collective-permute-done.7.rest_4_ = bf16[256,512]{1,0:T(8,128)(2,1)S(1)} collective-permute-done((bf16[256,512]{1,0:T(8,128)(2,1)S(1)}, bf16[256,512]{1,0:T(8,128)(2,1)S(1)}, u32[]{:S(2)}, u32[]{:S(2)}) %collective-permute-start.7) | collective-permute-done | bytes 262176 | tf_op jit(solution)/shard_map/ppermute | solution.py:21
  25.4 0.0 collective-permute-start.8
  25.4 0.2 collective-permute-start.12
  25.7 1.3 %collective-permute-done.8.rest_5_ = bf16[256,512]{1,0:T(8,128)(2,1)S(1)} collective-permute-done((bf16[256,512]{1,0:T(8,128)(2,1)S(1)}, bf16[256,512]{1,0:T(8,128)(2,1)S(1)}, u32[]{:S(2)}, u32[]{:S(2)}) %collective-permute-start.8) | collective-permute-done | bytes 262176 | tf_op jit(solution)/shard_map/ppermute | solution.py:35
  26.9 2.4 %shard_map.59 = (f32[64,4096]{1,0:T(8,128)S(1)}, f32[64,512]{1,0:T(8,128)S(1)}) custom-call(s32[8]{0:T(128)S(1)} %copy-done.2, s32[8]{0:T(128)S(1)} %copy-done.3, bf16[64,4096]{1,0:T(8,128)(2,1)S(1)} %copy-done, bf16[512,4096]{1,0:T(8,128)(2,1)S(1)} %get-tuple-element.22.subspace_ref.refs_5_, ...), custom_call_target="tpu_custom_call", output_to_operand_aliasing={{0}: (10, {})} | custom-call | tf_op jit(solution)/shard_map/pallas_call | solution.py:302
  29.3 2.9 %collective-permute-start.9 = (bf16[64,512]{1,0:T(8,128)(2,1)S(1)}, bf16[64,512]{1,0:T(8,128)(2,1)S(1)}, u32[]{:S(2)}, u32[]{:S(2)}) collective-permute-start(bf16[64,512]{1,0:T(8,128)(2,1)S(1)} %convert_element_type.15), channel_id=1, source_target_pairs={{2,0},{0,2},{6,4},{4,6},{10,8},{8,10},{14,12},{12,14},{3,1},{1,3},... | collective-permute-start | bytes 196616 | tf_op jit(solution)/shard_map/ppermute | solution.py:21
  32.3 0.1 shard_map.60.mine_ref
  32.4 1.6 %collective-permute-start.13 = (bf16[176,256]{1,0:T(8,128)(2,1)S(1)}, bf16[176,256]{1,0:T(8,128)(2,1)S(1)}, u32[]{:S(2)}, u32[]{:S(2)}) collective-permute-start(bf16[176,256]{1,0:T(8,128)(2,1)S(1)} %shard_map.60.mine_ref), channel_id=1, source_target_pairs={{2,0},{0,2},{6,4},{4,6},{10,8},{8,10},{14,12},{12,14},{3,1},{1,3},... | collective-permute-start | bytes 270344 | tf_op jit(solution)/shard_map/ppermute | solution.py:21
  34.0 0.6 %collective-permute-done.9 = bf16[64,512]{1,0:T(8,128)(2,1)S(1)} collective-permute-done((bf16[64,512]{1,0:T(8,128)(2,1)S(1)}, bf16[64,512]{1,0:T(8,128)(2,1)S(1)}, u32[]{:S(2)}, u32[]{:S(2)}) %collective-permute-start.9) | collective-permute-done | bytes 65568 | tf_op jit(solution)/shard_map/ppermute | solution.py:21
  34.7 0.1 collective-permute-start.10
  34.7 0.1 collective-permute-start.14
  34.8 2.2 %collective-permute-done.13.got_ref = bf16[176,256]{1,0:T(8,128)(2,1)S(1)} collective-permute-done((bf16[176,256]{1,0:T(8,128)(2,1)S(1)}, bf16[176,256]{1,0:T(8,128)(2,1)S(1)}, u32[]{:S(2)}, u32[]{:S(2)}) %collective-permute-start.13) | collective-permute-done | bytes 90144 | tf_op jit(solution)/shard_map/ppermute | solution.py:21
  37.0 2.0 %collective-permute-done.10 = bf16[64,512]{1,0:T(8,128)(2,1)S(1)} collective-permute-done((bf16[64,512]{1,0:T(8,128)(2,1)S(1)}, bf16[64,512]{1,0:T(8,128)(2,1)S(1)}, u32[]{:S(2)}, u32[]{:S(2)}) %collective-permute-start.10) | collective-permute-done | bytes 65568 | tf_op jit(solution)/shard_map/ppermute | solution.py:21
  39.0 1.6 %collective-permute-start.11 = (bf16[64,512]{1,0:T(8,128)(2,1)S(1)}, bf16[64,512]{1,0:T(8,128)(2,1)S(1)}, u32[]{:S(2)}, u32[]{:S(2)}) collective-permute-start(bf16[64,512]{1,0:T(8,128)(2,1)S(1)} %get-tuple-element.39), channel_id=1, source_target_pairs={{8,0},{10,2},{12,4},{14,6},{0,8},{2,10},{4,12},{6,14},{9,1},{11,3}... | collective-permute-start | bytes 196616 | tf_op jit(solution)/shard_map/ppermute | solution.py:21
  40.6 0.3 shard_map.61
  40.9 3.5 %collective-permute-done.11.refs_2_ = bf16[64,512]{1,0:T(8,128)(2,1)S(1)} collective-permute-done((bf16[64,512]{1,0:T(8,128)(2,1)S(1)}, bf16[64,512]{1,0:T(8,128)(2,1)S(1)}, u32[]{:S(2)}, u32[]{:S(2)}) %collective-permute-start.11) | collective-permute-done | bytes 65568 | tf_op jit(solution)/shard_map/ppermute | solution.py:21
  44.4 1.6 %shard_map.62 = f32[64,4096]{1,0:T(8,128)} custom-call(f32[64,4096]{1,0:T(8,128)S(1)} %get-tuple-element.34.refs_0_, f32[64,512]{1,0:T(8,128)S(1)} %get-tuple-element.40.refs_1_, bf16[64,512]{1,0:T(8,128)(2,1)S(1)} %collective-permute-done.11.refs_2_, bf16[512,512]{1,0:T(8,128)(2,1)S(1)} %get-tuple-element.37.refs_3_, ...), custom_call_target="tpu_custom_call" | custom-call | tf_op jit(solution)/shard_map/pallas_call | solution.py:335
  (20 shorter events, 0.1 us)
Async XLA Ops:
  1.0 16.0 %copy-start = (bf16[64,4096]{1,0:T(8,128)(2,1)S(1)}, bf16[64,4096]{1,0:T(8,128)(2,1)}, u32[]{:S(2)}) copy-start(bf16[64,4096]{1,0:T(8,128)(2,1)} %residual_ref.3) | copy-start | bytes 1572868
  1.0 16.0 %copy-start.1 = (bf16[1,512,512]{2,1,0:T(8,128)(2,1)S(1)}, bf16[1,512,512]{2,1,0:T(8,128)(2,1)}, u32[]{:S(2)}) copy-start(bf16[1,512,512]{2,1,0:T(8,128)(2,1)} %param.7) | copy-start | bytes 1572868
  1.0 16.0 %copy-start.2 = (s32[8]{0:T(128)S(1)}, s32[8]{0:T(128)}, u32[]{:S(2)}) copy-start(s32[8]{0:T(128)} %offset_ref.3) | copy-start | bytes 100
  1.0 16.0 %copy-start.3 = (s32[8]{0:T(128)S(1)}, s32[8]{0:T(128)}, u32[]{:S(2)}) copy-start(s32[8]{0:T(128)} %listed_ref.3) | copy-start | bytes 100
  1.0 13.5 %collective-permute-start = (bf16[256,512]{1,0:T(8,128)(2,1)S(1)}, bf16[256,512]{1,0:T(8,128)(2,1)S(1)}, u32[]{:S(2)}, u32[]{:S(2)}) collective-permute-start(bf16[256,512]{1,0:T(8,128)(2,1)S(1)} %dynamic-slice_bitcast_fusion), channel_id=1, source_target_pairs={{4,0},{6,2},{8,4},{10,6},{12,8},{14,10},{0,12},{2,14},{5,1},{7,3},... | collective-permute-start | bytes 786440 | tf_op jit(solution)/shard_map/ppermute | solution.py:21
  6.1 5.2 %collective-permute-start.1 = (bf16[256,512]{1,0:T(8,128)(2,1)S(1)}, bf16[256,512]{1,0:T(8,128)(2,1)S(1)}, u32[]{:S(2)}, u32[]{:S(2)}) collective-permute-start(bf16[256,512]{1,0:T(8,128)(2,1)S(1)} %dynamic-slice_bitcast_fusion), channel_id=1, source_target_pairs={{0,0},{3,1},{2,2},{1,3},{4,4},{7,5},{6,6},{5,7},{8,8},{11,9},{10,1... | collective-permute-start | bytes 786440 | tf_op jit(solution)/shard_map/ppermute | solution.py:31
  9.7 4.6 %collective-permute-start.2 = (bf16[176,256]{1,0:T(8,128)(2,1)S(1)}, bf16[176,256]{1,0:T(8,128)(2,1)S(1)}, u32[]{:S(2)}, u32[]{:S(2)}) collective-permute-start(bf16[176,256]{1,0:T(8,128)(2,1)S(1)} %get-tuple-element.25), channel_id=1, source_target_pairs={{2,0},{0,2},{6,4},{4,6},{10,8},{8,10},{14,12},{12,14},{3,1},{1,3},... | collective-permute-start | bytes 270344 | tf_op jit(solution)/shard_map/ppermute | solution.py:21
  11.3 11.6 %collective-permute-start.4 = (bf16[256,512]{1,0:T(8,128)(2,1)S(1)}, bf16[256,512]{1,0:T(8,128)(2,1)S(1)}, u32[]{:S(2)}, u32[]{:S(2)}) collective-permute-start(bf16[256,512]{1,0:T(8,128)(2,1)S(1)} %collective-permute-done.1), channel_id=1, source_target_pairs={{2,0},{1,1},{8,2},{11,3},{6,4},{5,5},{12,6},{15,7},{10,8},{9,9},{0... | collective-permute-start | bytes 786440 | tf_op jit(solution)/shard_map/ppermute | solution.py:31
  14.5 10.9 %collective-permute-start.7 = (bf16[256,512]{1,0:T(8,128)(2,1)S(1)}, bf16[256,512]{1,0:T(8,128)(2,1)S(1)}, u32[]{:S(2)}, u32[]{:S(2)}) collective-permute-start(bf16[256,512]{1,0:T(8,128)(2,1)S(1)} %collective-permute-done.rest_0_), channel_id=1, source_target_pairs={{2,0},{0,2},{6,4},{4,6},{10,8},{8,10},{14,12},{12,14},{3,1},{1,3},... | collective-permute-start | bytes 786440 | tf_op jit(solution)/shard_map/ppermute | solution.py:21
  16.9 5.8 %collective-permute-start.5 = (bf16[176,256]{1,0:T(8,128)(2,1)S(1)}, bf16[176,256]{1,0:T(8,128)(2,1)S(1)}, u32[]{:S(2)}, u32[]{:S(2)}) collective-permute-start(bf16[176,256]{1,0:T(8,128)(2,1)S(1)} %shard_map.56.sent_ref), channel_id=1, source_target_pairs={{4,0},{6,2},{0,4},{2,6},{12,8},{14,10},{8,12},{10,14},{5,1},{7,3},... | collective-permute-start | bytes 270344 | tf_op jit(solution)/shard_map/ppermute | solution.py:21
  19.4 6.3 %collective-permute-start.3 = (bf16[256,512]{1,0:T(8,128)(2,1)S(1)}, bf16[256,512]{1,0:T(8,128)(2,1)S(1)}, u32[]{:S(2)}, u32[]{:S(2)}) collective-permute-start(bf16[256,512]{1,0:T(8,128)(2,1)S(1)} %collective-permute-done.rest_0_), channel_id=1, source_target_pairs={{0,1},{1,0},{2,3},{3,2},{4,5},{5,4},{6,7},{7,6},{8,9},{9,8},{10,11... | collective-permute-start | bytes 786440 | tf_op jit(solution)/shard_map/ppermute | solution.py:35
  22.9 2.8 %collective-permute-start.6 = (bf16[256,512]{1,0:T(8,128)(2,1)S(1)}, bf16[256,512]{1,0:T(8,128)(2,1)S(1)}, u32[]{:S(2)}, u32[]{:S(2)}) collective-permute-start(bf16[256,512]{1,0:T(8,128)(2,1)S(1)} %collective-permute-done.4.rest_2_), channel_id=1, source_target_pairs={{0,1},{1,0},{2,3},{3,2},{4,5},{5,4},{6,7},{7,6},{8,9},{9,8},{10,11... | collective-permute-start | bytes 786440 | tf_op jit(solution)/shard_map/ppermute | solution.py:35
  25.4 1.5 %collective-permute-start.8 = (bf16[256,512]{1,0:T(8,128)(2,1)S(1)}, bf16[256,512]{1,0:T(8,128)(2,1)S(1)}, u32[]{:S(2)}, u32[]{:S(2)}) collective-permute-start(bf16[256,512]{1,0:T(8,128)(2,1)S(1)} %collective-permute-done.7.rest_4_), channel_id=1, source_target_pairs={{0,1},{1,0},{2,3},{3,2},{4,5},{5,4},{6,7},{7,6},{8,9},{9,8},{10,11... | collective-permute-start | bytes 786440 | tf_op jit(solution)/shard_map/ppermute | solution.py:35
  25.4 6.8 %collective-permute-start.12 = (bf16[176,256]{1,0:T(8,128)(2,1)S(1)}, bf16[176,256]{1,0:T(8,128)(2,1)S(1)}, u32[]{:S(2)}, u32[]{:S(2)}) collective-permute-start(bf16[176,256]{1,0:T(8,128)(2,1)S(1)} %shard_map.57.sent_ref), channel_id=1, source_target_pairs={{8,0},{10,2},{12,4},{14,6},{0,8},{2,10},{4,12},{6,14},{9,1},{11,3}... | collective-permute-start | bytes 270344 | tf_op jit(solution)/shard_map/ppermute | solution.py:21
  29.3 5.3 %collective-permute-start.9 = (bf16[64,512]{1,0:T(8,128)(2,1)S(1)}, bf16[64,512]{1,0:T(8,128)(2,1)S(1)}, u32[]{:S(2)}, u32[]{:S(2)}) collective-permute-start(bf16[64,512]{1,0:T(8,128)(2,1)S(1)} %convert_element_type.15), channel_id=1, source_target_pairs={{2,0},{0,2},{6,4},{4,6},{10,8},{8,10},{14,12},{12,14},{3,1},{1,3},... | collective-permute-start | bytes 196616 | tf_op jit(solution)/shard_map/ppermute | solution.py:21
  32.4 4.6 %collective-permute-start.13 = (bf16[176,256]{1,0:T(8,128)(2,1)S(1)}, bf16[176,256]{1,0:T(8,128)(2,1)S(1)}, u32[]{:S(2)}, u32[]{:S(2)}) collective-permute-start(bf16[176,256]{1,0:T(8,128)(2,1)S(1)} %shard_map.60.mine_ref), channel_id=1, source_target_pairs={{2,0},{0,2},{6,4},{4,6},{10,8},{8,10},{14,12},{12,14},{3,1},{1,3},... | collective-permute-start | bytes 270344 | tf_op jit(solution)/shard_map/ppermute | solution.py:21
  34.7 4.3 %collective-permute-start.10 = (bf16[64,512]{1,0:T(8,128)(2,1)S(1)}, bf16[64,512]{1,0:T(8,128)(2,1)S(1)}, u32[]{:S(2)}, u32[]{:S(2)}) collective-permute-start(bf16[64,512]{1,0:T(8,128)(2,1)S(1)} %fusion), channel_id=1, source_target_pairs={{4,0},{6,2},{0,4},{2,6},{12,8},{14,10},{8,12},{10,14},{5,1},{7,3},... | collective-permute-start | bytes 196616 | tf_op jit(solution)/shard_map/ppermute | solution.py:21
  34.7 5.9 %collective-permute-start.14 = (bf16[176,256]{1,0:T(8,128)(2,1)S(1)}, bf16[176,256]{1,0:T(8,128)(2,1)S(1)}, u32[]{:S(2)}, u32[]{:S(2)}) collective-permute-start(bf16[176,256]{1,0:T(8,128)(2,1)S(1)} %shard_map.60.mine_ref), channel_id=1, source_target_pairs={{0,1},{1,0},{2,3},{3,2},{4,5},{5,4},{6,7},{7,6},{8,9},{9,8},{10,11... | collective-permute-start | bytes 270344 | tf_op jit(solution)/shard_map/ppermute | solution.py:35
  37.0 3.6 %collective-permute-start.15 = (bf16[176,256]{1,0:T(8,128)(2,1)S(1)}, bf16[176,256]{1,0:T(8,128)(2,1)S(1)}, u32[]{:S(2)}, u32[]{:S(2)}) collective-permute-start(bf16[176,256]{1,0:T(8,128)(2,1)S(1)} %collective-permute-done.13.got_ref), channel_id=1, source_target_pairs={{0,1},{1,0},{2,3},{3,2},{4,5},{5,4},{6,7},{7,6},{8,9},{9,8},{10,11... | collective-permute-start | bytes 270344 | tf_op jit(solution)/shard_map/ppermute | solution.py:35
  39.0 5.4 %collective-permute-start.11 = (bf16[64,512]{1,0:T(8,128)(2,1)S(1)}, bf16[64,512]{1,0:T(8,128)(2,1)S(1)}, u32[]{:S(2)}, u32[]{:S(2)}) collective-permute-start(bf16[64,512]{1,0:T(8,128)(2,1)S(1)} %get-tuple-element.39), channel_id=1, source_target_pairs={{8,0},{10,2},{12,4},{14,6},{0,8},{2,10},{4,12},{6,14},{9,1},{11,3}... | collective-permute-start | bytes 196616 | tf_op jit(solution)/shard_map/ppermute | solution.py:21

commit v6 on v5

--- a/solution.py
+++ b/solution.py
@@ -203,8 +203,11 @@
                 corr_ref[...] += correlate(solved, subspace_ref[:, columns])
 
 
-def last_kernel(size, precond_ref, corr_ref, got_ref, gram_ref, lost_ref, subspace_ref, out_hbm, out_ref, sems):
-    corr = corr_ref[...] + got_ref[...].astype(F32)
+def last_kernel(size, precond_ref, corr_ref, *rest):
+    *got_refs, gram_ref, lost_ref, subspace_ref, out_hbm, out_ref, sems = rest
+    corr = corr_ref[...]
+    for got_ref in got_refs:
+        corr += got_ref[...].astype(F32)
     coef = corr.astype(BF16)
     again = jnp.dot(coef, gram_ref[...], preferred_element_type=F32)
     coef_2 = corr - again - coef.astype(F32) * lost_ref[0:1, :]
@@ -319,15 +322,20 @@
     gram, lost = call(
         assemble_kernel,
         (shape(vectors, vectors), shape(PAD, vectors, dtype=F32)),
-        gram, gram_far, other_core(gram), other_core(gram_far),
+        gram, gram_far, other_core(gram),
+        permute_cores(gram, lambda i, core: (i ^ 1, 1 - core)),
         scratch=[pltpu.VMEM((2 * count_half, block), F32)],
     )
 
-    step = 1
-    while 2 * step < lax.axis_size("tr"):
-        corr = corr + permute(corr.astype(BF16), lambda i: i ^ step).astype(F32)
-        step *= 2
-    got = permute(corr.astype(BF16), lambda i: i ^ step)
+    corr = corr + permute(corr.astype(BF16), lambda i: i ^ 1).astype(F32)
+    base, got = 2, []
+    while base < lax.axis_size("tr"):
+        for part in got:
+            corr = corr + part.astype(F32)
+        steps = [base, 2 * base, 3 * base] if 2 * base < lax.axis_size("tr") else [base]
+        sent = corr.astype(BF16)
+        got = [permute(sent, lambda i: i ^ step) for step in steps]
+        base *= 4
 
     def last(*refs):
         last_kernel(size, *refs)
@@ -335,11 +343,11 @@
     return pl.pallas_call(
         last,
         out_shape=wide,
-        in_specs=[VMEM] * 6,
+        in_specs=[VMEM] * (5 + len(got)),
         out_specs=HBM,
         scratch_shapes=[pltpu.VMEM((roots, columns), F32), pltpu.SemaphoreType.DMA((count,))],
         compiler_params=PARAMS,
-    )(precond, corr, got, gram, lost, subspace)
+    )(precond, corr, *got, gram, lost, subspace)
 
 
 def solution(mesh):

time: 46.4 us -> 44.9 us (0.968)
  waiting for transfers between devices: 16.4 us -> 13 us
  starting transfers between devices: 18.4 us -> 20.9 us
    ppermute x9 -> x10, waiting for transfers between devices: 15.1 us -> 11.7 us  [permute(): return lax.ppermute(block, 'tr', [(source(i) % n, i) for i in range(n)])]
    ppermute x9 -> x10, starting transfers between devices: 15.5 us -> 17.5 us  [permute(): return lax.ppermute(block, 'tr', [(source(i) % n, i) for i in range(n)])]
    pallas_call x1, Pallas kernels: 2.39 us -> 1.43 us  [per_device(): pl.pallas_call(local_kernel, out_shape=(wide, small), in_specs=[SMEM, SME...]
    pallas_call x1, Pallas kernels: 2.36 us -> 3.17 us  [fetched(): pl.pallas_call(functools.partial(fetched_kernel, kinds), out_shape=(wide,...]
    ppermute x2 -> x3, starting transfers between devices: 2.57 us -> 3.17 us  [permute_cores(): return lax.ppermute(block, ('tr', 'root'), pairs)]
    ppermute x5 -> x4, waiting for transfers between devices: 1.28 us -> 1.28 us  [other_core(): return lax.ppermute(block, 'root', [(0, 1), (1, 0)])]
  transfers between devices with their start and end apart: 16 -> 17, of which waited for: 8 -> 7; matrix products, arithmetic and copies ran while one was open for 0% -> 0% of each run, Pallas kernels for 18% -> 18%
where the time goes in v6:
time: 44.9 us
  starting transfers between devices  20.9 us (47%)
  waiting for transfers between devices  13 us (29%)
  Pallas kernels  9.84 us (22%)
  local copies, waits for them, and re-layouts  0.99 us (2%)
    ppermute x10, starting transfers between devices, permute(): return lax.ppermute(block, 'tr', [(source(i) % n, i) for i in range(n)])  17.5 us
    ppermute x10, waiting for transfers between devices, permute(): return lax.ppermute(block, 'tr', [(source(i) % n, i) for i in range(n)])  11.7 us
    pallas_call x1, Pallas kernels, fetched(): pl.pallas_call(functools.partial(fetched_kernel, kinds), out_shape=(wide,...  3.17 us
    ppermute x3, starting transfers between devices, permute_cores(): return lax.ppermute(block, ('tr', 'root'), pairs)  3.17 us
    pallas_call x1, Pallas kernels, per_device(): pl.pallas_call(gram_kernel, out_shape=(shape(*subspace.shape), shape(coun...  2.94 us
    pallas_call x1, Pallas kernels, per_device(): pl.pallas_call(last, out_shape=wide, in_specs=[VMEM] * (5 + len(got)), ou...  1.62 us
    pallas_call x1, Pallas kernels, per_device(): pl.pallas_call(local_kernel, out_shape=(wide, small), in_specs=[SMEM, SME...  1.43 us
    ppermute x4, waiting for transfers between devices, other_core(): return lax.ppermute(block, 'root', [(0, 1), (1, 0)])  1.28 us
  transfers between devices with their start and end apart: 17, of which 7 were waited for; matrix products, arithmetic and copies ran while one was open for 0% of the time, Pallas kernels for 18%

profile of v6, /device:TPU:0, one launch (start us, length us, event | category | flops | bytes accessed | tf_op | source)
XLA Modules:
  0.0 44.9 jit_solution(4190136881775256339)
XLA Ops:
  0.0 1.0 %dynamic-slice_bitcast_fusion = bf16[256,512]{1,0:T(8,128)(2,1)S(1)} fusion(bf16[1,512,512]{2,1,0:T(8,128)(2,1)} %param.7, s32[]{:T(128)S(6)} %select_n.3), kind=kLoop, calls=%fused_computation | loop fusion | bytes 524292 | tf_op jit(solution)/shard_map/dynamic_slice | solution.py:268
  1.0 5.1 %collective-permute-start = (bf16[256,512]{1,0:T(8,128)(2,1)S(1)}, bf16[256,512]{1,0:T(8,128)(2,1)S(1)}, u32[]{:S(2)}, u32[]{:S(2)}) collective-permute-start(bf16[256,512]{1,0:T(8,128)(2,1)S(1)} %dynamic-slice_bitcast_fusion), channel_id=1, source_target_pairs={{4,0},{6,2},{8,4},{10,6},{12,8},{14,10},{0,12},{2,14},{5,1},{7,3},... | collective-permute-start | bytes 786440 | tf_op jit(solution)/shard_map/ppermute | solution.py:21
  6.1 0.7 %collective-permute-start.1 = (bf16[256,512]{1,0:T(8,128)(2,1)S(1)}, bf16[256,512]{1,0:T(8,128)(2,1)S(1)}, u32[]{:S(2)}, u32[]{:S(2)}) collective-permute-start(bf16[256,512]{1,0:T(8,128)(2,1)S(1)} %dynamic-slice_bitcast_fusion), channel_id=1, source_target_pairs={{0,0},{3,1},{2,2},{1,3},{4,4},{7,5},{6,6},{5,7},{8,8},{11,9},{10,1... | collective-permute-start | bytes 786440 | tf_op jit(solution)/shard_map/ppermute | solution.py:31
  6.8 2.9 %shard_map.55 = (bf16[512,4096]{1,0:T(8,128)(2,1)S(1)}, f32[160,256]{1,0:T(8,128)S(1)}, bf16[176,256]{1,0:T(8,128)(2,1)S(1)}) custom-call(bf16[512,4096]{1,0:T(8,128)(2,1)} %subspace_hbm.1), custom_call_target="tpu_custom_call" | custom-call | flops 2147483648 | bytes 33554432 | tf_op jit(solution)/shard_map/pallas_call | solution.py:272
  9.7 1.6 %collective-permute-start.2 = (bf16[176,256]{1,0:T(8,128)(2,1)S(1)}, bf16[176,256]{1,0:T(8,128)(2,1)S(1)}, u32[]{:S(2)}, u32[]{:S(2)}) collective-permute-start(bf16[176,256]{1,0:T(8,128)(2,1)S(1)} %get-tuple-element.25), channel_id=1, source_target_pairs={{2,0},{0,2},{6,4},{4,6},{10,8},{8,10},{14,12},{12,14},{3,1},{1,3},... | collective-permute-start | bytes 270344 | tf_op jit(solution)/shard_map/ppermute | solution.py:21
  11.3 1.9 %collective-permute-start.4 = (bf16[256,512]{1,0:T(8,128)(2,1)S(1)}, bf16[256,512]{1,0:T(8,128)(2,1)S(1)}, u32[]{:S(2)}, u32[]{:S(2)}) collective-permute-start(bf16[256,512]{1,0:T(8,128)(2,1)S(1)} %collective-permute-done.1), channel_id=1, source_target_pairs={{2,0},{1,1},{8,2},{11,3},{6,4},{5,5},{12,6},{15,7},{10,8},{9,9},{0... | collective-permute-start | bytes 786440 | tf_op jit(solution)/shard_map/ppermute | solution.py:31
  13.2 1.1 %collective-permute-done.2.got_ref = bf16[176,256]{1,0:T(8,128)(2,1)S(1)} collective-permute-done((bf16[176,256]{1,0:T(8,128)(2,1)S(1)}, bf16[176,256]{1,0:T(8,128)(2,1)S(1)}, u32[]{:S(2)}, u32[]{:S(2)}) %collective-permute-start.2) | collective-permute-done | bytes 90144 | tf_op jit(solution)/shard_map/ppermute | solution.py:21
  14.3 0.1 shard_map.56.sent_ref
  14.5 2.5 %collective-permute-start.7 = (bf16[256,512]{1,0:T(8,128)(2,1)S(1)}, bf16[256,512]{1,0:T(8,128)(2,1)S(1)}, u32[]{:S(2)}, u32[]{:S(2)}) collective-permute-start(bf16[256,512]{1,0:T(8,128)(2,1)S(1)} %collective-permute-done.rest_0_), channel_id=1, source_target_pairs={{2,0},{0,2},{6,4},{4,6},{10,8},{8,10},{14,12},{12,14},{3,1},{1,3},... | collective-permute-start | bytes 786440 | tf_op jit(solution)/shard_map/ppermute | solution.py:21
  17.0 1.4 %shard_map.58 = (f32[64,4096]{1,0:T(8,128)S(1)}, f32[64,512]{1,0:T(8,128)S(1)}) custom-call(s32[8]{0:T(128)S(1)} %copy-done.2, s32[8]{0:T(128)S(1)} %copy-done.3, bf16[64,4096]{1,0:T(8,128)(2,1)S(1)} %copy-done, bf16[512,4096]{1,0:T(8,128)(2,1)S(1)} %get-tuple-element.22.subspace_ref.refs_7_, bf16[512,512]{1,0:T(8,128)(2,1)S(1)} %bitcast.3), custom_call_target="tpu_custom_call" | custom-call | tf_op jit(solution)/shard_map/pallas_call | solution.py:296
  18.4 0.1 collective-permute-start.3
  18.5 4.2 %collective-permute-done.5.got_ref = bf16[176,256]{1,0:T(8,128)(2,1)S(1)} collective-permute-done((bf16[176,256]{1,0:T(8,128)(2,1)S(1)}, bf16[176,256]{1,0:T(8,128)(2,1)S(1)}, u32[]{:S(2)}, u32[]{:S(2)}) %collective-permute-start.5) | collective-permute-done | bytes 90144 | tf_op jit(solution)/shard_map/ppermute | solution.py:21
  22.7 0.1 shard_map.57.sent_ref
  22.9 0.1 collective-permute-start.6
  23.0 2.4 %collective-permute-done.7.rest_4_ = bf16[256,512]{1,0:T(8,128)(2,1)S(1)} collective-permute-done((bf16[256,512]{1,0:T(8,128)(2,1)S(1)}, bf16[256,512]{1,0:T(8,128)(2,1)S(1)}, u32[]{:S(2)}, u32[]{:S(2)}) %collective-permute-start.7) | collective-permute-done | bytes 262176 | tf_op jit(solution)/shard_map/ppermute | solution.py:21
  25.4 0.0 collective-permute-start.8
  25.4 0.2 collective-permute-start.13
  25.7 1.3 %collective-permute-done.8.rest_5_ = bf16[256,512]{1,0:T(8,128)(2,1)S(1)} collective-permute-done((bf16[256,512]{1,0:T(8,128)(2,1)S(1)}, bf16[256,512]{1,0:T(8,128)(2,1)S(1)}, u32[]{:S(2)}, u32[]{:S(2)}) %collective-permute-start.8) | collective-permute-done | bytes 262176 | tf_op jit(solution)/shard_map/ppermute | solution.py:35
  26.9 3.2 %shard_map.59 = (f32[64,4096]{1,0:T(8,128)S(1)}, f32[64,512]{1,0:T(8,128)S(1)}) custom-call(s32[8]{0:T(128)S(1)} %copy-done.2, s32[8]{0:T(128)S(1)} %copy-done.3, bf16[64,4096]{1,0:T(8,128)(2,1)S(1)} %copy-done, bf16[512,4096]{1,0:T(8,128)(2,1)S(1)} %get-tuple-element.22.subspace_ref.refs_7_, ...), custom_call_target="tpu_custom_call", output_to_operand_aliasing={{0}: (10, {})} | custom-call | tf_op jit(solution)/shard_map/pallas_call | solution.py:305
  30.1 2.1 %collective-permute-start.9 = (bf16[64,512]{1,0:T(8,128)(2,1)S(1)}, bf16[64,512]{1,0:T(8,128)(2,1)S(1)}, u32[]{:S(2)}, u32[]{:S(2)}) collective-permute-start(bf16[64,512]{1,0:T(8,128)(2,1)S(1)} %convert_element_type.9), channel_id=1, source_target_pairs={{2,0},{0,2},{6,4},{4,6},{10,8},{8,10},{14,12},{12,14},{3,1},{1,3},... | collective-permute-start | bytes 196616 | tf_op jit(solution)/shard_map/ppermute | solution.py:21
  32.3 0.1 shard_map.60.mine_ref
  32.4 1.6 %collective-permute-start.14 = (bf16[176,256]{1,0:T(8,128)(2,1)S(1)}, bf16[176,256]{1,0:T(8,128)(2,1)S(1)}, u32[]{:S(2)}, u32[]{:S(2)}) collective-permute-start(bf16[176,256]{1,0:T(8,128)(2,1)S(1)} %shard_map.60.mine_ref), channel_id=1, source_target_pairs={{2,0},{0,2},{6,4},{4,6},{10,8},{8,10},{14,12},{12,14},{3,1},{1,3},... | collective-permute-start | bytes 270344 | tf_op jit(solution)/shard_map/ppermute | solution.py:21
  34.0 0.6 %collective-permute-start.16 = (bf16[176,256]{1,0:T(8,128)(2,1)S(1)}, bf16[176,256]{1,0:T(8,128)(2,1)S(1)}, u32[]{:S(2)}, u32[]{:S(2)}) collective-permute-start(bf16[176,256]{1,0:T(8,128)(2,1)S(1)} %shard_map.60.mine_ref), channel_id=1, source_target_pairs={{3,0},{2,1},{1,2},{0,3},{7,4},{6,5},{5,6},{4,7},{11,8},{10,9},{9,1... | collective-permute-start | bytes 270344 | tf_op jit(solution)/shard_map/ppermute | solution.py:31
  34.6 0.0 collective-permute-done.9
  34.7 0.1 collective-permute-start.10
  34.8 2.2 %collective-permute-start.11 = (bf16[64,512]{1,0:T(8,128)(2,1)S(1)}, bf16[64,512]{1,0:T(8,128)(2,1)S(1)}, u32[]{:S(2)}, u32[]{:S(2)}) collective-permute-start(bf16[64,512]{1,0:T(8,128)(2,1)S(1)} %get-tuple-element.39), channel_id=1, source_target_pairs={{8,0},{10,2},{12,4},{14,6},{0,8},{2,10},{4,12},{6,14},{9,1},{11,3}... | collective-permute-start | bytes 196616 | tf_op jit(solution)/shard_map/ppermute | solution.py:21
  36.9 0.1 collective-permute-done.14.got_ref
  37.0 2.1 %collective-permute-start.12 = (bf16[64,512]{1,0:T(8,128)(2,1)S(1)}, bf16[64,512]{1,0:T(8,128)(2,1)S(1)}, u32[]{:S(2)}, u32[]{:S(2)}) collective-permute-start(bf16[64,512]{1,0:T(8,128)(2,1)S(1)} %get-tuple-element.39), channel_id=1, source_target_pairs={{12,0},{14,2},{8,4},{10,6},{4,8},{6,10},{0,12},{2,14},{13,1},{15,3... | collective-permute-start | bytes 196616 | tf_op jit(solution)/shard_map/ppermute | solution.py:21
  39.1 0.3 shard_map.61
  39.4 0.6 %collective-permute-done.10.refs_2_ = bf16[64,512]{1,0:T(8,128)(2,1)S(1)} collective-permute-done((bf16[64,512]{1,0:T(8,128)(2,1)S(1)}, bf16[64,512]{1,0:T(8,128)(2,1)S(1)}, u32[]{:S(2)}, u32[]{:S(2)}) %collective-permute-start.10) | collective-permute-done | bytes 65568 | tf_op jit(solution)/shard_map/ppermute | solution.py:21
  40.0 3.2 %collective-permute-done.11.refs_3_ = bf16[64,512]{1,0:T(8,128)(2,1)S(1)} collective-permute-done((bf16[64,512]{1,0:T(8,128)(2,1)S(1)}, bf16[64,512]{1,0:T(8,128)(2,1)S(1)}, u32[]{:S(2)}, u32[]{:S(2)}) %collective-permute-start.11) | collective-permute-done | bytes 65568 | tf_op jit(solution)/shard_map/ppermute | solution.py:21
  43.2 1.6 %shard_map.62 = f32[64,4096]{1,0:T(8,128)} custom-call(f32[64,4096]{1,0:T(8,128)S(1)} %get-tuple-element.34.refs_0_, f32[64,512]{1,0:T(8,128)S(1)} %get-tuple-element.40.refs_1_, bf16[64,512]{1,0:T(8,128)(2,1)S(1)} %collective-permute-done.10.refs_2_, bf16[64,512]{1,0:T(8,128)(2,1)S(1)} %collective-permute-done.11.refs_3_, ...), custom_call_target="tpu_custom_call" | custom-call | tf_op jit(solution)/shard_map/pallas_call | solution.py:343
  (21 shorter events, 0.1 us)
Async XLA Ops:
  1.0 16.0 %copy-start = (bf16[64,4096]{1,0:T(8,128)(2,1)S(1)}, bf16[64,4096]{1,0:T(8,128)(2,1)}, u32[]{:S(2)}) copy-start(bf16[64,4096]{1,0:T(8,128)(2,1)} %residual_ref.3) | copy-start | bytes 1572868
  1.0 16.0 %copy-start.1 = (bf16[1,512,512]{2,1,0:T(8,128)(2,1)S(1)}, bf16[1,512,512]{2,1,0:T(8,128)(2,1)}, u32[]{:S(2)}) copy-start(bf16[1,512,512]{2,1,0:T(8,128)(2,1)} %param.7) | copy-start | bytes 1572868
  1.0 16.0 %copy-start.2 = (s32[8]{0:T(128)S(1)}, s32[8]{0:T(128)}, u32[]{:S(2)}) copy-start(s32[8]{0:T(128)} %offset_ref.3) | copy-start | bytes 100
  1.0 16.0 %copy-start.3 = (s32[8]{0:T(128)S(1)}, s32[8]{0:T(128)}, u32[]{:S(2)}) copy-start(s32[8]{0:T(128)} %listed_ref.3) | copy-start | bytes 100
  1.0 13.5 %collective-permute-start = (bf16[256,512]{1,0:T(8,128)(2,1)S(1)}, bf16[256,512]{1,0:T(8,128)(2,1)S(1)}, u32[]{:S(2)}, u32[]{:S(2)}) collective-permute-start(bf16[256,512]{1,0:T(8,128)(2,1)S(1)} %dynamic-slice_bitcast_fusion), channel_id=1, source_target_pairs={{4,0},{6,2},{8,4},{10,6},{12,8},{14,10},{0,12},{2,14},{5,1},{7,3},... | collective-permute-start | bytes 786440 | tf_op jit(solution)/shard_map/ppermute | solution.py:21
  6.1 5.2 %collective-permute-start.1 = (bf16[256,512]{1,0:T(8,128)(2,1)S(1)}, bf16[256,512]{1,0:T(8,128)(2,1)S(1)}, u32[]{:S(2)}, u32[]{:S(2)}) collective-permute-start(bf16[256,512]{1,0:T(8,128)(2,1)S(1)} %dynamic-slice_bitcast_fusion), channel_id=1, source_target_pairs={{0,0},{3,1},{2,2},{1,3},{4,4},{7,5},{6,6},{5,7},{8,8},{11,9},{10,1... | collective-permute-start | bytes 786440 | tf_op jit(solution)/shard_map/ppermute | solution.py:31
  9.7 4.6 %collective-permute-start.2 = (bf16[176,256]{1,0:T(8,128)(2,1)S(1)}, bf16[176,256]{1,0:T(8,128)(2,1)S(1)}, u32[]{:S(2)}, u32[]{:S(2)}) collective-permute-start(bf16[176,256]{1,0:T(8,128)(2,1)S(1)} %get-tuple-element.25), channel_id=1, source_target_pairs={{2,0},{0,2},{6,4},{4,6},{10,8},{8,10},{14,12},{12,14},{3,1},{1,3},... | collective-permute-start | bytes 270344 | tf_op jit(solution)/shard_map/ppermute | solution.py:21
  11.3 11.6 %collective-permute-start.4 = (bf16[256,512]{1,0:T(8,128)(2,1)S(1)}, bf16[256,512]{1,0:T(8,128)(2,1)S(1)}, u32[]{:S(2)}, u32[]{:S(2)}) collective-permute-start(bf16[256,512]{1,0:T(8,128)(2,1)S(1)} %collective-permute-done.1), channel_id=1, source_target_pairs={{2,0},{1,1},{8,2},{11,3},{6,4},{5,5},{12,6},{15,7},{10,8},{9,9},{0... | collective-permute-start | bytes 786440 | tf_op jit(solution)/shard_map/ppermute | solution.py:31
  14.5 10.9 %collective-permute-start.7 = (bf16[256,512]{1,0:T(8,128)(2,1)S(1)}, bf16[256,512]{1,0:T(8,128)(2,1)S(1)}, u32[]{:S(2)}, u32[]{:S(2)}) collective-permute-start(bf16[256,512]{1,0:T(8,128)(2,1)S(1)} %collective-permute-done.rest_0_), channel_id=1, source_target_pairs={{2,0},{0,2},{6,4},{4,6},{10,8},{8,10},{14,12},{12,14},{3,1},{1,3},... | collective-permute-start | bytes 786440 | tf_op jit(solution)/shard_map/ppermute | solution.py:21
  16.9 5.8 %collective-permute-start.5 = (bf16[176,256]{1,0:T(8,128)(2,1)S(1)}, bf16[176,256]{1,0:T(8,128)(2,1)S(1)}, u32[]{:S(2)}, u32[]{:S(2)}) collective-permute-start(bf16[176,256]{1,0:T(8,128)(2,1)S(1)} %shard_map.56.sent_ref), channel_id=1, source_target_pairs={{4,0},{6,2},{0,4},{2,6},{12,8},{14,10},{8,12},{10,14},{5,1},{7,3},... | collective-permute-start | bytes 270344 | tf_op jit(solution)/shard_map/ppermute | solution.py:21
  18.4 7.3 %collective-permute-start.3 = (bf16[256,512]{1,0:T(8,128)(2,1)S(1)}, bf16[256,512]{1,0:T(8,128)(2,1)S(1)}, u32[]{:S(2)}, u32[]{:S(2)}) collective-permute-start(bf16[256,512]{1,0:T(8,128)(2,1)S(1)} %collective-permute-done.rest_0_), channel_id=1, source_target_pairs={{0,1},{1,0},{2,3},{3,2},{4,5},{5,4},{6,7},{7,6},{8,9},{9,8},{10,11... | collective-permute-start | bytes 786440 | tf_op jit(solution)/shard_map/ppermute | solution.py:35
  22.9 2.8 %collective-permute-start.6 = (bf16[256,512]{1,0:T(8,128)(2,1)S(1)}, bf16[256,512]{1,0:T(8,128)(2,1)S(1)}, u32[]{:S(2)}, u32[]{:S(2)}) collective-permute-start(bf16[256,512]{1,0:T(8,128)(2,1)S(1)} %collective-permute-done.4.rest_2_), channel_id=1, source_target_pairs={{0,1},{1,0},{2,3},{3,2},{4,5},{5,4},{6,7},{7,6},{8,9},{9,8},{10,11... | collective-permute-start | bytes 786440 | tf_op jit(solution)/shard_map/ppermute | solution.py:35
  25.4 1.5 %collective-permute-start.8 = (bf16[256,512]{1,0:T(8,128)(2,1)S(1)}, bf16[256,512]{1,0:T(8,128)(2,1)S(1)}, u32[]{:S(2)}, u32[]{:S(2)}) collective-permute-start(bf16[256,512]{1,0:T(8,128)(2,1)S(1)} %collective-permute-done.7.rest_4_), channel_id=1, source_target_pairs={{0,1},{1,0},{2,3},{3,2},{4,5},{5,4},{6,7},{7,6},{8,9},{9,8},{10,11... | collective-permute-start | bytes 786440 | tf_op jit(solution)/shard_map/ppermute | solution.py:35
  25.4 6.8 %collective-permute-start.13 = (bf16[176,256]{1,0:T(8,128)(2,1)S(1)}, bf16[176,256]{1,0:T(8,128)(2,1)S(1)}, u32[]{:S(2)}, u32[]{:S(2)}) collective-permute-start(bf16[176,256]{1,0:T(8,128)(2,1)S(1)} %shard_map.57.sent_ref), channel_id=1, source_target_pairs={{8,0},{10,2},{12,4},{14,6},{0,8},{2,10},{4,12},{6,14},{9,1},{11,3}... | collective-permute-start | bytes 270344 | tf_op jit(solution)/shard_map/ppermute | solution.py:21
  30.1 4.5 %collective-permute-start.9 = (bf16[64,512]{1,0:T(8,128)(2,1)S(1)}, bf16[64,512]{1,0:T(8,128)(2,1)S(1)}, u32[]{:S(2)}, u32[]{:S(2)}) collective-permute-start(bf16[64,512]{1,0:T(8,128)(2,1)S(1)} %convert_element_type.9), channel_id=1, source_target_pairs={{2,0},{0,2},{6,4},{4,6},{10,8},{8,10},{14,12},{12,14},{3,1},{1,3},... | collective-permute-start | bytes 196616 | tf_op jit(solution)/shard_map/ppermute | solution.py:21
  32.4 4.6 %collective-permute-start.14 = (bf16[176,256]{1,0:T(8,128)(2,1)S(1)}, bf16[176,256]{1,0:T(8,128)(2,1)S(1)}, u32[]{:S(2)}, u32[]{:S(2)}) collective-permute-start(bf16[176,256]{1,0:T(8,128)(2,1)S(1)} %shard_map.60.mine_ref), channel_id=1, source_target_pairs={{2,0},{0,2},{6,4},{4,6},{10,8},{8,10},{14,12},{12,14},{3,1},{1,3},... | collective-permute-start | bytes 270344 | tf_op jit(solution)/shard_map/ppermute | solution.py:21
  34.0 5.1 %collective-permute-start.15 = (bf16[176,256]{1,0:T(8,128)(2,1)S(1)}, bf16[176,256]{1,0:T(8,128)(2,1)S(1)}, u32[]{:S(2)}, u32[]{:S(2)}) collective-permute-start(bf16[176,256]{1,0:T(8,128)(2,1)S(1)} %shard_map.60.mine_ref), channel_id=1, source_target_pairs={{0,1},{1,0},{2,3},{3,2},{4,5},{5,4},{6,7},{7,6},{8,9},{9,8},{10,11... | collective-permute-start | bytes 270344 | tf_op jit(solution)/shard_map/ppermute | solution.py:35
  34.0 5.1 %collective-permute-start.16 = (bf16[176,256]{1,0:T(8,128)(2,1)S(1)}, bf16[176,256]{1,0:T(8,128)(2,1)S(1)}, u32[]{:S(2)}, u32[]{:S(2)}) collective-permute-start(bf16[176,256]{1,0:T(8,128)(2,1)S(1)} %shard_map.60.mine_ref), channel_id=1, source_target_pairs={{3,0},{2,1},{1,2},{0,3},{7,4},{6,5},{5,6},{4,7},{11,8},{10,9},{9,1... | collective-permute-start | bytes 270344 | tf_op jit(solution)/shard_map/ppermute | solution.py:31
  34.7 5.4 %collective-permute-start.10 = (bf16[64,512]{1,0:T(8,128)(2,1)S(1)}, bf16[64,512]{1,0:T(8,128)(2,1)S(1)}, u32[]{:S(2)}, u32[]{:S(2)}) collective-permute-start(bf16[64,512]{1,0:T(8,128)(2,1)S(1)} %get-tuple-element.39), channel_id=1, source_target_pairs={{4,0},{6,2},{0,4},{2,6},{12,8},{14,10},{8,12},{10,14},{5,1},{7,3},... | collective-permute-start | bytes 196616 | tf_op jit(solution)/shard_map/ppermute | solution.py:21
  34.8 8.5 %collective-permute-start.11 = (bf16[64,512]{1,0:T(8,128)(2,1)S(1)}, bf16[64,512]{1,0:T(8,128)(2,1)S(1)}, u32[]{:S(2)}, u32[]{:S(2)}) collective-permute-start(bf16[64,512]{1,0:T(8,128)(2,1)S(1)} %get-tuple-element.39), channel_id=1, source_target_pairs={{8,0},{10,2},{12,4},{14,6},{0,8},{2,10},{4,12},{6,14},{9,1},{11,3}... | collective-permute-start | bytes 196616 | tf_op jit(solution)/shard_map/ppermute | solution.py:21
  37.0 6.2 %collective-permute-start.12 = (bf16[64,512]{1,0:T(8,128)(2,1)S(1)}, bf16[64,512]{1,0:T(8,128)(2,1)S(1)}, u32[]{:S(2)}, u32[]{:S(2)}) collective-permute-start(bf16[64,512]{1,0:T(8,128)(2,1)S(1)} %get-tuple-element.39), channel_id=1, source_target_pairs={{12,0},{14,2},{8,4},{10,6},{4,8},{6,10},{0,12},{2,14},{13,1},{15,3... | collective-permute-start | bytes 196616 | tf_op jit(solution)/shard_map/ppermute | solution.py:21

commit v7 on v6

--- a/solution.py
+++ b/solution.py
@@ -327,15 +327,16 @@
         scratch=[pltpu.VMEM((2 * count_half, block), F32)],
     )
 
-    corr = corr + permute(corr.astype(BF16), lambda i: i ^ 1).astype(F32)
-    base, got = 2, []
+    groups, base = [[4], [1, 2, 3]], 8
     while base < lax.axis_size("tr"):
+        groups.append([base])
+        base *= 2
+    got = []
+    for steps in groups:
         for part in got:
             corr = corr + part.astype(F32)
-        steps = [base, 2 * base, 3 * base] if 2 * base < lax.axis_size("tr") else [base]
         sent = corr.astype(BF16)
         got = [permute(sent, lambda i: i ^ step) for step in steps]
-        base *= 4
 
     def last(*refs):
         last_kernel(size, *refs)

time: 44.9 us -> 44.5 us (level)
  starting transfers between devices: 20.9 us -> 20.1 us
  transfers between devices with their start and end apart: 17 -> 17, of which waited for: 7 -> 8; matrix products, arithmetic and copies ran while one was open for 0% -> 0% of each run, Pallas kernels for 18% -> 19%
where the time goes in v7:
time: 44.5 us; the launch traced here: 44.3 us
  starting transfers between devices  20.1 us (45%)
  waiting for transfers between devices  13.2 us (30%)
  Pallas kernels  9.83 us (22%)
  local copies, waits for them, and re-layouts  0.99 us (2%)
    ppermute x10, starting transfers between devices, permute(): return lax.ppermute(block, 'tr', [(source(i) % n, i) for i in range(n)])  17.1 us
    ppermute x10, waiting for transfers between devices, permute(): return lax.ppermute(block, 'tr', [(source(i) % n, i) for i in range(n)])  11.9 us
    pallas_call x1, Pallas kernels, fetched(): pl.pallas_call(functools.partial(fetched_kernel, kinds), out_shape=(wide,...  3.16 us
    pallas_call x1, Pallas kernels, per_device(): pl.pallas_call(gram_kernel, out_shape=(shape(*subspace.shape), shape(coun...  2.94 us
    ppermute x3, starting transfers between devices, permute_cores(): return lax.ppermute(block, ('tr', 'root'), pairs)  2.78 us
    pallas_call x1, Pallas kernels, per_device(): pl.pallas_call(last, out_shape=wide, in_specs=[VMEM] * (5 + len(got)), ou...  1.62 us
    pallas_call x1, Pallas kernels, per_device(): pl.pallas_call(local_kernel, out_shape=(wide, small), in_specs=[SMEM, SME...  1.43 us
    ppermute x4, waiting for transfers between devices, other_core(): return lax.ppermute(block, 'root', [(0, 1), (1, 0)])  1.28 us
  transfers between devices with their start and end apart: 17, of which 8 were waited for; matrix products, arithmetic and copies ran while one was open for 0% of the time, Pallas kernels for 19%

profile of v7, /device:TPU:0, one launch (start us, length us, event | category | flops | bytes accessed | tf_op | source)
XLA Modules:
  0.0 44.3 jit_solution(2109652293109804739)
XLA Ops:
  0.0 1.0 %dynamic-slice_bitcast_fusion = bf16[256,512]{1,0:T(8,128)(2,1)S(1)} fusion(bf16[1,512,512]{2,1,0:T(8,128)(2,1)} %param.7, s32[]{:T(128)S(6)} %select_n.3), kind=kLoop, calls=%fused_computation | loop fusion | bytes 524292 | tf_op jit(solution)/shard_map/dynamic_slice | solution.py:268
  1.0 0.0 copy-start.2
  1.0 5.1 %collective-permute-start = (bf16[256,512]{1,0:T(8,128)(2,1)S(1)}, bf16[256,512]{1,0:T(8,128)(2,1)S(1)}, u32[]{:S(2)}, u32[]{:S(2)}) collective-permute-start(bf16[256,512]{1,0:T(8,128)(2,1)S(1)} %dynamic-slice_bitcast_fusion), channel_id=1, source_target_pairs={{4,0},{6,2},{8,4},{10,6},{12,8},{14,10},{0,12},{2,14},{5,1},{7,3},... | collective-permute-start | bytes 786440 | tf_op jit(solution)/shard_map/ppermute | solution.py:21
  6.1 0.7 %collective-permute-start.1 = (bf16[256,512]{1,0:T(8,128)(2,1)S(1)}, bf16[256,512]{1,0:T(8,128)(2,1)S(1)}, u32[]{:S(2)}, u32[]{:S(2)}) collective-permute-start(bf16[256,512]{1,0:T(8,128)(2,1)S(1)} %dynamic-slice_bitcast_fusion), channel_id=1, source_target_pairs={{0,0},{3,1},{2,2},{1,3},{4,4},{7,5},{6,6},{5,7},{8,8},{11,9},{10,1... | collective-permute-start | bytes 786440 | tf_op jit(solution)/shard_map/ppermute | solution.py:31
  6.8 2.9 %shard_map.55 = (bf16[512,4096]{1,0:T(8,128)(2,1)S(1)}, f32[160,256]{1,0:T(8,128)S(1)}, bf16[176,256]{1,0:T(8,128)(2,1)S(1)}) custom-call(bf16[512,4096]{1,0:T(8,128)(2,1)} %subspace_hbm.1), custom_call_target="tpu_custom_call" | custom-call | flops 2147483648 | bytes 33554432 | tf_op jit(solution)/shard_map/pallas_call | solution.py:272
  9.7 1.6 %collective-permute-start.2 = (bf16[176,256]{1,0:T(8,128)(2,1)S(1)}, bf16[176,256]{1,0:T(8,128)(2,1)S(1)}, u32[]{:S(2)}, u32[]{:S(2)}) collective-permute-start(bf16[176,256]{1,0:T(8,128)(2,1)S(1)} %get-tuple-element.25), channel_id=1, source_target_pairs={{2,0},{0,2},{6,4},{4,6},{10,8},{8,10},{14,12},{12,14},{3,1},{1,3},... | collective-permute-start | bytes 270344 | tf_op jit(solution)/shard_map/ppermute | solution.py:21
  11.3 1.9 %collective-permute-start.4 = (bf16[256,512]{1,0:T(8,128)(2,1)S(1)}, bf16[256,512]{1,0:T(8,128)(2,1)S(1)}, u32[]{:S(2)}, u32[]{:S(2)}) collective-permute-start(bf16[256,512]{1,0:T(8,128)(2,1)S(1)} %collective-permute-done.1), channel_id=1, source_target_pairs={{2,0},{1,1},{8,2},{11,3},{6,4},{5,5},{12,6},{15,7},{10,8},{9,9},{0... | collective-permute-start | bytes 786440 | tf_op jit(solution)/shard_map/ppermute | solution.py:31
  13.2 1.1 %collective-permute-done.2.got_ref = bf16[176,256]{1,0:T(8,128)(2,1)S(1)} collective-permute-done((bf16[176,256]{1,0:T(8,128)(2,1)S(1)}, bf16[176,256]{1,0:T(8,128)(2,1)S(1)}, u32[]{:S(2)}, u32[]{:S(2)}) %collective-permute-start.2) | collective-permute-done | bytes 90144 | tf_op jit(solution)/shard_map/ppermute | solution.py:21
  14.3 0.1 shard_map.56.sent_ref
  14.5 2.5 %collective-permute-start.7 = (bf16[256,512]{1,0:T(8,128)(2,1)S(1)}, bf16[256,512]{1,0:T(8,128)(2,1)S(1)}, u32[]{:S(2)}, u32[]{:S(2)}) collective-permute-start(bf16[256,512]{1,0:T(8,128)(2,1)S(1)} %collective-permute-done.rest_0_), channel_id=1, source_target_pairs={{2,0},{0,2},{6,4},{4,6},{10,8},{8,10},{14,12},{12,14},{3,1},{1,3},... | collective-permute-start | bytes 786440 | tf_op jit(solution)/shard_map/ppermute | solution.py:21
  17.0 1.4 %shard_map.58 = (f32[64,4096]{1,0:T(8,128)S(1)}, f32[64,512]{1,0:T(8,128)S(1)}) custom-call(s32[8]{0:T(128)S(1)} %copy-done.2, s32[8]{0:T(128)S(1)} %copy-done.3, bf16[64,4096]{1,0:T(8,128)(2,1)S(1)} %copy-done, bf16[512,4096]{1,0:T(8,128)(2,1)S(1)} %get-tuple-element.22.subspace_ref.refs_7_, bf16[512,512]{1,0:T(8,128)(2,1)S(1)} %bitcast.3), custom_call_target="tpu_custom_call" | custom-call | tf_op jit(solution)/shard_map/pallas_call | solution.py:296
  18.4 0.1 collective-permute-start.3
  18.5 4.2 %collective-permute-done.5.got_ref = bf16[176,256]{1,0:T(8,128)(2,1)S(1)} collective-permute-done((bf16[176,256]{1,0:T(8,128)(2,1)S(1)}, bf16[176,256]{1,0:T(8,128)(2,1)S(1)}, u32[]{:S(2)}, u32[]{:S(2)}) %collective-permute-start.5) | collective-permute-done | bytes 90144 | tf_op jit(solution)/shard_map/ppermute | solution.py:21
  22.7 0.1 shard_map.57.sent_ref
  22.9 0.1 collective-permute-start.6
  23.0 2.4 %collective-permute-done.7.rest_4_ = bf16[256,512]{1,0:T(8,128)(2,1)S(1)} collective-permute-done((bf16[256,512]{1,0:T(8,128)(2,1)S(1)}, bf16[256,512]{1,0:T(8,128)(2,1)S(1)}, u32[]{:S(2)}, u32[]{:S(2)}) %collective-permute-start.7) | collective-permute-done | bytes 262176 | tf_op jit(solution)/shard_map/ppermute | solution.py:21
  25.4 0.0 collective-permute-start.8
  25.4 0.2 collective-permute-start.13
  25.7 1.3 %collective-permute-done.8.rest_5_ = bf16[256,512]{1,0:T(8,128)(2,1)S(1)} collective-permute-done((bf16[256,512]{1,0:T(8,128)(2,1)S(1)}, bf16[256,512]{1,0:T(8,128)(2,1)S(1)}, u32[]{:S(2)}, u32[]{:S(2)}) %collective-permute-start.8) | collective-permute-done | bytes 262176 | tf_op jit(solution)/shard_map/ppermute | solution.py:35
  26.9 3.2 %shard_map.59 = (f32[64,4096]{1,0:T(8,128)S(1)}, f32[64,512]{1,0:T(8,128)S(1)}) custom-call(s32[8]{0:T(128)S(1)} %copy-done.2, s32[8]{0:T(128)S(1)} %copy-done.3, bf16[64,4096]{1,0:T(8,128)(2,1)S(1)} %copy-done, bf16[512,4096]{1,0:T(8,128)(2,1)S(1)} %get-tuple-element.22.subspace_ref.refs_7_, ...), custom_call_target="tpu_custom_call", output_to_operand_aliasing={{0}: (10, {})} | custom-call | tf_op jit(solution)/shard_map/pallas_call | solution.py:305
  30.1 1.5 %collective-permute-start.9 = (bf16[64,512]{1,0:T(8,128)(2,1)S(1)}, bf16[64,512]{1,0:T(8,128)(2,1)S(1)}, u32[]{:S(2)}, u32[]{:S(2)}) collective-permute-start(bf16[64,512]{1,0:T(8,128)(2,1)S(1)} %convert_element_type.9), channel_id=1, source_target_pairs={{8,0},{10,2},{12,4},{14,6},{0,8},{2,10},{4,12},{6,14},{9,1},{11,3}... | collective-permute-start | bytes 196616 | tf_op jit(solution)/shard_map/ppermute | solution.py:21
  31.6 0.1 shard_map.60.mine_ref
  31.8 2.5 %collective-permute-start.14 = (bf16[176,256]{1,0:T(8,128)(2,1)S(1)}, bf16[176,256]{1,0:T(8,128)(2,1)S(1)}, u32[]{:S(2)}, u32[]{:S(2)}) collective-permute-start(bf16[176,256]{1,0:T(8,128)(2,1)S(1)} %shard_map.60.mine_ref), channel_id=1, source_target_pairs={{2,0},{0,2},{6,4},{4,6},{10,8},{8,10},{14,12},{12,14},{3,1},{1,3},... | collective-permute-start | bytes 270344 | tf_op jit(solution)/shard_map/ppermute | solution.py:21
  34.3 0.2 collective-permute-start.16
  34.5 0.8 %collective-permute-done.9 = bf16[64,512]{1,0:T(8,128)(2,1)S(1)} collective-permute-done((bf16[64,512]{1,0:T(8,128)(2,1)S(1)}, bf16[64,512]{1,0:T(8,128)(2,1)S(1)}, u32[]{:S(2)}, u32[]{:S(2)}) %collective-permute-start.9) | collective-permute-done | bytes 65568 | tf_op jit(solution)/shard_map/ppermute | solution.py:21
  35.4 2.2 %collective-permute-start.10 = (bf16[64,512]{1,0:T(8,128)(2,1)S(1)}, bf16[64,512]{1,0:T(8,128)(2,1)S(1)}, u32[]{:S(2)}, u32[]{:S(2)}) collective-permute-start(bf16[64,512]{1,0:T(8,128)(2,1)S(1)} %get-tuple-element.39), channel_id=1, source_target_pairs={{2,0},{0,2},{6,4},{4,6},{10,8},{8,10},{14,12},{12,14},{3,1},{1,3},... | collective-permute-start | bytes 196616 | tf_op jit(solution)/shard_map/ppermute | solution.py:21
  37.5 1.5 %collective-permute-start.12 = (bf16[64,512]{1,0:T(8,128)(2,1)S(1)}, bf16[64,512]{1,0:T(8,128)(2,1)S(1)}, u32[]{:S(2)}, u32[]{:S(2)}) collective-permute-start(bf16[64,512]{1,0:T(8,128)(2,1)S(1)} %get-tuple-element.39), channel_id=1, source_target_pairs={{6,0},{4,2},{2,4},{0,6},{14,8},{12,10},{10,12},{8,14},{7,1},{5,3},... | collective-permute-start | bytes 196616 | tf_op jit(solution)/shard_map/ppermute | solution.py:21
  39.1 0.3 shard_map.61
  39.4 2.0 %collective-permute-done.10.refs_2_ = bf16[64,512]{1,0:T(8,128)(2,1)S(1)} collective-permute-done((bf16[64,512]{1,0:T(8,128)(2,1)S(1)}, bf16[64,512]{1,0:T(8,128)(2,1)S(1)}, u32[]{:S(2)}, u32[]{:S(2)}) %collective-permute-start.10) | collective-permute-done | bytes 65568 | tf_op jit(solution)/shard_map/ppermute | solution.py:21
  41.4 0.4 %collective-permute-done.11.refs_3_ = bf16[64,512]{1,0:T(8,128)(2,1)S(1)} collective-permute-done((bf16[64,512]{1,0:T(8,128)(2,1)S(1)}, bf16[64,512]{1,0:T(8,128)(2,1)S(1)}, u32[]{:S(2)}, u32[]{:S(2)}) %collective-permute-start.11) | collective-permute-done | bytes 65568 | tf_op jit(solution)/shard_map/ppermute | solution.py:21
  41.8 0.9 %collective-permute-done.12.refs_4_ = bf16[64,512]{1,0:T(8,128)(2,1)S(1)} collective-permute-done((bf16[64,512]{1,0:T(8,128)(2,1)S(1)}, bf16[64,512]{1,0:T(8,128)(2,1)S(1)}, u32[]{:S(2)}, u32[]{:S(2)}) %collective-permute-start.12) | collective-permute-done | bytes 65568 | tf_op jit(solution)/shard_map/ppermute | solution.py:21
  42.7 1.6 %shard_map.62 = f32[64,4096]{1,0:T(8,128)} custom-call(f32[64,4096]{1,0:T(8,128)S(1)} %get-tuple-element.34.refs_0_, f32[64,512]{1,0:T(8,128)S(1)} %get-tuple-element.40.refs_1_, bf16[64,512]{1,0:T(8,128)(2,1)S(1)} %collective-permute-done.10.refs_2_, bf16[64,512]{1,0:T(8,128)(2,1)S(1)} %collective-permute-done.11.refs_3_, ...), custom_call_target="tpu_custom_call" | custom-call | tf_op jit(solution)/shard_map/pallas_call | solution.py:344
  (21 shorter events, 0.1 us)
Async XLA Ops:
  1.0 16.0 %copy-start = (bf16[64,4096]{1,0:T(8,128)(2,1)S(1)}, bf16[64,4096]{1,0:T(8,128)(2,1)}, u32[]{:S(2)}) copy-start(bf16[64,4096]{1,0:T(8,128)(2,1)} %residual_ref.3) | copy-start | bytes 1572868
  1.0 16.0 %copy-start.1 = (bf16[1,512,512]{2,1,0:T(8,128)(2,1)S(1)}, bf16[1,512,512]{2,1,0:T(8,128)(2,1)}, u32[]{:S(2)}) copy-start(bf16[1,512,512]{2,1,0:T(8,128)(2,1)} %param.7) | copy-start | bytes 1572868
  1.0 16.0 %copy-start.2 = (s32[8]{0:T(128)S(1)}, s32[8]{0:T(128)}, u32[]{:S(2)}) copy-start(s32[8]{0:T(128)} %offset_ref.3) | copy-start | bytes 100
  1.0 16.0 %copy-start.3 = (s32[8]{0:T(128)S(1)}, s32[8]{0:T(128)}, u32[]{:S(2)}) copy-start(s32[8]{0:T(128)} %listed_ref.3) | copy-start | bytes 100
  1.0 13.5 %collective-permute-start = (bf16[256,512]{1,0:T(8,128)(2,1)S(1)}, bf16[256,512]{1,0:T(8,128)(2,1)S(1)}, u32[]{:S(2)}, u32[]{:S(2)}) collective-permute-start(bf16[256,512]{1,0:T(8,128)(2,1)S(1)} %dynamic-slice_bitcast_fusion), channel_id=1, source_target_pairs={{4,0},{6,2},{8,4},{10,6},{12,8},{14,10},{0,12},{2,14},{5,1},{7,3},... | collective-permute-start | bytes 786440 | tf_op jit(solution)/shard_map/ppermute | solution.py:21
  6.1 5.2 %collective-permute-start.1 = (bf16[256,512]{1,0:T(8,128)(2,1)S(1)}, bf16[256,512]{1,0:T(8,128)(2,1)S(1)}, u32[]{:S(2)}, u32[]{:S(2)}) collective-permute-start(bf16[256,512]{1,0:T(8,128)(2,1)S(1)} %dynamic-slice_bitcast_fusion), channel_id=1, source_target_pairs={{0,0},{3,1},{2,2},{1,3},{4,4},{7,5},{6,6},{5,7},{8,8},{11,9},{10,1... | collective-permute-start | bytes 786440 | tf_op jit(solution)/shard_map/ppermute | solution.py:31
  9.7 4.6 %collective-permute-start.2 = (bf16[176,256]{1,0:T(8,128)(2,1)S(1)}, bf16[176,256]{1,0:T(8,128)(2,1)S(1)}, u32[]{:S(2)}, u32[]{:S(2)}) collective-permute-start(bf16[176,256]{1,0:T(8,128)(2,1)S(1)} %get-tuple-element.25), channel_id=1, source_target_pairs={{2,0},{0,2},{6,4},{4,6},{10,8},{8,10},{14,12},{12,14},{3,1},{1,3},... | collective-permute-start | bytes 270344 | tf_op jit(solution)/shard_map/ppermute | solution.py:21
  11.3 11.6 %collective-permute-start.4 = (bf16[256,512]{1,0:T(8,128)(2,1)S(1)}, bf16[256,512]{1,0:T(8,128)(2,1)S(1)}, u32[]{:S(2)}, u32[]{:S(2)}) collective-permute-start(bf16[256,512]{1,0:T(8,128)(2,1)S(1)} %collective-permute-done.1), channel_id=1, source_target_pairs={{2,0},{1,1},{8,2},{11,3},{6,4},{5,5},{12,6},{15,7},{10,8},{9,9},{0... | collective-permute-start | bytes 786440 | tf_op jit(solution)/shard_map/ppermute | solution.py:31
  14.5 10.9 %collective-permute-start.7 = (bf16[256,512]{1,0:T(8,128)(2,1)S(1)}, bf16[256,512]{1,0:T(8,128)(2,1)S(1)}, u32[]{:S(2)}, u32[]{:S(2)}) collective-permute-start(bf16[256,512]{1,0:T(8,128)(2,1)S(1)} %collective-permute-done.rest_0_), channel_id=1, source_target_pairs={{2,0},{0,2},{6,4},{4,6},{10,8},{8,10},{14,12},{12,14},{3,1},{1,3},... | collective-permute-start | bytes 786440 | tf_op jit(solution)/shard_map/ppermute | solution.py:21
  16.9 5.8 %collective-permute-start.5 = (bf16[176,256]{1,0:T(8,128)(2,1)S(1)}, bf16[176,256]{1,0:T(8,128)(2,1)S(1)}, u32[]{:S(2)}, u32[]{:S(2)}) collective-permute-start(bf16[176,256]{1,0:T(8,128)(2,1)S(1)} %shard_map.56.sent_ref), channel_id=1, source_target_pairs={{4,0},{6,2},{0,4},{2,6},{12,8},{14,10},{8,12},{10,14},{5,1},{7,3},... | collective-permute-start | bytes 270344 | tf_op jit(solution)/shard_map/ppermute | solution.py:21
  18.4 7.3 %collective-permute-start.3 = (bf16[256,512]{1,0:T(8,128)(2,1)S(1)}, bf16[256,512]{1,0:T(8,128)(2,1)S(1)}, u32[]{:S(2)}, u32[]{:S(2)}) collective-permute-start(bf16[256,512]{1,0:T(8,128)(2,1)S(1)} %collective-permute-done.rest_0_), channel_id=1, source_target_pairs={{0,1},{1,0},{2,3},{3,2},{4,5},{5,4},{6,7},{7,6},{8,9},{9,8},{10,11... | collective-permute-start | bytes 786440 | tf_op jit(solution)/shard_map/ppermute | solution.py:35
  22.9 2.8 %collective-permute-start.6 = (bf16[256,512]{1,0:T(8,128)(2,1)S(1)}, bf16[256,512]{1,0:T(8,128)(2,1)S(1)}, u32[]{:S(2)}, u32[]{:S(2)}) collective-permute-start(bf16[256,512]{1,0:T(8,128)(2,1)S(1)} %collective-permute-done.4.rest_2_), channel_id=1, source_target_pairs={{0,1},{1,0},{2,3},{3,2},{4,5},{5,4},{6,7},{7,6},{8,9},{9,8},{10,11... | collective-permute-start | bytes 786440 | tf_op jit(solution)/shard_map/ppermute | solution.py:35
  25.4 1.5 %collective-permute-start.8 = (bf16[256,512]{1,0:T(8,128)(2,1)S(1)}, bf16[256,512]{1,0:T(8,128)(2,1)S(1)}, u32[]{:S(2)}, u32[]{:S(2)}) collective-permute-start(bf16[256,512]{1,0:T(8,128)(2,1)S(1)} %collective-permute-done.7.rest_4_), channel_id=1, source_target_pairs={{0,1},{1,0},{2,3},{3,2},{4,5},{5,4},{6,7},{7,6},{8,9},{9,8},{10,11... | collective-permute-start | bytes 786440 | tf_op jit(solution)/shard_map/ppermute | solution.py:35
  25.4 6.2 %collective-permute-start.13 = (bf16[176,256]{1,0:T(8,128)(2,1)S(1)}, bf16[176,256]{1,0:T(8,128)(2,1)S(1)}, u32[]{:S(2)}, u32[]{:S(2)}) collective-permute-start(bf16[176,256]{1,0:T(8,128)(2,1)S(1)} %shard_map.57.sent_ref), channel_id=1, source_target_pairs={{8,0},{10,2},{12,4},{14,6},{0,8},{2,10},{4,12},{6,14},{9,1},{11,3}... | collective-permute-start | bytes 270344 | tf_op jit(solution)/shard_map/ppermute | solution.py:21
  30.1 5.2 %collective-permute-start.9 = (bf16[64,512]{1,0:T(8,128)(2,1)S(1)}, bf16[64,512]{1,0:T(8,128)(2,1)S(1)}, u32[]{:S(2)}, u32[]{:S(2)}) collective-permute-start(bf16[64,512]{1,0:T(8,128)(2,1)S(1)} %convert_element_type.9), channel_id=1, source_target_pairs={{8,0},{10,2},{12,4},{14,6},{0,8},{2,10},{4,12},{6,14},{9,1},{11,3}... | collective-permute-start | bytes 196616 | tf_op jit(solution)/shard_map/ppermute | solution.py:21
  31.8 5.8 %collective-permute-start.14 = (bf16[176,256]{1,0:T(8,128)(2,1)S(1)}, bf16[176,256]{1,0:T(8,128)(2,1)S(1)}, u32[]{:S(2)}, u32[]{:S(2)}) collective-permute-start(bf16[176,256]{1,0:T(8,128)(2,1)S(1)} %shard_map.60.mine_ref), channel_id=1, source_target_pairs={{2,0},{0,2},{6,4},{4,6},{10,8},{8,10},{14,12},{12,14},{3,1},{1,3},... | collective-permute-start | bytes 270344 | tf_op jit(solution)/shard_map/ppermute | solution.py:21
  34.3 4.8 %collective-permute-start.15 = (bf16[176,256]{1,0:T(8,128)(2,1)S(1)}, bf16[176,256]{1,0:T(8,128)(2,1)S(1)}, u32[]{:S(2)}, u32[]{:S(2)}) collective-permute-start(bf16[176,256]{1,0:T(8,128)(2,1)S(1)} %shard_map.60.mine_ref), channel_id=1, source_target_pairs={{0,1},{1,0},{2,3},{3,2},{4,5},{5,4},{6,7},{7,6},{8,9},{9,8},{10,11... | collective-permute-start | bytes 270344 | tf_op jit(solution)/shard_map/ppermute | solution.py:35
  34.3 4.8 %collective-permute-start.16 = (bf16[176,256]{1,0:T(8,128)(2,1)S(1)}, bf16[176,256]{1,0:T(8,128)(2,1)S(1)}, u32[]{:S(2)}, u32[]{:S(2)}) collective-permute-start(bf16[176,256]{1,0:T(8,128)(2,1)S(1)} %shard_map.60.mine_ref), channel_id=1, source_target_pairs={{3,0},{2,1},{1,2},{0,3},{7,4},{6,5},{5,6},{4,7},{11,8},{10,9},{9,1... | collective-permute-start | bytes 270344 | tf_op jit(solution)/shard_map/ppermute | solution.py:31
  35.4 6.0 %collective-permute-start.10 = (bf16[64,512]{1,0:T(8,128)(2,1)S(1)}, bf16[64,512]{1,0:T(8,128)(2,1)S(1)}, u32[]{:S(2)}, u32[]{:S(2)}) collective-permute-start(bf16[64,512]{1,0:T(8,128)(2,1)S(1)} %get-tuple-element.39), channel_id=1, source_target_pairs={{2,0},{0,2},{6,4},{4,6},{10,8},{8,10},{14,12},{12,14},{3,1},{1,3},... | collective-permute-start | bytes 196616 | tf_op jit(solution)/shard_map/ppermute | solution.py:21
  37.5 4.3 %collective-permute-start.11 = (bf16[64,512]{1,0:T(8,128)(2,1)S(1)}, bf16[64,512]{1,0:T(8,128)(2,1)S(1)}, u32[]{:S(2)}, u32[]{:S(2)}) collective-permute-start(bf16[64,512]{1,0:T(8,128)(2,1)S(1)} %get-tuple-element.39), channel_id=1, source_target_pairs={{4,0},{6,2},{0,4},{2,6},{12,8},{14,10},{8,12},{10,14},{5,1},{7,3},... | collective-permute-start | bytes 196616 | tf_op jit(solution)/shard_map/ppermute | solution.py:21
  37.5 5.2 %collective-permute-start.12 = (bf16[64,512]{1,0:T(8,128)(2,1)S(1)}, bf16[64,512]{1,0:T(8,128)(2,1)S(1)}, u32[]{:S(2)}, u32[]{:S(2)}) collective-permute-start(bf16[64,512]{1,0:T(8,128)(2,1)S(1)} %get-tuple-element.39), channel_id=1, source_target_pairs={{6,0},{4,2},{2,4},{0,6},{14,8},{12,10},{10,12},{8,14},{7,1},{5,3},... | collective-permute-start | bytes 196616 | tf_op jit(solution)/shard_map/ppermute | solution.py:21
